TPU v7x, 256 devices: a whole 4x4x8 slice. The times are simulated.
256 devices in a mesh: row: 64 (over z, y_lo, x), dev: 4 (over y_hi, core).
Axes of the slice: x: 4, y: 4 (y_hi: 2, y_lo: 2; y = y_hi * 2 + y_lo), z: 8, core: 2. Of those that a mesh axis runs over, the one named last changes fastest.
Arguments:
- rider_emb: bfloat16 [16384, 128], P('row'), may hold values from -40 to 40
- driver_emb: bfloat16 [32768, 128], P(('row', 'dev')), may hold values from -5 to 5
- log_a: float32 [16384], P('row'), may hold values from -0.7 to 0.7
- log_b: float32 [32768], P(('row', 'dev')), may hold values from -0.7 to 0.7
- rider_zone: int32 [128], P('row'), may hold values from 0 to 15, as said below
- driver_zone: int32 [256], P(('row', 'dev')), may hold values from 0 to 15, as said below
- zone_table: int32 [16, 16], replicated, may hold values from 0 to 1, as said below
Outputs:
- rider_pot: float32 [16384], P('row')
- driver_pot: float32 [32768], P(('row', 'dev'))
Inputs may be any that keep to these rules, and one draw needn't show every extreme that they name: `rider_zone`: every one of the 16 zones names at least one rider block. `driver_zone`: every one of the 16 zones names at least one driver block. `zone_table`: the diagonal is all ones.
All inputs are finite; a program needn't handle non-finite values.
Results may differ from a plain program's by a relative error of at most 0.00035.
Values may be sent and summed in bfloat16 or wider, within the bound.
No kernel may reach another device: no remote copies, remote signals or barrier semaphores. Data moves between devices by JAX's collectives and lax.ppermute only.
A program may use at most 64 MiB of HBM per device.

v0:
```python
import math

import jax
import jax.numpy as jnp
from jax import lax
from jax.sharding import PartitionSpec as P

ITERS = 3


NEG_FILL = -1e30


def onehot_ints(labels, zone_count):
    return (labels[:, None] == jnp.arange(zone_count, dtype=jnp.int32)[None, :]).astype(
        jnp.bfloat16
    )


def onehot_tags(tags, zone_count):
    return (
        tags.astype(jnp.float32)[:, None] == jnp.arange(zone_count, dtype=jnp.float32)[None, :]
    ).astype(jnp.bfloat16)


def fold_into(state_pair, local_emb, local_feas, values, emb_piece, tag_piece):
    peak_old, mass_old = state_pair
    eta_cost = jnp.einsum("ie,je->ij", local_emb, emb_piece, preferred_element_type=jnp.float32)
    allowed = (
        jnp.einsum(
            "iz,jz->ij",
            local_feas,
            onehot_tags(tag_piece, local_feas.shape[1]),
            preferred_element_type=jnp.float32,
        )
        > 0.5
    )
    scores = values[None, :] - eta_cost
    peak_new = jnp.maximum(peak_old, jnp.max(jnp.where(allowed, scores, NEG_FILL), axis=1))
    mass_new = jnp.sum(jnp.where(allowed, jnp.exp(scores - peak_new[:, None]), 0.0), axis=1)
    return (peak_new, mass_new)


def per_device(rider_emb, driver_emb, log_a, log_b, rider_zone, driver_zone, zone_table):
    zone_count = zone_table.shape[0]
    block_rows = rider_emb.shape[0] // rider_zone.shape[0]
    row_count = lax.axis_size("row")
    dev_count = lax.axis_size("dev")
    rider_count = rider_emb.shape[0]
    driver_count = driver_emb.shape[0]
    log_drivers = math.log(driver_count * row_count * dev_count)
    log_riders = math.log(rider_count * row_count)
    table_bf = zone_table.astype(jnp.bfloat16)
    rider_labels = jnp.repeat(rider_zone, block_rows)
    driver_labels = jnp.repeat(driver_zone, block_rows)
    rider_tag = rider_labels.astype(jnp.bfloat16)
    driver_tag = driver_labels.astype(jnp.bfloat16)
    rider_feas = jnp.dot(
        onehot_ints(rider_labels, zone_count), table_bf, preferred_element_type=jnp.float32
    ).astype(jnp.bfloat16)
    driver_feas = jnp.einsum(
        "jk,lk->jl",
        onehot_ints(driver_labels, zone_count),
        table_bf,
        preferred_element_type=jnp.float32,
    ).astype(jnp.bfloat16)
    driver_pot = jnp.zeros((driver_count,), jnp.float32)
    rider_pot = jnp.zeros((rider_count,), jnp.float32)
    for iteration in range(ITERS):
        driver_all = lax.all_gather(driver_pot, "row", axis=0, tiled=True)
        rider_start = (
            jnp.full((rider_count,), NEG_FILL, jnp.float32),
            jnp.zeros((rider_count,), jnp.float32),
        )
        peak_val, mass_sum = fold_into(
            rider_start,
            rider_emb,
            rider_feas,
            driver_all,
            lax.all_gather(driver_emb, "row", axis=0, tiled=True),
            lax.all_gather(driver_tag, "row", axis=0, tiled=True),
        )
        global_peak = lax.pmax(peak_val, "dev")
        mass_sum = lax.psum(mass_sum * jnp.exp(peak_val - global_peak), "dev")
        peak_val = global_peak
        rider_pot = log_a - (peak_val + jnp.log(mass_sum) - log_drivers)
        rider_all = lax.all_gather(rider_pot, "row", axis=0, tiled=True)
        driver_start = (
            jnp.full((driver_count,), NEG_FILL, jnp.float32),
            jnp.zeros((driver_count,), jnp.float32),
        )
        driver_peak, driver_mass = fold_into(
            driver_start,
            driver_emb,
            driver_feas,
            rider_all,
            lax.all_gather(rider_emb, "row", axis=0, tiled=True),
            lax.all_gather(rider_tag, "row", axis=0, tiled=True),
        )
        driver_pot = log_b - (driver_peak + jnp.log(driver_mass) - log_riders)
    return (rider_pot, driver_pot)


def solution(mesh):
    placed = (
        P("row", None),
        P(("row", "dev"), None),
        P("row"),
        P(("row", "dev")),
        P("row"),
        P(("row", "dev")),
        P(),
    )
    return jax.shard_map(
        per_device,
        mesh=mesh,
        in_specs=placed,
        out_specs=(P("row"), P(("row", "dev"))),
        check_vma=False,
    )
```

profile of v0, /device:TPU:2, one launch (start us, length us, event | category | flops | bytes accessed | tf_op | source)
XLA Modules:
  0.0 1311.1 jit_solution(14156890656540785914)
XLA Ops:
  7.2 0.7 all-gather.10.cloned.1.call-update
  8.0 0.7 all-gather.12.cloned.1.call-update
  9.3 0.7 bitcast_convert_fusion
  10.0 153.2 %all-gather = bf16[64,1,128]{2,1,0:T(2,128)(2,1)S(1)} all-gather(bf16[1,1,128]{2,1,0:T(2,128)(2,1)S(1)} %broadcast.76), channel_id=1, replica_groups=mesh['row'=64,'dev'=4] {'row'}, dimensions={0}, use_global_device_ids=true | all-gather | bytes 16640 | tf_op jit(solution)/shard_map/all_gather | solution.py:81
  163.3 155.4 %all-gather.1 = bf16[64,1,256]{2,1,0:T(2,128)(2,1)S(1)} all-gather(bf16[1,1,256]{2,1,0:T(2,128)(2,1)S(1)} %reshape.38), channel_id=1, replica_groups=mesh['row'=64,'dev'=4] {'row'}, dimensions={0}, use_global_device_ids=true | all-gather | bytes 33280 | tf_op jit(solution)/shard_map/all_gather | solution.py:98
  318.8 6.1 fusion.16
  324.9 5.5 select_reduce_fusion.11
  330.5 7.2 pmax.21
  337.7 4.7 select_reduce_fusion.10
  342.4 9.5 psum.21
  351.9 150.0 %all-gather.2 = f32[64,1,256]{2,1,0:T(1,128)S(1)} all-gather(f32[1,1,256]{2,1,0:T(1,128)S(1)} %bitcast.41), channel_id=1, replica_groups=mesh['row'=64,'dev'=4] {'row'}, dimensions={0}, use_global_device_ids=true | all-gather | bytes 66560 | tf_op jit(solution)/shard_map/all_gather | solution.py:87
  501.9 112.9 %all-gather.12.cloned.1.call-done = bf16[16384,128]{1,0:T(8,128)(2,1)} async-done(((bf16[256,128]{1,0:T(8,128)(2,1)}), bf16[16384,128]{1,0:T(8,128)(2,1)}) %all-gather.12.cloned.1.call-update) | async-done | bytes 4194320 | tf_op jit(solution)/shard_map/all_gather | solution.py:97
  614.8 6.7 fusion.17
  621.5 6.0 select_reduce_fusion.9
  627.5 5.4 select_reduce_fusion.8
  633.0 150.7 %all-gather.3 = f32[64,1,128]{2,1,0:T(1,128)S(1)} all-gather(f32[1,1,128]{2,1,0:T(1,128)S(1)} %subtract_bitcast_fusion.1), channel_id=1, replica_groups=mesh['row'=64,'dev'=4] {'row'}, dimensions={0}, use_global_device_ids=true | all-gather | bytes 33280 | tf_op jit(solution)/shard_map/all_gather | solution.py:70
  783.7 4.8 select_reduce_fusion.7
  788.6 2.5 select_reduce_fusion.6
  791.1 7.2 pmax.22
  798.3 9.5 psum.22
  807.8 154.9 %all-gather.4 = f32[64,1,256]{2,1,0:T(1,128)S(1)} all-gather(f32[1,1,256]{2,1,0:T(1,128)S(1)} %bitcast.42), channel_id=1, replica_groups=mesh['row'=64,'dev'=4] {'row'}, dimensions={0}, use_global_device_ids=true | all-gather | bytes 66560 | tf_op jit(solution)/shard_map/all_gather | solution.py:87
  962.6 5.6 select_reduce_fusion.5
  968.3 4.9 select_reduce_fusion.4
  973.1 149.1 %all-gather.5 = f32[64,1,128]{2,1,0:T(1,128)S(1)} all-gather(f32[1,1,128]{2,1,0:T(1,128)S(1)} %subtract_bitcast_fusion), channel_id=1, replica_groups=mesh['row'=64,'dev'=4] {'row'}, dimensions={0}, use_global_device_ids=true | all-gather | bytes 33280 | tf_op jit(solution)/shard_map/all_gather | solution.py:70
  1122.2 1.5 select_reduce_fusion.3
  1123.7 2.5 select_reduce_fusion.2
  1126.2 7.3 pmax.23
  1133.5 8.2 psum.23
  1141.7 151.8 %all-gather.6 = f32[64,1,256]{2,1,0:T(1,128)S(1)} all-gather(f32[1,1,256]{2,1,0:T(1,128)S(1)} %bitcast.40), channel_id=1, replica_groups=mesh['row'=64,'dev'=4] {'row'}, dimensions={0}, use_global_device_ids=true | all-gather | bytes 66560 | tf_op jit(solution)/shard_map/all_gather | solution.py:87
  1293.5 5.5 select_reduce_fusion.1
  1299.0 4.7 select_reduce_fusion
  1303.7 0.5 add_subtract_fusion.3
  (46 shorter events, 0.4 us)
Async XLA Ops:
  7.2 317.7 %copy-start.6 = (s32[16,16]{1,0:T(8,128)S(1)}, s32[16,16]{1,0:T(8,128)}, u32[]{:S(2)}) copy-start(s32[16,16]{1,0:T(8,128)} %param.13) | copy-start | bytes 3076
  7.2 311.6 %all-gather.10.cloned.1.call-start = ((), (), s32[]{:S(2)}) async-start(), calls=%async_computation | async-start | bytes 2129920 | tf_op jit(solution)/shard_map/all_gather | solution.py:80
  7.9 606.9 %all-gather.12.cloned.1.call-start = ((), (), s32[]{:S(2)}) async-start(), calls=%async_computation.1 | async-start | bytes 4259840 | tf_op jit(solution)/shard_map/all_gather | solution.py:97
  330.5 21.5 %copy-start.3 = (f32[256]{0:T(256)S(1)}, f32[256]{0:T(256)}, u32[]{:S(2)}) copy-start(f32[256]{0:T(256)} %param.9) | copy-start | bytes 3076
  330.5 284.4 %copy-start.2 = (bf16[128,128]{1,0:T(8,128)(2,1)S(1)}, bf16[128,128]{1,0:T(8,128)(2,1)}, u32[]{:S(2)}) copy-start(bf16[128,128]{1,0:T(8,128)(2,1)} %param.8) | copy-start | bytes 98308
  627.5 5.5 copy-start.4
  627.5 161.1 %slice-start = ((s8[8388608]{0:T(1024)(128)(4,1)}), s8[4194304]{0:T(1024)(128)(4,1)S(1)}, s32[]{:S(2)}) async-start(s8[8388608]{0:T(1024)(128)(4,1)} %bitcast.24), calls=%async_computation.2 | async-start | bytes 8388608
  633.0 155.6 %slice-start.1 = ((s8[8388608]{0:T(1024)(128)(4,1)}), s8[4194304]{0:T(1024)(128)(4,1)S(1)}, s32[]{:S(2)}) async-start(s8[8388608]{0:T(1024)(128)(4,1)} %bitcast.24), calls=%async_computation.3 | async-start | bytes 8388608
  807.8 160.5 %copy-start = (pred[128,16384]{1,0:T(8,128)(4,1)S(1)}, pred[128,16384]{1,0:T(8,128)(4,1)}, u32[]{:S(2)}) copy-start(pred[128,16384]{1,0:T(8,128)(4,1)} %get-tuple-element.7) | copy-start | bytes 6291460
  962.6 159.5 %slice-start.2 = ((s8[8388608]{0:T(1024)(128)(4,1)}), s8[4194304]{0:T(1024)(128)(4,1)S(1)}, s32[]{:S(2)}) async-start(s8[8388608]{0:T(1024)(128)(4,1)} %bitcast.26), calls=%async_computation.4 | async-start | bytes 8388608
  968.3 153.9 %slice-start.3 = ((s8[8388608]{0:T(1024)(128)(4,1)}), s8[4194304]{0:T(1024)(128)(4,1)S(1)}, s32[]{:S(2)}) async-start(s8[8388608]{0:T(1024)(128)(4,1)} %bitcast.26), calls=%async_computation.5 | async-start | bytes 8388608
  1126.2 172.8 %copy-start.1 = (pred[128,16384]{1,0:T(8,128)(4,1)S(1)}, pred[128,16384]{1,0:T(8,128)(4,1)}, u32[]{:S(2)}) copy-start(pred[128,16384]{1,0:T(8,128)(4,1)} %get-tuple-element.7) | copy-start | bytes 6291460
  1141.7 162.0 %copy-start.5 = (f32[256]{0:T(256)}, f32[256]{0:T(256)S(1)}, u32[]{:S(2)}) copy-start(f32[256]{0:T(256)S(1)} %add_subtract_fusion) | copy-start | bytes 3076
Sparse Core Ops, SparseCore 0:
  9.8 301.5 all-gather.9
  313.2 301.5 all-gather.11
where the time goes:
time: 1310 us
  blocking collectives  1110 us (85%)
  waiting for transfers between devices  114 us (9%)
  other arithmetic  43.5 us (3%)
  matrix products  24.3 us (2%)
  between operations  14.9 us (1%)
    all_gather x3, blocking collectives, per_device(): rider_all = lax.all_gather(rider_pot, 'row', axis=0, tiled=True)  457 us
    all_gather x2, blocking collectives, per_device(): driver_all = lax.all_gather(driver_pot, 'row', axis=0, tiled=True)  300 us
    all_gather x1, blocking collectives, per_device(): lax.all_gather(rider_tag, 'row', axis=0, tiled=True)  155 us
    all_gather x1, blocking collectives, per_device(): lax.all_gather(driver_tag, 'row', axis=0, tiled=True)  153 us
    all_gather x1, waiting for transfers between devices, per_device(): lax.all_gather(rider_emb, 'row', axis=0, tiled=True)  113 us
    psum x3, blocking collectives, per_device(): mass_sum = lax.psum(mass_sum * jnp.exp(peak_val - global_peak), 'dev')  27.2 us
  transfers between devices with their start and end apart: 2, of which 1 were waited for; matrix products, arithmetic and copies ran while one was open for 1% of the time, Pallas kernels for 0%

commit v1 on v0

v1 whole, which is shorter than its diff:
```python
import math

import jax
import jax.numpy as jnp
from jax import lax
from jax.experimental import pallas as pl
from jax.experimental.pallas import tpu as pltpu
from jax.sharding import Mesh, PartitionSpec as P

AXES = ("z", "yl", "x", "yh", "c")
SIZES = (8, 2, 4, 2, 2)
RGROUP = ("yl", "x", "yh")
DGROUP = ("z", "c")

B = 128
RB = 8
DB = 16
GROUP = 16
PAY = B + 16
ITERS = 3
LOG_DRIVERS = math.log(32768)
LOG_RIDERS = math.log(16384)
PENALTY = 1e30
FLOOR = -1e29

F32 = jnp.float32
BF16 = jnp.bfloat16
VM = pl.BlockSpec(memory_space=pltpu.VMEM)
SM = pl.BlockSpec(memory_space=pltpu.SMEM)


def call(body, outs, ins, scratch=(), limit=40):
    return pl.pallas_call(
        body,
        out_shape=outs,
        in_specs=ins,
        out_specs=[VM] * len(outs),
        scratch_shapes=list(scratch),
        compiler_params=pltpu.CompilerParams(vmem_limit_bytes=limit * 2**20),
    )


def f32(*shape):
    return jax.ShapeDtypeStruct(shape, F32)


def bf16(*shape):
    return jax.ShapeDtypeStruct(shape, BF16)


def product(left, right):
    return lax.dot_general(left, right, (((1,), (1,)), ((), ())), preferred_element_type=F32)


def fold(block, op):
    rows = [block[8 * k : 8 * k + 8] for k in range(B // 8)]
    while len(rows) > 1:
        rows = [op(rows[2 * k], rows[2 * k + 1]) for k in range(len(rows) // 2)]
    return rows[0]


def with_zone(message):
    return jnp.concatenate([message[:B], jnp.concatenate([message[B:]] * (B // 16), axis=0)], axis=1)


def column(row):
    return jnp.broadcast_to(row, (B, B)).T


def pack_body(rider, driver, rzone, dzone, table, rider_out, driver_out):
    c = lax.axis_index("c")
    lane = lax.broadcasted_iota(jnp.int32, (16, B), 1)
    hot = jnp.where(lane == rzone[c], 1.0, 0.0)
    zone = dzone[0]
    shut = jnp.zeros((16, B), F32)
    for k in range(16):
        shut = jnp.where((lane == k) & (table[k, zone] != 1), PENALTY, shut)
    mine = rider[c]
    for k in range(8):
        rider_out[k, :B, :] = mine
        rider_out[k, B:, :] = hot.astype(BF16)
        driver_out[k, :B, :] = driver[...]
        driver_out[k, B:, :] = shut.astype(BF16)


def rider_first_body(rider, own, other, log_a, out):
    c = lax.axis_index("c")

    def pair(p, carry):
        right = jnp.concatenate([with_zone(rider[2 * p]), with_zone(rider[2 * p + 1])], axis=0)
        peak = jnp.full((8, 2 * B), -3e38, F32)
        mass = jnp.zeros((8, 2 * B), F32)
        for z in range(8):
            for source in (own, other):
                cost = product(with_zone(source[z]), right)
                fresh = jnp.maximum(peak, -fold(cost, jnp.minimum))
                terms = jnp.exp(-cost - jnp.concatenate([fresh] * 16, axis=0))
                mass = mass * jnp.exp(peak - fresh) + fold(terms, jnp.add)
                peak = fresh
        top = jnp.max(peak, axis=0, keepdims=True)
        mass = jnp.sum(mass * jnp.exp(peak - top), axis=0, keepdims=True)
        for h in range(2):
            out[0, pl.ds(2 * p + h, 1), :] = top[:, h * B : (h + 1) * B]
            out[0, pl.ds(8 + 2 * p + h, 1), :] = mass[:, h * B : (h + 1) * B]
        return carry

    lax.fori_loop(0, RB // 2, pair, 0)
    out[0, 16:24, :] = jnp.broadcast_to(log_a[pl.ds(c, 1), :], (8, B))
    for k in range(1, GROUP):
        out[k] = out[0]


def driver_first_body(sums, rider, own, other, log_b, out, kernel, peaks, pots, ucol, right):
    c = lax.axis_index("c")
    peak = sums[0, 0:8]
    for k in range(1, GROUP):
        peak = jnp.maximum(peak, sums[k, 0:8])
    mass = jnp.zeros((8, B), F32)
    for k in range(GROUP):
        mass = mass + sums[k, 8:16] * jnp.exp(sums[k, 0:8] - peak)
    log_a = jnp.concatenate([sums[2 * k, 16:17] for k in range(RB)], axis=0)
    pot = log_a - (peak + jnp.log(mass) - LOG_DRIVERS)
    pots[0:8] = pot
    pots[8:16] = log_a
    for r in range(RB):
        ucol[r * B : (r + 1) * B, :] = column(pot[r : r + 1])

    def pair(z, carry):
        right[pl.ds(pl.multiple_of(c * B, B), B), :] = with_zone(own[z])
        right[pl.ds(pl.multiple_of((1 - c) * B, B), B), :] = with_zone(other[z])
        rhs = right[...]
        lanes = pl.ds(pl.multiple_of(z * 2 * B, 2 * B), 2 * B)
        high = jnp.full((8, 2 * B), FLOOR, F32)
        for r in range(RB):
            u = ucol[r * B : (r + 1) * B, :]
            score = jnp.concatenate([u, u], axis=1) - product(with_zone(rider[r]), rhs)
            kernel[r * B : (r + 1) * B, lanes] = score
            high = jnp.maximum(high, fold(score, jnp.maximum))
        top = jnp.max(high, axis=0, keepdims=True)
        total = jnp.zeros((8, 2 * B), F32)
        for r in range(RB):
            term = jnp.exp(kernel[r * B : (r + 1) * B, lanes] - top)
            kernel[r * B : (r + 1) * B, lanes] = term
            total = total + fold(term, jnp.add)
        total = jnp.sum(total, axis=0, keepdims=True)
        for h in range(2):
            out[0, pl.ds(2 * z + h, 1), :] = top[:, h * B : (h + 1) * B]
            out[0, pl.ds(16 + 2 * z + h, 1), :] = total[:, h * B : (h + 1) * B]
        return carry

    lax.fori_loop(0, DB // 2, pair, 0)
    out[0, 32:40, :] = jnp.broadcast_to(log_b[...], (8, B))
    peaks[...] = out[0, 0:16]
    for k in range(1, GROUP):
        out[k] = out[0]


def row_sums(kernel, weight, out):
    def block(r, carry):
        rows = pl.ds(pl.multiple_of(r * B, B), B)
        acc = kernel[rows, 0:B] * weight[0:1]
        for k in range(1, DB):
            acc = acc + kernel[rows, k * B : (k + 1) * B] * weight[k : k + 1]
        out[0, pl.ds(r, 1), :] = jnp.sum(acc.T, axis=0, keepdims=True)
        return carry

    lax.fori_loop(0, RB, block, 0)
    for k in range(1, GROUP):
        out[k] = out[0]


def column_sums(kernel, fcol):
    def block(r, acc):
        for k in range(B // 8):
            rows = pl.ds(pl.multiple_of(r * B + 8 * k, 8), 8)
            f = fcol[rows, :]
            acc = tuple(a + kernel[rows, j * B : (j + 1) * B] * f for j, a in enumerate(acc))
        return acc

    return lax.fori_loop(0, RB, block, tuple(jnp.zeros((8, B), F32) for _ in range(DB)))


def rider_second_body(sums, peaks, kernel, out, state, weight):
    peak = sums[0, 0:16]
    for k in range(1, GROUP):
        peak = jnp.maximum(peak, sums[k, 0:16])
    mass = jnp.zeros((DB, B), F32)
    for k in range(GROUP):
        mass = mass + sums[k, 16:32] * jnp.exp(sums[k, 0:16] - peak)
    log_b = jnp.concatenate([sums[k, 32:33] for k in range(GROUP)], axis=0)
    pot = log_b - (peak + jnp.log(mass) - LOG_RIDERS)
    scale = jnp.exp(pot + peaks[...])
    state[0:16] = pot
    state[16:32] = log_b
    state[32:48] = scale
    weight[...] = scale
    row_sums(kernel, weight, out)


def total_of(sums):
    parts = [sums[k] for k in range(GROUP)]
    while len(parts) > 1:
        parts = [parts[2 * k] + parts[2 * k + 1] for k in range(len(parts) // 2)]
    return parts[0]


def driver_next_body(sums, pots, state, kernel, out, fcol):
    f = jnp.exp(pots[8:16] + LOG_DRIVERS) / total_of(sums)
    for r in range(RB):
        fcol[r * B : (r + 1) * B, :] = column(f[r : r + 1])
    acc = column_sums(kernel, fcol)
    rows = jnp.concatenate([jnp.sum(a, axis=0, keepdims=True) for a in acc], axis=0)
    rows = rows * state[32:48]
    for k in range(GROUP):
        out[k] = rows


def rider_next_body(sums, state, kernel, out, weight):
    weight[...] = state[32:48] * (jnp.exp(state[16:32] + LOG_RIDERS) / total_of(sums))
    row_sums(kernel, weight, out)


def driver_last_body(sums, pots, state, kernel, out, mine, fcol):
    block = lax.axis_index("yl") * 4 + lax.axis_index("x")
    total = total_of(sums)
    log_a = pots[8:16]
    f = jnp.exp(log_a + LOG_DRIVERS) / total
    for r in range(RB):
        fcol[r * B : (r + 1) * B, :] = column(f[r : r + 1])
    pot = pots[0:8] + (log_a + LOG_DRIVERS - jnp.log(total))
    row = lax.broadcasted_iota(jnp.int32, (8, B), 0)
    mine[...] = jnp.broadcast_to(jnp.sum(jnp.where(row == block, pot, 0.0), axis=0, keepdims=True), (8, B))
    acc = column_sums(kernel, fcol)
    for k in range(DB):
        out[k] = jnp.broadcast_to(jnp.sum(acc[k], axis=0, keepdims=True) * state[32 + k : 33 + k], (8, B))


def finish_body(sums, state, mine, other, rider_pot, driver_pot):
    c = lax.axis_index("c")
    block = lax.axis_index("z") * 2 + c
    total = total_of(sums)[0:1]
    pot = state[pl.ds(block, 1), :]
    log_b = state[pl.ds(16 + block, 1), :]
    driver_pot[...] = pot + (log_b + LOG_RIDERS - jnp.log(total))
    rider_pot[pl.ds(c, 1), :] = mine[0:1]
    rider_pot[pl.ds(1 - c, 1), :] = other[0:1]


def exchange(message, axes):
    return lax.all_to_all(message, axes, 0, 0, tiled=True)


def swap_core(value):
    return lax.ppermute(value, "c", [(0, 1), (1, 0)])


def per_device(rider_emb, driver_emb, log_a, log_b, rider_zone, driver_zone, zone_table):
    rider_msg, driver_msg = call(
        pack_body, [bf16(8, PAY, B), bf16(8, PAY, B)], [VM, VM, SM, SM, SM]
    )(rider_emb.reshape(2, B, B), driver_emb, rider_zone, driver_zone, zone_table)
    own = exchange(driver_msg, ("z",))
    other = swap_core(own)
    rider = exchange(rider_msg, ("yl", "x"))
    (message,) = call(rider_first_body, [f32(GROUP, 24, B)], [VM] * 4)(
        rider, own, other, log_a.reshape(2, B)
    )
    sums = exchange(message, RGROUP)
    message, kernel, peaks, pots = call(
        driver_first_body,
        [f32(GROUP, 40, B), f32(RB * B, DB * B), f32(DB, B), f32(16, B)],
        [VM] * 5,
        [pltpu.VMEM((RB * B, B), F32), pltpu.VMEM((2 * B, 2 * B), BF16)],
    )(sums, rider, own, other, log_b.reshape(1, B))
    sums = exchange(message, DGROUP)
    weights = [pltpu.VMEM((DB, B), F32)]
    columns = [pltpu.VMEM((RB * B, B), F32)]
    message, state = call(
        rider_second_body, [f32(GROUP, 8, B), f32(48, B)], [VM] * 3, weights
    )(sums, peaks, kernel)
    sums = exchange(message, RGROUP)
    for _ in range(ITERS - 2):
        (message,) = call(driver_next_body, [f32(GROUP, DB, B)], [VM] * 4, columns)(
            sums, pots, state, kernel
        )
        sums = exchange(message, DGROUP)
        (message,) = call(rider_next_body, [f32(GROUP, 8, B)], [VM] * 3, weights)(
            sums, state, kernel
        )
        sums = exchange(message, RGROUP)
    message, mine = call(
        driver_last_body, [f32(GROUP, 8, B), f32(8, B)], [VM] * 4, columns
    )(sums, pots, state, kernel)
    theirs = swap_core(mine)
    sums = exchange(message, DGROUP)
    rider_pot, driver_pot = call(finish_body, [f32(2, B), f32(1, B)], [VM] * 4)(
        sums, state, mine, theirs
    )
    return rider_pot.reshape(2 * B), driver_pot.reshape(B)


def solution(mesh):
    fine = Mesh(mesh.devices.reshape(SIZES), AXES)
    row, every = ("z", "yl", "x"), AXES
    placed = (
        P(row, None),
        P(every, None),
        P(row),
        P(every),
        P(row),
        P(every),
        P(),
    )
    return jax.shard_map(
        per_device,
        mesh=fine,
        in_specs=placed,
        out_specs=(P(row), P(every)),
        check_vma=False,
    )
```

time: 1310 us -> 131 us (0.10)
  the two profiles are of different devices: /device:TPU:2 before, /device:TPU:1 now
where the time goes in v1:
time: 131 us; the launch traced here: 130 us
  blocking collectives  94.4 us (72%)
  Pallas kernels  15.5 us (12%)
  waiting for transfers between devices  7.53 us (6%)
  starting transfers between devices  7.31 us (6%)
  local copies, waits for them, and re-layouts  4.28 us (3%)
  between operations  1.32 us (1%)
    all_to_all x7, blocking collectives, exchange(): return lax.all_to_all(message, axes, 0, 0, tiled=True)  94.4 us
    all_to_all x1, waiting for transfers between devices, exchange(): return lax.all_to_all(message, axes, 0, 0, tiled=True)  6.67 us
    pallas_call x1, Pallas kernels, per_device(): call(driver_first_body, [f32(GROUP, 40, B), f32(RB * B, DB * B), f32(DB,...  5.55 us
    all_to_all x1, starting transfers between devices, exchange(): return lax.all_to_all(message, axes, 0, 0, tiled=True)  4.31 us
    unnamed x12, local copies, waits for them, and re-layouts  4.28 us
    pallas_call x1, Pallas kernels, per_device(): call(rider_first_body, [f32(GROUP, 24, B)], [VM] * 4)  3.7 us
    ppermute x2, starting transfers between devices, swap_core(): return lax.ppermute(value, 'c', [(0, 1), (1, 0)])  3 us
  transfers between devices with their start and end apart: 3, of which 2 were waited for; matrix products, arithmetic and copies ran while one was open for 0% of the time, Pallas kernels for 0%

profile of v1, /device:TPU:1, one launch (start us, length us, event | category | flops | bytes accessed | tf_op | source)
XLA Modules:
  0.0 130.4 jit_solution(10796141839024653404)
XLA Ops:
  1.3 0.0 copy-start
  1.3 0.8 copy-done
  2.1 0.0 copy-start.1
  2.1 0.8 copy-done.1
  2.9 0.0 copy-start.2
  2.9 0.7 copy-done.2
  3.6 0.0 copy-start.4
  3.6 0.7 copy-done.4
  4.2 0.8 shard_map.86
  5.0 19.7 %all_to_all.40.own = bf16[8,144,128]{2,1,0:T(8,128)(2,1)S(1)} all-to-all(bf16[8,144,128]{2,1,0:T(8,128)(2,1)S(1)} %get-tuple-element.15), channel_id=1, replica_groups=mesh['z'=8,'yl'=2,'x'=4,'yh'=2,'c'=2] {'z'}, dimensions={0} | all-to-all | bytes 589824 | tf_op jit(solution)/shard_map/all_to_all | solution.py:250
  24.6 2.7 %collective-permute-start = (bf16[8,144,128]{2,1,0:T(8,128)(2,1)S(1)}, bf16[8,144,128]{2,1,0:T(8,128)(2,1)S(1)}, u32[]{:S(2)}, u32[]{:S(2)}) collective-permute-start(bf16[8,144,128]{2,1,0:T(8,128)(2,1)S(1)} %all_to_all.40.own), channel_id=1, source_target_pairs={{0,1},{1,0},{2,3},{3,2},{4,5},{5,4},{6,7},{7,6},{8,9},{9,8},{10,11... | collective-permute-start | bytes 884744 | tf_op jit(solution)/shard_map/ppermute | solution.py:254
  27.3 12.6 %all_to_all.41.rider = bf16[8,144,128]{2,1,0:T(8,128)(2,1)S(1)} all-to-all(bf16[8,144,128]{2,1,0:T(8,128)(2,1)S(1)} %get-tuple-element.14), channel_id=1, replica_groups=mesh['z'=8,'yl'=2,'x'=4,'yh'=2,'c'=2] {'yl','x'}, dimensions={0} | all-to-all | bytes 589824 | tf_op jit(solution)/shard_map/all_to_all | solution.py:250
  39.9 0.0 collective-permute-done.other
  39.9 0.0 copy-start.3
  39.9 0.7 copy-done.3
  40.6 3.7 %shard_map.87 = f32[16,24,128]{2,1,0:T(8,128)S(1)} custom-call(bf16[8,144,128]{2,1,0:T(8,128)(2,1)S(1)} %all_to_all.41.rider, bf16[8,144,128]{2,1,0:T(8,128)(2,1)S(1)} %all_to_all.40.own, bf16[8,144,128]{2,1,0:T(8,128)(2,1)S(1)} %collective-permute-done.other, f32[2,128]{1,0:T(2,128)S(1)} %bitcast.6), custom_call_target="tpu_custom_call" | custom-call | tf_op jit(solution)/shard_map/pallas_call | solution.py:264
  44.3 11.8 %all_to_all.42.sums = f32[16,24,128]{2,1,0:T(8,128)S(1)} all-to-all(f32[16,24,128]{2,1,0:T(8,128)S(1)} %shard_map.87), channel_id=1, replica_groups=mesh['z'=8,'yl'=2,'x'=4,'yh'=2,'c'=2] {'yl','x','yh'}, dimensions={0} | all-to-all | bytes 393216 | tf_op jit(solution)/shard_map/all_to_all | solution.py:250
  56.1 0.7 copy-done.5
  56.7 5.5 %shard_map.88 = (f32[16,40,128]{2,1,0:T(8,128)S(1)}, f32[1024,2048]{1,0:T(8,128)S(1)}, f32[16,128]{1,0:T(8,128)S(1)}, f32[16,128]{1,0:T(8,128)S(1)}) custom-call(f32[16,24,128]{2,1,0:T(8,128)S(1)} %all_to_all.42.sums, bf16[8,144,128]{2,1,0:T(8,128)(2,1)S(1)} %all_to_all.41.rider, bf16[8,144,128]{2,1,0:T(8,128)(2,1)S(1)} %all_to_all.40.own, ...), custom_call_target="tpu_custom_call" | custom-call | tf_op jit(solution)/shard_map/pallas_call | solution.py:268
  62.3 17.9 %all_to_all.43.sums = f32[16,40,128]{2,1,0:T(8,128)S(1)} all-to-all(f32[16,40,128]{2,1,0:T(8,128)S(1)} %get-tuple-element.16), channel_id=1, replica_groups=mesh['z'=8,'yl'=2,'x'=4,'yh'=2,'c'=2] {'z','c'}, dimensions={0} | all-to-all | bytes 655360 | tf_op jit(solution)/shard_map/all_to_all | solution.py:250
  80.2 1.3 %shard_map.89 = (f32[16,8,128]{2,1,0:T(8,128)S(1)}, f32[48,128]{1,0:T(8,128)S(1)}) custom-call(f32[16,40,128]{2,1,0:T(8,128)S(1)} %all_to_all.43.sums, f32[16,128]{1,0:T(8,128)S(1)} %get-tuple-element.17.peaks, f32[1024,2048]{1,0:T(8,128)S(1)} %get-tuple-element.18.kernel), custom_call_target="tpu_custom_call" | custom-call | tf_op jit(solution)/shard_map/pallas_call | solution.py:277
  81.6 9.7 %all_to_all.44.sums = f32[16,8,128]{2,1,0:T(8,128)S(1)} all-to-all(f32[16,8,128]{2,1,0:T(8,128)S(1)} %get-tuple-element.19), channel_id=1, replica_groups=mesh['z'=8,'yl'=2,'x'=4,'yh'=2,'c'=2] {'yl','x','yh'}, dimensions={0} | all-to-all | bytes 131072 | tf_op jit(solution)/shard_map/all_to_all | solution.py:250
  91.2 0.8 shard_map.90
  92.1 13.3 %all_to_all.45.sums = f32[16,16,128]{2,1,0:T(8,128)S(1)} all-to-all(f32[16,16,128]{2,1,0:T(8,128)S(1)} %shard_map.90), channel_id=1, replica_groups=mesh['z'=8,'yl'=2,'x'=4,'yh'=2,'c'=2] {'z','c'}, dimensions={0} | all-to-all | bytes 262144 | tf_op jit(solution)/shard_map/all_to_all | solution.py:250
  105.4 1.3 shard_map.91
  106.6 9.5 %all_to_all.46.sums = f32[16,8,128]{2,1,0:T(8,128)S(1)} all-to-all(f32[16,8,128]{2,1,0:T(8,128)S(1)} %shard_map.91), channel_id=1, replica_groups=mesh['z'=8,'yl'=2,'x'=4,'yh'=2,'c'=2] {'yl','x','yh'}, dimensions={0} | all-to-all | bytes 131072 | tf_op jit(solution)/shard_map/all_to_all | solution.py:250
  116.2 1.5 %shard_map.92 = (f32[16,8,128]{2,1,0:T(8,128)}, f32[8,128]{1,0:T(8,128)S(1)}) custom-call(f32[16,8,128]{2,1,0:T(8,128)S(1)} %all_to_all.46.sums, f32[16,128]{1,0:T(8,128)S(1)} %get-tuple-element.20.pots, f32[48,128]{1,0:T(8,128)S(1)} %get-tuple-element.21.state, f32[1024,2048]{1,0:T(8,128)S(1)} %get-tuple-element.18.kernel), custom_call_target="tpu_custom_call" | custom-call | tf_op jit(solution)/shard_map/pallas_call | solution.py:290
  117.6 4.3 %all-to-all-start.7 = ((f32[16,8,128]{2,1,0:T(8,128)}), f32[16,8,128]{2,1,0:T(8,128)S(1)}, u32[]{:S(2)}, u32[]{:S(2)}) async-start(f32[16,8,128]{2,1,0:T(8,128)} %get-tuple-element.22), calls=%async_computation.7 | async-start | bytes 131072 | tf_op jit(solution)/shard_map/all_to_all | solution.py:250
  122.0 0.3 collective-permute-start.1
  122.3 0.9 collective-permute-done.1.other
  123.1 6.7 %all-to-all-done.7.sums = f32[16,8,128]{2,1,0:T(8,128)S(1)} async-done(((f32[16,8,128]{2,1,0:T(8,128)}), f32[16,8,128]{2,1,0:T(8,128)S(1)}, u32[]{:S(2)}, u32[]{:S(2)}) %all-to-all-start.7) | async-done | bytes 65568 | tf_op jit(solution)/shard_map/all_to_all | solution.py:250
  129.8 0.6 shard_map.93
  (1 shorter events, 0.0 us)
Async XLA Ops:
  1.3 0.8 copy-start
  2.1 0.8 copy-start.1
  2.9 0.7 copy-start.2
  3.6 0.7 copy-start.4
  24.6 15.3 %collective-permute-start = (bf16[8,144,128]{2,1,0:T(8,128)(2,1)S(1)}, bf16[8,144,128]{2,1,0:T(8,128)(2,1)S(1)}, u32[]{:S(2)}, u32[]{:S(2)}) collective-permute-start(bf16[8,144,128]{2,1,0:T(8,128)(2,1)S(1)} %all_to_all.40.own), channel_id=1, source_target_pairs={{0,1},{1,0},{2,3},{3,2},{4,5},{5,4},{6,7},{7,6},{8,9},{9,8},{10,11... | collective-permute-start | bytes 884744 | tf_op jit(solution)/shard_map/ppermute | solution.py:254
  39.9 0.7 copy-start.3
  56.1 0.7 copy-start.5
  117.6 12.2 %all-to-all-start.7 = ((f32[16,8,128]{2,1,0:T(8,128)}), f32[16,8,128]{2,1,0:T(8,128)S(1)}, u32[]{:S(2)}, u32[]{:S(2)}) async-start(f32[16,8,128]{2,1,0:T(8,128)} %get-tuple-element.22), calls=%async_computation.7 | async-start | bytes 131072 | tf_op jit(solution)/shard_map/all_to_all | solution.py:250
  122.0 1.2 collective-permute-start.1

commit v2 on v1

v2 whole, which is shorter than its diff:
```python
import math

import jax
import jax.numpy as jnp
from jax import lax
from jax.experimental import pallas as pl
from jax.experimental.pallas import tpu as pltpu
from jax.sharding import Mesh, PartitionSpec as P

AXES = ("z", "yl", "x", "yh", "c")
SIZES = (8, 2, 4, 2, 2)
RGROUP = ("yl", "x", "yh", "c")
DGROUP = ("z",)
RPEERS = 32
DPEERS = 8

B = 128
RB = 16
DB = 8
PAY = B + 16
ITERS = 3
LOG_DRIVERS = math.log(32768)
LOG_RIDERS = math.log(16384)
PENALTY = 1e30
FLOOR = -1e29
TINY = 1e-37

F32 = jnp.float32
BF16 = jnp.bfloat16
VM = pl.BlockSpec(memory_space=pltpu.VMEM)
FAR = pl.BlockSpec(memory_space=pltpu.HBM)


def call(body, outs, ins, scratch=(), limit=40, to=VM):
    return pl.pallas_call(
        body,
        out_shape=outs,
        in_specs=ins,
        out_specs=[to] * len(outs),
        scratch_shapes=list(scratch),
        compiler_params=pltpu.CompilerParams(vmem_limit_bytes=limit * 2**20),
    )


def f32(*shape):
    return jax.ShapeDtypeStruct(shape, F32)


def bf16(*shape):
    return jax.ShapeDtypeStruct(shape, BF16)


def product(left, right):
    return lax.dot_general(left, right, (((1,), (1,)), ((), ())), preferred_element_type=F32)


def tree(parts, op):
    while len(parts) > 1:
        parts = [op(parts[2 * k], parts[2 * k + 1]) for k in range(len(parts) // 2)]
    return parts[0]


def fold(block, op):
    return tree([block[8 * k : 8 * k + 8] for k in range(B // 8)], op)


def column(row):
    return jnp.broadcast_to(row, (B, B)).T


def three_parts(value):
    high = value.astype(BF16)
    rest = value - high.astype(F32)
    middle = rest.astype(BF16)
    return high, middle, (rest - middle.astype(F32)).astype(BF16)


def zone_rows(message):
    return jnp.broadcast_to(message[B : B + 1].astype(F32), (16, B)).astype(BF16)


def weight_row(message):
    tail = message[B:].astype(F32)
    return (tail[1:2] + tail[2:3]) + tail[3:4]


def with_zone(message, zone):
    return jnp.concatenate([message[:B], jnp.concatenate([zone] * (B // 16), axis=0)], axis=1)


def tail_rows(zone_row, log_row):
    row = lax.broadcasted_iota(jnp.int32, (16, B), 0)
    tail = jnp.where(row == 0, zone_row, 0.0)
    for k, part in enumerate(three_parts(log_row)):
        tail = jnp.where(row == k + 1, part.astype(F32), tail)
    return tail.astype(BF16)


def pack_body(rider, driver, log_a, log_b, rzone, dzone, table, rider_out, driver_out,
              a_row, b_row, rz, dz, tab, tails, sems):
    c = lax.axis_index("c")
    small = [
        pltpu.make_async_copy(log_a.at[pl.ds(c, 1)], a_row, sems.at[0]),
        pltpu.make_async_copy(log_b, b_row, sems.at[1]),
        pltpu.make_async_copy(rzone, rz, sems.at[2]),
        pltpu.make_async_copy(dzone, dz, sems.at[3]),
        pltpu.make_async_copy(table, tab, sems.at[4]),
    ]
    for copy in small:
        copy.start()
    large = []
    for k in range(8):
        large.append(pltpu.make_async_copy(rider.at[c], rider_out.at[k, pl.ds(0, B)], sems.at[5 + k]))
        large.append(pltpu.make_async_copy(driver, driver_out.at[k, pl.ds(0, B)], sems.at[13 + k]))
    for copy in large:
        copy.start()
    for copy in small:
        copy.wait()
    lane = lax.broadcasted_iota(jnp.int32, (16, B), 1)
    hot = jnp.where(lane == rz[c], 1.0, 0.0)
    zone = dz[0]
    shut = jnp.zeros((16, B), F32)
    for k in range(16):
        shut = jnp.where((lane == k) & (tab[k, zone] != 1), PENALTY, shut)
    tails[0] = tail_rows(hot, a_row[...])
    tails[1] = tail_rows(shut, b_row[...])
    ends = []
    for k in range(8):
        ends.append(pltpu.make_async_copy(tails.at[0], rider_out.at[k, pl.ds(B, 16)], sems.at[21 + k]))
        ends.append(pltpu.make_async_copy(tails.at[1], driver_out.at[k, pl.ds(B, 16)], sems.at[29 + k]))
    for copy in ends:
        copy.start()
    for copy in large + ends:
        copy.wait()


def rider_first_body(own, other, driver, out, dzone):
    c = lax.axis_index("c")
    for z in range(DB):
        dzone[z] = zone_rows(driver[z])

    def pair(p, carry):
        mine, theirs = own[p], other[p]
        right = jnp.concatenate(
            [with_zone(mine, zone_rows(mine)), with_zone(theirs, zone_rows(theirs))], axis=0
        )
        peak = jnp.full((8, 2 * B), -3e38, F32)
        mass = jnp.zeros((8, 2 * B), F32)
        for z in range(DB):
            cost = product(with_zone(driver[z], dzone[z]), right)
            fresh = jnp.maximum(peak, -fold(cost, jnp.minimum))
            terms = jnp.exp(-cost - jnp.concatenate([fresh] * 16, axis=0))
            mass = mass * jnp.exp(peak - fresh) + fold(terms, jnp.add)
            peak = fresh
        top = jnp.max(peak, axis=0, keepdims=True)
        mass = jnp.sum(mass * jnp.exp(peak - top), axis=0, keepdims=True)
        total = top + jnp.log(mass)
        out[0, pl.ds(2 * p + c, 1), :] = total[:, :B]
        out[0, pl.ds(2 * p + 1 - c, 1), :] = total[:, B:]
        return carry

    lax.fori_loop(0, RB // 2, pair, 0)
    for k in range(1, RPEERS):
        out[k] = out[0]


def log_total(sums, peers):
    parts = [sums[k] for k in range(peers)]
    peak = tree(parts, jnp.maximum)
    return peak + jnp.log(tree([jnp.exp(part - peak) for part in parts], jnp.add))


def total_of(sums, peers):
    return tree([sums[k] for k in range(peers)], jnp.add)


def driver_first_body(sums, own, other, driver, out, kernel, peaks, pots, ucol):
    c = lax.axis_index("c")
    for p in range(RB // 2):
        pots[pl.ds(RB + 2 * p + c, 1), :] = weight_row(own[p])
        pots[pl.ds(RB + 2 * p + 1 - c, 1), :] = weight_row(other[p])
    pots[0:RB] = pots[RB:] - (log_total(sums, RPEERS) - LOG_DRIVERS)
    for p in range(RB // 2):
        ucol[2 * p * B : (2 * p + 1) * B, :] = column(pots[pl.ds(2 * p + c, 1), :])
        ucol[(2 * p + 1) * B : (2 * p + 2) * B, :] = column(pots[pl.ds(2 * p + 1 - c, 1), :])

    def pair(h, carry):
        one, two = driver[2 * h], driver[2 * h + 1]
        right = jnp.concatenate(
            [with_zone(one, zone_rows(one)), with_zone(two, zone_rows(two))], axis=0
        )
        lanes = pl.ds(pl.multiple_of(h * 2 * B, 2 * B), 2 * B)
        high = jnp.full((8, 2 * B), FLOOR, F32)
        for r in range(RB):
            u = ucol[r * B : (r + 1) * B, :]
            left = own[r // 2] if r % 2 == 0 else other[r // 2]
            score = jnp.concatenate([u, u], axis=1) - product(with_zone(left, zone_rows(left)), right)
            kernel[r * B : (r + 1) * B, lanes] = score
            high = jnp.maximum(high, fold(score, jnp.maximum))
        top = jnp.max(high, axis=0, keepdims=True)
        total = jnp.zeros((8, 2 * B), F32)
        for r in range(RB):
            term = jnp.exp(kernel[r * B : (r + 1) * B, lanes] - top)
            kernel[r * B : (r + 1) * B, lanes] = term
            total = total + fold(term, jnp.add)
        total = top + jnp.log(jnp.maximum(jnp.sum(total, axis=0, keepdims=True), TINY))
        for k in range(2):
            peaks[pl.ds(2 * h + k, 1), :] = top[:, k * B : (k + 1) * B]
            out[0, pl.ds(2 * h + k, 1), :] = total[:, k * B : (k + 1) * B]
        return carry

    lax.fori_loop(0, DB // 2, pair, 0)
    for k in range(1, DPEERS):
        out[k] = out[0]


def row_sums(kernel, weight, out):
    c = lax.axis_index("c")

    def block(r, carry):
        rows = pl.ds(pl.multiple_of(r * B, B), B)
        acc = kernel[rows, 0:B] * weight[0:1]
        for k in range(1, DB):
            acc = acc + kernel[rows, k * B : (k + 1) * B] * weight[k : k + 1]
        place = r + c - 2 * c * (r % 2)
        out[0, pl.ds(place, 1), :] = jnp.sum(acc.T, axis=0, keepdims=True)
        return carry

    lax.fori_loop(0, RB, block, 0)
    for k in range(1, RPEERS):
        out[k] = out[0]


def column_sums(kernel, fcol, state):
    def block(r, acc):
        for k in range(B // 8):
            rows = pl.ds(pl.multiple_of(r * B + 8 * k, 8), 8)
            f = fcol[rows, :]
            acc = tuple(a + kernel[rows, j * B : (j + 1) * B] * f for j, a in enumerate(acc))
        return acc

    acc = lax.fori_loop(0, RB, block, tuple(jnp.zeros((8, B), F32) for _ in range(DB)))
    rows = jnp.concatenate([jnp.sum(a, axis=0, keepdims=True) for a in acc], axis=0)
    return rows * state[2 * DB : 3 * DB]


def rider_second_body(sums, peaks, driver, kernel, out, state, weight):
    log_b = jnp.concatenate([weight_row(driver[k]) for k in range(DB)], axis=0)
    pot = log_b - (log_total(sums, DPEERS) - LOG_RIDERS)
    scale = jnp.exp(pot + peaks[...])
    state[0:DB] = pot
    state[DB : 2 * DB] = log_b
    state[2 * DB : 3 * DB] = scale
    weight[...] = scale
    row_sums(kernel, weight, out)


def spread_columns(f, fcol, hold):
    c = lax.axis_index("c")
    hold[...] = f
    for p in range(RB // 2):
        fcol[2 * p * B : (2 * p + 1) * B, :] = column(hold[pl.ds(2 * p + c, 1), :])
        fcol[(2 * p + 1) * B : (2 * p + 2) * B, :] = column(hold[pl.ds(2 * p + 1 - c, 1), :])


def driver_next_body(sums, pots, state, kernel, out, fcol, hold):
    f = jnp.exp(pots[RB:] + LOG_DRIVERS) / total_of(sums, RPEERS)
    spread_columns(f, fcol, hold)
    rows = column_sums(kernel, fcol, state)
    for k in range(DPEERS):
        out[k] = rows


def rider_next_body(sums, state, kernel, out, weight):
    g = jnp.exp(state[DB : 2 * DB] + LOG_RIDERS) / total_of(sums, DPEERS)
    weight[...] = state[2 * DB : 3 * DB] * g
    row_sums(kernel, weight, out)


def driver_last_body(sums, pots, state, kernel, out, rider_pot, fcol, hold):
    total = total_of(sums, RPEERS)
    log_a = pots[RB:]
    hold[...] = pots[0:RB] + (log_a + LOG_DRIVERS - jnp.log(total))
    block = lax.axis_index("yl") * 4 + lax.axis_index("x")
    rider_pot[0:1] = hold[pl.ds(2 * block, 1), :]
    rider_pot[1:2] = hold[pl.ds(2 * block + 1, 1), :]
    spread_columns(jnp.exp(log_a + LOG_DRIVERS) / total, fcol, hold)
    rows = column_sums(kernel, fcol, state)
    for k in range(DPEERS):
        out[k] = jnp.broadcast_to(rows[k : k + 1], (8, B))


def finish_body(sums, state, driver_pot):
    z = lax.axis_index("z")
    pot = state[pl.ds(z, 1), :]
    log_b = state[pl.ds(DB + z, 1), :]
    driver_pot[...] = pot + (log_b + LOG_RIDERS - jnp.log(total_of(sums, DPEERS)[0:1]))


def exchange(message, axes):
    return lax.all_to_all(message, axes, 0, 0, tiled=True)


def swap_core(value):
    return lax.ppermute(value, "c", [(0, 1), (1, 0)])


def per_device(rider_emb, driver_emb, log_a, log_b, rider_zone, driver_zone, zone_table):
    rider_msg, driver_msg = call(
        pack_body,
        [bf16(8, PAY, B), bf16(8, PAY, B)],
        [FAR] * 7,
        [
            pltpu.VMEM((1, B), F32),
            pltpu.VMEM((1, B), F32),
            pltpu.SMEM((2,), jnp.int32),
            pltpu.SMEM((1,), jnp.int32),
            pltpu.SMEM((16, 16), jnp.int32),
            pltpu.VMEM((2, 16, B), BF16),
            pltpu.SemaphoreType.DMA((37,)),
        ],
        limit=60,
        to=FAR,
    )(
        rider_emb.reshape(2, B, B), driver_emb, log_a.reshape(2, B), log_b.reshape(1, B),
        rider_zone, driver_zone, zone_table,
    )
    own = exchange(rider_msg, ("yl", "x"))
    other = swap_core(own)
    driver = exchange(driver_msg, ("z",))
    (message,) = call(
        rider_first_body, [f32(RPEERS, RB, B)], [VM] * 3, [pltpu.VMEM((DB, 16, B), BF16)]
    )(own, other, driver)
    sums = exchange(message, RGROUP)
    columns = pltpu.VMEM((RB * B, B), F32)
    message, kernel, peaks, pots = call(
        driver_first_body,
        [f32(DPEERS, DB, B), f32(RB * B, DB * B), f32(DB, B), f32(2 * RB, B)],
        [VM] * 4,
        [columns],
    )(sums, own, other, driver)
    sums = exchange(message, DGROUP)
    weights = [pltpu.VMEM((DB, B), F32)]
    columns = [columns, pltpu.VMEM((RB, B), F32)]
    message, state = call(
        rider_second_body, [f32(RPEERS, RB, B), f32(3 * DB, B)], [VM] * 4, weights
    )(sums, peaks, driver, kernel)
    sums = exchange(message, RGROUP)
    for _ in range(ITERS - 2):
        (message,) = call(driver_next_body, [f32(DPEERS, DB, B)], [VM] * 4, columns)(
            sums, pots, state, kernel
        )
        sums = exchange(message, DGROUP)
        (message,) = call(rider_next_body, [f32(RPEERS, RB, B)], [VM] * 3, weights)(
            sums, state, kernel
        )
        sums = exchange(message, RGROUP)
    message, rider_pot = call(
        driver_last_body, [f32(DPEERS, 8, B), f32(2, B)], [VM] * 4, columns
    )(sums, pots, state, kernel)
    sums = exchange(message, DGROUP)
    (driver_pot,) = call(finish_body, [f32(1, B)], [VM] * 2)(sums, state)
    return rider_pot.reshape(2 * B), driver_pot.reshape(B)


def solution(mesh):
    fine = Mesh(mesh.devices.reshape(SIZES), AXES)
    row, every = ("z", "yl", "x"), AXES
    placed = (
        P(row, None),
        P(every, None),
        P(row),
        P(every),
        P(row),
        P(every),
        P(),
    )
    return jax.shard_map(
        per_device,
        mesh=fine,
        in_specs=placed,
        out_specs=(P(row), P(every)),
        check_vma=False,
    )
```

time: 131 us -> 139 us (1.061)
  the two profiles are of different devices: /device:TPU:1 before, /device:TPU:2 now
where the time goes in v2:
time: 139 us; the launch traced here: 137 us
  blocking collectives  82.7 us (59%)
  Pallas kernels  33.9 us (24%)
  waiting for transfers between devices  11.1 us (8%)
  starting transfers between devices  8.47 us (6%)
    all_to_all x7, blocking collectives, exchange(): return lax.all_to_all(message, axes, 0, 0, tiled=True)  82.7 us
    pallas_call x1, Pallas kernels, per_device(): call(pack_body, [bf16(8, PAY, B), bf16(8, PAY, B)], [FAR] * 7, [pltpu.VME...  17.3 us
    all_to_all x1, waiting for transfers between devices, exchange(): return lax.all_to_all(message, axes, 0, 0, tiled=True)  11.1 us
    all_to_all x1, starting transfers between devices, exchange(): return lax.all_to_all(message, axes, 0, 0, tiled=True)  8.47 us
    pallas_call x1, Pallas kernels, per_device(): call(driver_first_body, [f32(DPEERS, DB, B), f32(RB * B, DB * B), f32(DB,...  5.07 us
    pallas_call x1, Pallas kernels, per_device(): call(rider_first_body, [f32(RPEERS, RB, B)], [VM] * 3, [pltpu.VMEM((DB, 1...  4.55 us
  transfers between devices with their start and end apart: 2, of which 1 were waited for; matrix products, arithmetic and copies ran while one was open for 0% of the time, Pallas kernels for 0%

profile of v2, /device:TPU:2, one launch (start us, length us, event | category | flops | bytes accessed | tf_op | source)
XLA Modules:
  0.0 137.5 jit_solution(17243371786862366181)
XLA Ops:
  1.3 17.3 %shard_map.86 = (bf16[8,144,128]{2,1,0:T(8,128)(2,1)}, bf16[8,144,128]{2,1,0:T(8,128)(2,1)}) custom-call(bf16[2,128,128]{2,1,0:T(8,128)(2,1)} %bitcast.5, bf16[128,128]{1,0:T(8,128)(2,1)} %driver.1, f32[2,128]{1,0:T(2,128)} %bitcast.6, f32[1,128]{1,0:T(1,128)} %bitcast.7, s32[2]{0:T(128)} %rzone.1, s32[1]{0:T(128)S(6)} %copy.9.dzone, s32[16,16]{1,0:T(8,128)} %table.1), custom_call_target="tpu_custom_call" | custom-call | tf_op jit(solution)/shard_map/pallas_call | solution.py:309
  18.6 12.3 %all_to_all.40.own = bf16[8,144,128]{2,1,0:T(8,128)(2,1)S(1)} all-to-all(bf16[8,144,128]{2,1,0:T(8,128)(2,1)} %get-tuple-element.12), channel_id=1, replica_groups=mesh['z'=8,'yl'=2,'x'=4,'yh'=2,'c'=2] {'yl','x'}, dimensions={0} | all-to-all | bytes 589824 | tf_op jit(solution)/shard_map/all_to_all | solution.py:301
  30.9 8.5 %all-to-all-start.1 = ((bf16[8,144,128]{2,1,0:T(8,128)(2,1)}), bf16[8,144,128]{2,1,0:T(8,128)(2,1)S(1)}, u32[]{:S(2)}, u32[]{:S(2)}) async-start(bf16[8,144,128]{2,1,0:T(8,128)(2,1)} %get-tuple-element.13), calls=%async_computation.1 | async-start | bytes 589824 | tf_op jit(solution)/shard_map/all_to_all | solution.py:301
  39.4 0.0 collective-permute-start
  39.4 11.1 %all-to-all-done.1.driver = bf16[8,144,128]{2,1,0:T(8,128)(2,1)S(1)} async-done(((bf16[8,144,128]{2,1,0:T(8,128)(2,1)}), bf16[8,144,128]{2,1,0:T(8,128)(2,1)S(1)}, u32[]{:S(2)}, u32[]{:S(2)}) %all-to-all-start.1) | async-done | bytes 294944 | tf_op jit(solution)/shard_map/all_to_all | solution.py:301
  50.5 0.0 collective-permute-done.other
  50.5 4.6 %shard_map.87 = f32[32,16,128]{2,1,0:T(8,128)S(1)} custom-call(bf16[8,144,128]{2,1,0:T(8,128)(2,1)S(1)} %all_to_all.40.own, bf16[8,144,128]{2,1,0:T(8,128)(2,1)S(1)} %collective-permute-done.other, bf16[8,144,128]{2,1,0:T(8,128)(2,1)S(1)} %all-to-all-done.1.driver), custom_call_target="tpu_custom_call" | custom-call | tf_op jit(solution)/shard_map/pallas_call | solution.py:331
  55.1 14.2 %all_to_all.41.sums = f32[32,16,128]{2,1,0:T(8,128)S(1)} all-to-all(f32[32,16,128]{2,1,0:T(8,128)S(1)} %shard_map.87), channel_id=1, replica_groups=mesh['z'=8,'yl'=2,'x'=4,'yh'=2,'c'=2] {'yl','x','yh','c'}, dimensions={0} | all-to-all | bytes 524288 | tf_op jit(solution)/shard_map/all_to_all | solution.py:301
  69.3 5.1 %shard_map.88 = (f32[8,8,128]{2,1,0:T(8,128)S(1)}, f32[2048,1024]{1,0:T(8,128)S(1)}, f32[8,128]{1,0:T(8,128)S(1)}, f32[32,128]{1,0:T(8,128)S(1)}) custom-call(f32[32,16,128]{2,1,0:T(8,128)S(1)} %all_to_all.41.sums, bf16[8,144,128]{2,1,0:T(8,128)(2,1)S(1)} %all_to_all.40.own, bf16[8,144,128]{2,1,0:T(8,128)(2,1)S(1)} %collective-permute-done.other, ...), custom_call_target="tpu_custom_call" | custom-call | tf_op jit(solution)/shard_map/pallas_call | solution.py:336
  74.4 10.4 %all_to_all.42.sums = f32[8,8,128]{2,1,0:T(8,128)S(1)} all-to-all(f32[8,8,128]{2,1,0:T(8,128)S(1)} %get-tuple-element.14), channel_id=1, replica_groups=mesh['z'=8,'yl'=2,'x'=4,'yh'=2,'c'=2] {'z'}, dimensions={0} | all-to-all | bytes 65536 | tf_op jit(solution)/shard_map/all_to_all | solution.py:301
  84.8 1.9 %shard_map.89 = (f32[32,16,128]{2,1,0:T(8,128)S(1)}, f32[24,128]{1,0:T(8,128)S(1)}) custom-call(f32[8,8,128]{2,1,0:T(8,128)S(1)} %all_to_all.42.sums, f32[8,128]{1,0:T(8,128)S(1)} %get-tuple-element.15.peaks, bf16[8,144,128]{2,1,0:T(8,128)(2,1)S(1)} %all-to-all-done.1.driver, f32[2048,1024]{1,0:T(8,128)S(1)} %get-tuple-element.16.kernel), custom_call_target="tpu_custom_call" | custom-call | tf_op jit(solution)/shard_map/pallas_call | solution.py:345
  86.7 12.5 %all_to_all.43.sums = f32[32,16,128]{2,1,0:T(8,128)S(1)} all-to-all(f32[32,16,128]{2,1,0:T(8,128)S(1)} %get-tuple-element.17), channel_id=1, replica_groups=mesh['z'=8,'yl'=2,'x'=4,'yh'=2,'c'=2] {'yl','x','yh','c'}, dimensions={0} | all-to-all | bytes 524288 | tf_op jit(solution)/shard_map/all_to_all | solution.py:301
  99.2 1.0 shard_map.90
  100.2 10.4 %all_to_all.44.sums = f32[8,8,128]{2,1,0:T(8,128)S(1)} all-to-all(f32[8,8,128]{2,1,0:T(8,128)S(1)} %shard_map.90), channel_id=1, replica_groups=mesh['z'=8,'yl'=2,'x'=4,'yh'=2,'c'=2] {'z'}, dimensions={0} | all-to-all | bytes 65536 | tf_op jit(solution)/shard_map/all_to_all | solution.py:301
  110.6 1.9 %shard_map.91 = f32[32,16,128]{2,1,0:T(8,128)S(1)} custom-call(f32[8,8,128]{2,1,0:T(8,128)S(1)} %all_to_all.44.sums, f32[24,128]{1,0:T(8,128)S(1)} %get-tuple-element.19.state, f32[2048,1024]{1,0:T(8,128)S(1)} %get-tuple-element.16.kernel), custom_call_target="tpu_custom_call" | custom-call | tf_op jit(solution)/shard_map/pallas_call | solution.py:354
  112.5 12.5 %all_to_all.45.sums = f32[32,16,128]{2,1,0:T(8,128)S(1)} all-to-all(f32[32,16,128]{2,1,0:T(8,128)S(1)} %shard_map.91), channel_id=1, replica_groups=mesh['z'=8,'yl'=2,'x'=4,'yh'=2,'c'=2] {'yl','x','yh','c'}, dimensions={0} | all-to-all | bytes 524288 | tf_op jit(solution)/shard_map/all_to_all | solution.py:301
  125.0 1.5 %shard_map.92 = (f32[8,8,128]{2,1,0:T(8,128)S(1)}, f32[2,128]{1,0:T(2,128)}) custom-call(f32[32,16,128]{2,1,0:T(8,128)S(1)} %all_to_all.45.sums, f32[32,128]{1,0:T(8,128)S(1)} %get-tuple-element.18.pots, f32[24,128]{1,0:T(8,128)S(1)} %get-tuple-element.19.state, f32[2048,1024]{1,0:T(8,128)S(1)} %get-tuple-element.16.kernel), custom_call_target="tpu_custom_call" | custom-call | tf_op jit(solution)/shard_map/pallas_call | solution.py:358
  126.6 10.4 %all_to_all.46.sums = f32[8,8,128]{2,1,0:T(8,128)S(1)} all-to-all(f32[8,8,128]{2,1,0:T(8,128)S(1)} %get-tuple-element.21), channel_id=1, replica_groups=mesh['z'=8,'yl'=2,'x'=4,'yh'=2,'c'=2] {'z'}, dimensions={0} | all-to-all | bytes 65536 | tf_op jit(solution)/shard_map/all_to_all | solution.py:301
  136.9 0.5 shard_map.93
Async XLA Ops:
  30.9 19.6 %all-to-all-start.1 = ((bf16[8,144,128]{2,1,0:T(8,128)(2,1)}), bf16[8,144,128]{2,1,0:T(8,128)(2,1)S(1)}, u32[]{:S(2)}, u32[]{:S(2)}) async-start(bf16[8,144,128]{2,1,0:T(8,128)(2,1)} %get-tuple-element.13), calls=%async_computation.1 | async-start | bytes 589824 | tf_op jit(solution)/shard_map/all_to_all | solution.py:301
  39.4 11.1 %collective-permute-start = (bf16[8,144,128]{2,1,0:T(8,128)(2,1)S(1)}, bf16[8,144,128]{2,1,0:T(8,128)(2,1)S(1)}, u32[]{:S(2)}, u32[]{:S(2)}) collective-permute-start(bf16[8,144,128]{2,1,0:T(8,128)(2,1)S(1)} %all_to_all.40.own), channel_id=1, source_target_pairs={{0,1},{1,0},{2,3},{3,2},{4,5},{5,4},{6,7},{7,6},{8,9},{9,8},{10,11... | collective-permute-start | bytes 884744 | tf_op jit(solution)/shard_map/ppermute | solution.py:305

commit v3 on v2

--- a/solution.py
+++ b/solution.py
@@ -97,24 +97,20 @@
 
 
 def pack_body(rider, driver, log_a, log_b, rzone, dzone, table, rider_out, driver_out,
-              a_row, b_row, rz, dz, tab, tails, sems):
+              a_row, b_row, rz, dz, tab, message, sems):
     c = lax.axis_index("c")
-    small = [
-        pltpu.make_async_copy(log_a.at[pl.ds(c, 1)], a_row, sems.at[0]),
-        pltpu.make_async_copy(log_b, b_row, sems.at[1]),
-        pltpu.make_async_copy(rzone, rz, sems.at[2]),
-        pltpu.make_async_copy(dzone, dz, sems.at[3]),
-        pltpu.make_async_copy(table, tab, sems.at[4]),
+    copies = [
+        pltpu.make_async_copy(rider.at[c], message.at[0, pl.ds(0, B)], sems.at[0]),
+        pltpu.make_async_copy(driver, message.at[1, pl.ds(0, B)], sems.at[1]),
+        pltpu.make_async_copy(log_a.at[pl.ds(c, 1)], a_row, sems.at[2]),
+        pltpu.make_async_copy(log_b, b_row, sems.at[3]),
+        pltpu.make_async_copy(rzone, rz, sems.at[4]),
+        pltpu.make_async_copy(dzone, dz, sems.at[5]),
+        pltpu.make_async_copy(table, tab, sems.at[6]),
     ]
-    for copy in small:
+    for copy in copies:
         copy.start()
-    large = []
-    for k in range(8):
-        large.append(pltpu.make_async_copy(rider.at[c], rider_out.at[k, pl.ds(0, B)], sems.at[5 + k]))
-        large.append(pltpu.make_async_copy(driver, driver_out.at[k, pl.ds(0, B)], sems.at[13 + k]))
-    for copy in large:
-        copy.start()
-    for copy in small:
+    for copy in copies:
         copy.wait()
     lane = lax.broadcasted_iota(jnp.int32, (16, B), 1)
     hot = jnp.where(lane == rz[c], 1.0, 0.0)
@@ -122,44 +118,53 @@
     shut = jnp.zeros((16, B), F32)
     for k in range(16):
         shut = jnp.where((lane == k) & (tab[k, zone] != 1), PENALTY, shut)
-    tails[0] = tail_rows(hot, a_row[...])
-    tails[1] = tail_rows(shut, b_row[...])
-    ends = []
+    message[0, B:, :] = tail_rows(hot, a_row[...])
+    message[1, B:, :] = tail_rows(shut, b_row[...])
+    copies = [pltpu.make_async_copy(message.at[0], rider_out.at[0], sems.at[7])]
     for k in range(8):
-        ends.append(pltpu.make_async_copy(tails.at[0], rider_out.at[k, pl.ds(B, 16)], sems.at[21 + k]))
-        ends.append(pltpu.make_async_copy(tails.at[1], driver_out.at[k, pl.ds(B, 16)], sems.at[29 + k]))
-    for copy in ends:
+        copies.append(pltpu.make_async_copy(message.at[1], driver_out.at[k], sems.at[8 + k]))
+    for copy in copies:
         copy.start()
-    for copy in large + ends:
+    for copy in copies:
         copy.wait()
 
 
-def rider_first_body(own, other, driver, out, dzone):
+def place(far, slot):
+    yl, x = lax.axis_index("yl"), lax.axis_index("x")
+    first, second = slot % 2, slot // 2
+    x = x + far * (3 - 2 * x)
+    x = x + second * (1 - 2 * (x % 2))
+    return (yl + first * (1 - 2 * yl)) * 4 + x
+
+
+def rider_first_body(own_near, own_far, other_near, other_far, driver, out, dzone):
     c = lax.axis_index("c")
     for z in range(DB):
         dzone[z] = zone_rows(driver[z])
 
-    def pair(p, carry):
-        mine, theirs = own[p], other[p]
-        right = jnp.concatenate(
-            [with_zone(mine, zone_rows(mine)), with_zone(theirs, zone_rows(theirs))], axis=0
-        )
-        peak = jnp.full((8, 2 * B), -3e38, F32)
-        mass = jnp.zeros((8, 2 * B), F32)
-        for z in range(DB):
-            cost = product(with_zone(driver[z], dzone[z]), right)
-            fresh = jnp.maximum(peak, -fold(cost, jnp.minimum))
-            terms = jnp.exp(-cost - jnp.concatenate([fresh] * 16, axis=0))
-            mass = mass * jnp.exp(peak - fresh) + fold(terms, jnp.add)
-            peak = fresh
-        top = jnp.max(peak, axis=0, keepdims=True)
-        mass = jnp.sum(mass * jnp.exp(peak - top), axis=0, keepdims=True)
-        total = top + jnp.log(mass)
-        out[0, pl.ds(2 * p + c, 1), :] = total[:, :B]
-        out[0, pl.ds(2 * p + 1 - c, 1), :] = total[:, B:]
+    def pair(slot, carry):
+        for far, (own, other) in enumerate(((own_near, other_near), (own_far, other_far))):
+            mine, theirs = own[slot], other[slot]
+            right = jnp.concatenate(
+                [with_zone(mine, zone_rows(mine)), with_zone(theirs, zone_rows(theirs))], axis=0
+            )
+            peak = jnp.full((8, 2 * B), -3e38, F32)
+            mass = jnp.zeros((8, 2 * B), F32)
+            for z in range(DB):
+                cost = product(with_zone(driver[z], dzone[z]), right)
+                fresh = jnp.maximum(peak, -fold(cost, jnp.minimum))
+                terms = jnp.exp(-cost - jnp.concatenate([fresh] * 16, axis=0))
+                mass = mass * jnp.exp(peak - fresh) + fold(terms, jnp.add)
+                peak = fresh
+            top = jnp.max(peak, axis=0, keepdims=True)
+            mass = jnp.sum(mass * jnp.exp(peak - top), axis=0, keepdims=True)
+            total = top + jnp.log(mass)
+            p = place(far, slot)
+            out[0, pl.ds(2 * p + c, 1), :] = total[:, :B]
+            out[0, pl.ds(2 * p + 1 - c, 1), :] = total[:, B:]
         return carry
 
-    lax.fori_loop(0, RB // 2, pair, 0)
+    lax.fori_loop(0, RB // 4, pair, 0)
     for k in range(1, RPEERS):
         out[k] = out[0]
 
@@ -174,15 +179,20 @@
     return tree([sums[k] for k in range(peers)], jnp.add)
 
 
-def driver_first_body(sums, own, other, driver, out, kernel, peaks, pots, ucol):
+def block_of(r):
     c = lax.axis_index("c")
-    for p in range(RB // 2):
-        pots[pl.ds(RB + 2 * p + c, 1), :] = weight_row(own[p])
-        pots[pl.ds(RB + 2 * p + 1 - c, 1), :] = weight_row(other[p])
+    other = r % 2
+    return 2 * place(r // 8, r // 2 % 4) + c + other * (1 - 2 * c)
+
+
+def driver_first_body(sums, own_near, own_far, other_near, other_far, driver, out, kernel, peaks, pots, ucol):
+    own = [own_near[k] for k in range(4)] + [own_far[k] for k in range(4)]
+    other = [other_near[k] for k in range(4)] + [other_far[k] for k in range(4)]
+    for r in range(RB):
+        pots[pl.ds(RB + block_of(r), 1), :] = weight_row((other if r % 2 else own)[r // 2])
     pots[0:RB] = pots[RB:] - (log_total(sums, RPEERS) - LOG_DRIVERS)
-    for p in range(RB // 2):
-        ucol[2 * p * B : (2 * p + 1) * B, :] = column(pots[pl.ds(2 * p + c, 1), :])
-        ucol[(2 * p + 1) * B : (2 * p + 2) * B, :] = column(pots[pl.ds(2 * p + 1 - c, 1), :])
+    for r in range(RB):
+        ucol[r * B : (r + 1) * B, :] = column(pots[pl.ds(block_of(r), 1), :])
 
     def pair(h, carry):
         one, two = driver[2 * h], driver[2 * h + 1]
@@ -193,7 +203,7 @@
         high = jnp.full((8, 2 * B), FLOOR, F32)
         for r in range(RB):
             u = ucol[r * B : (r + 1) * B, :]
-            left = own[r // 2] if r % 2 == 0 else other[r // 2]
+            left = (other if r % 2 else own)[r // 2]
             score = jnp.concatenate([u, u], axis=1) - product(with_zone(left, zone_rows(left)), right)
             kernel[r * B : (r + 1) * B, lanes] = score
             high = jnp.maximum(high, fold(score, jnp.maximum))
@@ -215,15 +225,12 @@
 
 
 def row_sums(kernel, weight, out):
-    c = lax.axis_index("c")
-
     def block(r, carry):
         rows = pl.ds(pl.multiple_of(r * B, B), B)
         acc = kernel[rows, 0:B] * weight[0:1]
         for k in range(1, DB):
             acc = acc + kernel[rows, k * B : (k + 1) * B] * weight[k : k + 1]
-        place = r + c - 2 * c * (r % 2)
-        out[0, pl.ds(place, 1), :] = jnp.sum(acc.T, axis=0, keepdims=True)
+        out[0, pl.ds(block_of(r), 1), :] = jnp.sum(acc.T, axis=0, keepdims=True)
         return carry
 
     lax.fori_loop(0, RB, block, 0)
@@ -256,11 +263,9 @@
 
 
 def spread_columns(f, fcol, hold):
-    c = lax.axis_index("c")
     hold[...] = f
-    for p in range(RB // 2):
-        fcol[2 * p * B : (2 * p + 1) * B, :] = column(hold[pl.ds(2 * p + c, 1), :])
-        fcol[(2 * p + 1) * B : (2 * p + 2) * B, :] = column(hold[pl.ds(2 * p + 1 - c, 1), :])
+    for r in range(RB):
+        fcol[r * B : (r + 1) * B, :] = column(hold[pl.ds(block_of(r), 1), :])
 
 
 def driver_next_body(sums, pots, state, kernel, out, fcol, hold):
@@ -301,14 +306,21 @@
     return lax.all_to_all(message, axes, 0, 0, tiled=True)
 
 
-def swap_core(value):
-    return lax.ppermute(value, "c", [(0, 1), (1, 0)])
+def swap(value, axis, partner):
+    return lax.ppermute(value, axis, [(k, partner(k)) for k in range(SIZES[AXES.index(axis)])])
+
+
+def gather_riders(message):
+    near = jnp.concatenate([message, swap(message, "yl", lambda k: 1 - k)], axis=0)
+    near = jnp.concatenate([near, swap(near, "x", lambda k: k ^ 1)], axis=0)
+    far = swap(near, "x", lambda k: 3 - k)
+    return near, far, swap(near, "c", lambda k: 1 - k), swap(far, "c", lambda k: 1 - k)
 
 
 def per_device(rider_emb, driver_emb, log_a, log_b, rider_zone, driver_zone, zone_table):
     rider_msg, driver_msg = call(
         pack_body,
-        [bf16(8, PAY, B), bf16(8, PAY, B)],
+        [bf16(1, PAY, B), bf16(8, PAY, B)],
         [FAR] * 7,
         [
             pltpu.VMEM((1, B), F32),
@@ -316,8 +328,8 @@
             pltpu.SMEM((2,), jnp.int32),
             pltpu.SMEM((1,), jnp.int32),
             pltpu.SMEM((16, 16), jnp.int32),
-            pltpu.VMEM((2, 16, B), BF16),
-            pltpu.SemaphoreType.DMA((37,)),
+            pltpu.VMEM((2, PAY, B), BF16),
+            pltpu.SemaphoreType.DMA((16,)),
         ],
         limit=60,
         to=FAR,
@@ -325,20 +337,19 @@
         rider_emb.reshape(2, B, B), driver_emb, log_a.reshape(2, B), log_b.reshape(1, B),
         rider_zone, driver_zone, zone_table,
     )
-    own = exchange(rider_msg, ("yl", "x"))
-    other = swap_core(own)
+    riders = gather_riders(rider_msg)
     driver = exchange(driver_msg, ("z",))
     (message,) = call(
-        rider_first_body, [f32(RPEERS, RB, B)], [VM] * 3, [pltpu.VMEM((DB, 16, B), BF16)]
-    )(own, other, driver)
+        rider_first_body, [f32(RPEERS, RB, B)], [VM] * 5, [pltpu.VMEM((DB, 16, B), BF16)]
+    )(*riders, driver)
     sums = exchange(message, RGROUP)
     columns = pltpu.VMEM((RB * B, B), F32)
     message, kernel, peaks, pots = call(
         driver_first_body,
         [f32(DPEERS, DB, B), f32(RB * B, DB * B), f32(DB, B), f32(2 * RB, B)],
-        [VM] * 4,
+        [VM] * 6,
         [columns],
-    )(sums, own, other, driver)
+    )(sums, *riders, driver)
     sums = exchange(message, DGROUP)
     weights = [pltpu.VMEM((DB, B), F32)]
     columns = [columns, pltpu.VMEM((RB, B), F32)]

time: 139 us -> 122 us (0.88)
  Pallas kernels: 33.9 us -> 17.7 us
  blocking collectives: 82.7 us -> 77.1 us
  starting transfers between devices: 8.47 us -> 12.2 us
    pallas_call x2, Pallas kernels: 21.9 us -> 5.63 us  [the longest x1 3.77 us: per_device(): call(rider_first_body, [f32(RPEERS, RB, B)], [VM] * 5, [pltpu.VMEM((DB, 1...]
    all_to_all x1, waiting for transfers between devices: 11.1 us -> 0.01 us  [exchange(): return lax.all_to_all(message, axes, 0, 0, tiled=True)]
    ppermute x1 -> x5, waiting for transfers between devices: 0.01 us -> 10.6 us  [swap(): lax.ppermute(value, axis, [(k, partner(k)) for k in range(SIZES[AXES.inde...]
    all_to_all x7 -> x6, blocking collectives: 82.7 us -> 77.1 us  [exchange(): return lax.all_to_all(message, axes, 0, 0, tiled=True)]
    ppermute x1 -> x5, starting transfers between devices: 0.01 us -> 3.69 us  [swap(): lax.ppermute(value, axis, [(k, partner(k)) for k in range(SIZES[AXES.inde...]
  transfers between devices with their start and end apart: 2 -> 6, of which waited for: 1 -> 4; matrix products, arithmetic and copies ran while one was open for 0% -> 1% of each run, Pallas kernels for 0% -> 0%
where the time goes in v3:
time: 122 us; the launch traced here: 121 us
  blocking collectives  77.1 us (63%)
  Pallas kernels  17.7 us (15%)
  starting transfers between devices  12.2 us (10%)
  waiting for transfers between devices  10.6 us (9%)
  between operations  1.33 us (1%)
    all_to_all x6, blocking collectives, exchange(): return lax.all_to_all(message, axes, 0, 0, tiled=True)  77.1 us
    ppermute x5, waiting for transfers between devices, swap(): lax.ppermute(value, axis, [(k, partner(k)) for k in range(SIZES[AXES.inde...  10.6 us
    all_to_all x1, starting transfers between devices, exchange(): return lax.all_to_all(message, axes, 0, 0, tiled=True)  8.48 us
    pallas_call x1, Pallas kernels, per_device(): call(driver_first_body, [f32(DPEERS, DB, B), f32(RB * B, DB * B), f32(DB,...  5.18 us
    pallas_call x1, Pallas kernels, per_device(): call(rider_first_body, [f32(RPEERS, RB, B)], [VM] * 5, [pltpu.VMEM((DB, 1...  3.77 us
    ppermute x5, starting transfers between devices, swap(): lax.ppermute(value, axis, [(k, partner(k)) for k in range(SIZES[AXES.inde...  3.69 us
  transfers between devices with their start and end apart: 6, of which 4 were waited for; matrix products, arithmetic and copies ran while one was open for 1% of the time, Pallas kernels for 0%

profile of v3, /device:TPU:2, one launch (start us, length us, event | category | flops | bytes accessed | tf_op | source)
XLA Modules:
  0.0 120.5 jit_solution(2374906759752726527)
XLA Ops:
  1.3 1.9 %shard_map.86 = (bf16[1,144,128]{2,1,0:T(8,128)(2,1)}, bf16[8,144,128]{2,1,0:T(8,128)(2,1)}) custom-call(bf16[2,128,128]{2,1,0:T(8,128)(2,1)} %bitcast.5, bf16[128,128]{1,0:T(8,128)(2,1)} %driver.1, f32[2,128]{1,0:T(2,128)} %bitcast.6, f32[1,128]{1,0:T(1,128)} %bitcast.7, s32[2]{0:T(128)} %rzone.1, s32[1]{0:T(128)S(6)} %copy.11.dzone, s32[16,16]{1,0:T(8,128)} %table.1), custom_call_target="tpu_custom_call" | custom-call | tf_op jit(solution)/shard_map/pallas_call | solution.py:321
  3.1 8.5 %all-to-all-start = ((bf16[8,144,128]{2,1,0:T(8,128)(2,1)}), bf16[8,144,128]{2,1,0:T(8,128)(2,1)S(1)}, u32[]{:S(2)}, u32[]{:S(2)}) async-start(bf16[8,144,128]{2,1,0:T(8,128)(2,1)} %get-tuple-element.13), calls=%async_computation | async-start | bytes 589824 | tf_op jit(solution)/shard_map/all_to_all | solution.py:306
  11.6 1.6 %collective-permute-start = (bf16[1,144,128]{2,1,0:T(8,128)(2,1)}, bf16[1,144,128]{2,1,0:T(8,128)(2,1)S(1)}, u32[]{:S(2)}, u32[]{:S(2)}) collective-permute-start(bf16[1,144,128]{2,1,0:T(8,128)(2,1)} %get-tuple-element.12), channel_id=1, source_target_pairs={{0,16},{16,0},{1,17},{17,1},{2,18},{18,2},{3,19},{19,3},{4,20},{20... | collective-permute-start | bytes 110600 | tf_op jit(solution)/shard_map/ppermute | solution.py:310
  13.2 0.8 constant_dynamic-update-slice_fusion.2
  14.0 1.8 %collective-permute-done = bf16[1,144,128]{2,1,0:T(8,128)(2,1)S(1)} collective-permute-done((bf16[1,144,128]{2,1,0:T(8,128)(2,1)}, bf16[1,144,128]{2,1,0:T(8,128)(2,1)S(1)}, u32[]{:S(2)}, u32[]{:S(2)}) %collective-permute-start) | collective-permute-done | bytes 36896 | tf_op jit(solution)/shard_map/ppermute | solution.py:310
  15.8 0.8 pad_maximum_fusion
  16.6 0.5 collective-permute-start.1
  17.1 3.8 %collective-permute-done.1 = bf16[2,144,128]{2,1,0:T(8,128)(2,1)S(1)} collective-permute-done((bf16[2,144,128]{2,1,0:T(8,128)(2,1)S(1)}, bf16[2,144,128]{2,1,0:T(8,128)(2,1)S(1)}, u32[]{:S(2)}, u32[]{:S(2)}) %collective-permute-start.1) | collective-permute-done | bytes 73760 | tf_op jit(solution)/shard_map/ppermute | solution.py:310
  20.9 1.6 %collective-permute-start.2 = (bf16[4,144,128]{2,1,0:T(8,128)(2,1)S(1)}, bf16[4,144,128]{2,1,0:T(8,128)(2,1)S(1)}, u32[]{:S(2)}, u32[]{:S(2)}) collective-permute-start(bf16[4,144,128]{2,1,0:T(8,128)(2,1)S(1)} %constant_dynamic-update-slice_fusion.own_near), channel_id=1, source_target_pairs={{0,12},{4,8},{8,4},{12,0},{1,13},{5,9},{9,5},{13,1},{2,14},{6,10},... | collective-permute-start | bytes 442376 | tf_op jit(solution)/shard_map/ppermute | solution.py:310
  22.5 0.0 collective-permute-start.3
  22.5 3.6 %collective-permute-done.2.own_far = bf16[4,144,128]{2,1,0:T(8,128)(2,1)S(1)} collective-permute-done((bf16[4,144,128]{2,1,0:T(8,128)(2,1)S(1)}, bf16[4,144,128]{2,1,0:T(8,128)(2,1)S(1)}, u32[]{:S(2)}, u32[]{:S(2)}) %collective-permute-start.2) | collective-permute-done | bytes 147488 | tf_op jit(solution)/shard_map/ppermute | solution.py:310
  26.2 0.0 collective-permute-start.4
  26.2 0.0 collective-permute-done.3.other_near
  26.2 1.4 %collective-permute-done.4.other_far = bf16[4,144,128]{2,1,0:T(8,128)(2,1)S(1)} collective-permute-done((bf16[4,144,128]{2,1,0:T(8,128)(2,1)S(1)}, bf16[4,144,128]{2,1,0:T(8,128)(2,1)S(1)}, u32[]{:S(2)}, u32[]{:S(2)}) %collective-permute-start.4) | collective-permute-done | bytes 147488 | tf_op jit(solution)/shard_map/ppermute | solution.py:310
  27.5 0.0 all-to-all-done.driver
  27.5 3.8 %shard_map.87 = f32[32,16,128]{2,1,0:T(8,128)S(1)} custom-call(bf16[4,144,128]{2,1,0:T(8,128)(2,1)S(1)} %constant_dynamic-update-slice_fusion.own_near, bf16[4,144,128]{2,1,0:T(8,128)(2,1)S(1)} %collective-permute-done.2.own_far, bf16[4,144,128]{2,1,0:T(8,128)(2,1)S(1)} %collective-permute-done.3.other_near, ...), custom_call_target="tpu_custom_call" | custom-call | tf_op jit(solution)/shard_map/pallas_call | solution.py:342
  31.3 16.3 %all_to_all.35.sums = f32[32,16,128]{2,1,0:T(8,128)S(1)} all-to-all(f32[32,16,128]{2,1,0:T(8,128)S(1)} %shard_map.87), channel_id=1, replica_groups=mesh['z'=8,'yl'=2,'x'=4,'yh'=2,'c'=2] {'yl','x','yh','c'}, dimensions={0} | all-to-all | bytes 524288 | tf_op jit(solution)/shard_map/all_to_all | solution.py:306
  47.6 5.2 %shard_map.88 = (f32[8,8,128]{2,1,0:T(8,128)S(1)}, f32[2048,1024]{1,0:T(8,128)S(1)}, f32[8,128]{1,0:T(8,128)S(1)}, f32[32,128]{1,0:T(8,128)S(1)}) custom-call(f32[32,16,128]{2,1,0:T(8,128)S(1)} %all_to_all.35.sums, bf16[4,144,128]{2,1,0:T(8,128)(2,1)S(1)} %constant_dynamic-update-slice_fusion.own_near, ...), custom_call_target="tpu_custom_call" | custom-call | tf_op jit(solution)/shard_map/pallas_call | solution.py:347
  52.8 15.0 %all_to_all.36.sums = f32[8,8,128]{2,1,0:T(8,128)S(1)} all-to-all(f32[8,8,128]{2,1,0:T(8,128)S(1)} %get-tuple-element.14), channel_id=1, replica_groups=mesh['z'=8,'yl'=2,'x'=4,'yh'=2,'c'=2] {'z'}, dimensions={0} | all-to-all | bytes 65536 | tf_op jit(solution)/shard_map/all_to_all | solution.py:306
  67.8 1.9 %shard_map.89 = (f32[32,16,128]{2,1,0:T(8,128)S(1)}, f32[24,128]{1,0:T(8,128)S(1)}) custom-call(f32[8,8,128]{2,1,0:T(8,128)S(1)} %all_to_all.36.sums, f32[8,128]{1,0:T(8,128)S(1)} %get-tuple-element.15.peaks, bf16[8,144,128]{2,1,0:T(8,128)(2,1)S(1)} %all-to-all-done.driver, f32[2048,1024]{1,0:T(8,128)S(1)} %get-tuple-element.16.kernel), custom_call_target="tpu_custom_call" | custom-call | tf_op jit(solution)/shard_map/pallas_call | solution.py:356
  69.7 12.5 %all_to_all.37.sums = f32[32,16,128]{2,1,0:T(8,128)S(1)} all-to-all(f32[32,16,128]{2,1,0:T(8,128)S(1)} %get-tuple-element.17), channel_id=1, replica_groups=mesh['z'=8,'yl'=2,'x'=4,'yh'=2,'c'=2] {'yl','x','yh','c'}, dimensions={0} | all-to-all | bytes 524288 | tf_op jit(solution)/shard_map/all_to_all | solution.py:306
  82.3 1.0 shard_map.90
  83.3 10.4 %all_to_all.38.sums = f32[8,8,128]{2,1,0:T(8,128)S(1)} all-to-all(f32[8,8,128]{2,1,0:T(8,128)S(1)} %shard_map.90), channel_id=1, replica_groups=mesh['z'=8,'yl'=2,'x'=4,'yh'=2,'c'=2] {'z'}, dimensions={0} | all-to-all | bytes 65536 | tf_op jit(solution)/shard_map/all_to_all | solution.py:306
  93.7 1.9 %shard_map.91 = f32[32,16,128]{2,1,0:T(8,128)S(1)} custom-call(f32[8,8,128]{2,1,0:T(8,128)S(1)} %all_to_all.38.sums, f32[24,128]{1,0:T(8,128)S(1)} %get-tuple-element.19.state, f32[2048,1024]{1,0:T(8,128)S(1)} %get-tuple-element.16.kernel), custom_call_target="tpu_custom_call" | custom-call | tf_op jit(solution)/shard_map/pallas_call | solution.py:365
  95.6 12.5 %all_to_all.39.sums = f32[32,16,128]{2,1,0:T(8,128)S(1)} all-to-all(f32[32,16,128]{2,1,0:T(8,128)S(1)} %shard_map.91), channel_id=1, replica_groups=mesh['z'=8,'yl'=2,'x'=4,'yh'=2,'c'=2] {'yl','x','yh','c'}, dimensions={0} | all-to-all | bytes 524288 | tf_op jit(solution)/shard_map/all_to_all | solution.py:306
  108.1 1.5 %shard_map.92 = (f32[8,8,128]{2,1,0:T(8,128)S(1)}, f32[2,128]{1,0:T(2,128)}) custom-call(f32[32,16,128]{2,1,0:T(8,128)S(1)} %all_to_all.39.sums, f32[32,128]{1,0:T(8,128)S(1)} %get-tuple-element.18.pots, f32[24,128]{1,0:T(8,128)S(1)} %get-tuple-element.19.state, f32[2048,1024]{1,0:T(8,128)S(1)} %get-tuple-element.16.kernel), custom_call_target="tpu_custom_call" | custom-call | tf_op jit(solution)/shard_map/pallas_call | solution.py:369
  109.6 10.4 %all_to_all.40.sums = f32[8,8,128]{2,1,0:T(8,128)S(1)} all-to-all(f32[8,8,128]{2,1,0:T(8,128)S(1)} %get-tuple-element.21), channel_id=1, replica_groups=mesh['z'=8,'yl'=2,'x'=4,'yh'=2,'c'=2] {'z'}, dimensions={0} | all-to-all | bytes 65536 | tf_op jit(solution)/shard_map/all_to_all | solution.py:306
  120.0 0.5 shard_map.93
  (2 shorter events, 0.0 us)
Async XLA Ops:
  3.1 24.4 %all-to-all-start = ((bf16[8,144,128]{2,1,0:T(8,128)(2,1)}), bf16[8,144,128]{2,1,0:T(8,128)(2,1)S(1)}, u32[]{:S(2)}, u32[]{:S(2)}) async-start(bf16[8,144,128]{2,1,0:T(8,128)(2,1)} %get-tuple-element.13), calls=%async_computation | async-start | bytes 589824 | tf_op jit(solution)/shard_map/all_to_all | solution.py:306
  11.6 4.2 %collective-permute-start = (bf16[1,144,128]{2,1,0:T(8,128)(2,1)}, bf16[1,144,128]{2,1,0:T(8,128)(2,1)S(1)}, u32[]{:S(2)}, u32[]{:S(2)}) collective-permute-start(bf16[1,144,128]{2,1,0:T(8,128)(2,1)} %get-tuple-element.12), channel_id=1, source_target_pairs={{0,16},{16,0},{1,17},{17,1},{2,18},{18,2},{3,19},{19,3},{4,20},{20... | collective-permute-start | bytes 110600 | tf_op jit(solution)/shard_map/ppermute | solution.py:310
  16.6 4.4 %collective-permute-start.1 = (bf16[2,144,128]{2,1,0:T(8,128)(2,1)S(1)}, bf16[2,144,128]{2,1,0:T(8,128)(2,1)S(1)}, u32[]{:S(2)}, u32[]{:S(2)}) collective-permute-start(bf16[2,144,128]{2,1,0:T(8,128)(2,1)S(1)} %pad_maximum_fusion), channel_id=1, source_target_pairs={{0,4},{4,0},{8,12},{12,8},{1,5},{5,1},{9,13},{13,9},{2,6},{6,2},{1... | collective-permute-start | bytes 221192 | tf_op jit(solution)/shard_map/ppermute | solution.py:310
  20.9 5.2 %collective-permute-start.2 = (bf16[4,144,128]{2,1,0:T(8,128)(2,1)S(1)}, bf16[4,144,128]{2,1,0:T(8,128)(2,1)S(1)}, u32[]{:S(2)}, u32[]{:S(2)}) collective-permute-start(bf16[4,144,128]{2,1,0:T(8,128)(2,1)S(1)} %constant_dynamic-update-slice_fusion.own_near), channel_id=1, source_target_pairs={{0,12},{4,8},{8,4},{12,0},{1,13},{5,9},{9,5},{13,1},{2,14},{6,10},... | collective-permute-start | bytes 442376 | tf_op jit(solution)/shard_map/ppermute | solution.py:310
  22.5 3.7 %collective-permute-start.3 = (bf16[4,144,128]{2,1,0:T(8,128)(2,1)S(1)}, bf16[4,144,128]{2,1,0:T(8,128)(2,1)S(1)}, u32[]{:S(2)}, u32[]{:S(2)}) collective-permute-start(bf16[4,144,128]{2,1,0:T(8,128)(2,1)S(1)} %constant_dynamic-update-slice_fusion.own_near), channel_id=1, source_target_pairs={{0,1},{1,0},{2,3},{3,2},{4,5},{5,4},{6,7},{7,6},{8,9},{9,8},{10,11... | collective-permute-start | bytes 442376 | tf_op jit(solution)/shard_map/ppermute | solution.py:310
  26.2 1.4 %collective-permute-start.4 = (bf16[4,144,128]{2,1,0:T(8,128)(2,1)S(1)}, bf16[4,144,128]{2,1,0:T(8,128)(2,1)S(1)}, u32[]{:S(2)}, u32[]{:S(2)}) collective-permute-start(bf16[4,144,128]{2,1,0:T(8,128)(2,1)S(1)} %collective-permute-done.2.own_far), channel_id=1, source_target_pairs={{0,1},{1,0},{2,3},{3,2},{4,5},{5,4},{6,7},{7,6},{8,9},{9,8},{10,11... | collective-permute-start | bytes 442376 | tf_op jit(solution)/shard_map/ppermute | solution.py:310

commit v4 on v3

--- a/solution.py
+++ b/solution.py
@@ -31,12 +31,13 @@
 FAR = pl.BlockSpec(memory_space=pltpu.HBM)
 
 
-def call(body, outs, ins, scratch=(), limit=40, to=VM):
+def call(body, outs, ins, scratch=(), limit=40, to=None, cost=None):
     return pl.pallas_call(
         body,
         out_shape=outs,
         in_specs=ins,
-        out_specs=[to] * len(outs),
+        out_specs=to or [VM] * len(outs),
+        cost_estimate=cost,
         scratch_shapes=list(scratch),
         compiler_params=pltpu.CompilerParams(vmem_limit_bytes=limit * 2**20),
     )
@@ -100,8 +101,8 @@
               a_row, b_row, rz, dz, tab, message, sems):
     c = lax.axis_index("c")
     copies = [
-        pltpu.make_async_copy(rider.at[c], message.at[0, pl.ds(0, B)], sems.at[0]),
-        pltpu.make_async_copy(driver, message.at[1, pl.ds(0, B)], sems.at[1]),
+        pltpu.make_async_copy(rider.at[c], rider_out.at[0, pl.ds(0, B)], sems.at[0]),
+        pltpu.make_async_copy(driver, message.at[pl.ds(0, B)], sems.at[1]),
         pltpu.make_async_copy(log_a.at[pl.ds(c, 1)], a_row, sems.at[2]),
         pltpu.make_async_copy(log_b, b_row, sems.at[3]),
         pltpu.make_async_copy(rzone, rz, sems.at[4]),
@@ -118,11 +119,9 @@
     shut = jnp.zeros((16, B), F32)
     for k in range(16):
         shut = jnp.where((lane == k) & (tab[k, zone] != 1), PENALTY, shut)
-    message[0, B:, :] = tail_rows(hot, a_row[...])
-    message[1, B:, :] = tail_rows(shut, b_row[...])
-    copies = [pltpu.make_async_copy(message.at[0], rider_out.at[0], sems.at[7])]
-    for k in range(8):
-        copies.append(pltpu.make_async_copy(message.at[1], driver_out.at[k], sems.at[8 + k]))
+    rider_out[0, B:, :] = tail_rows(hot, a_row[...])
+    message[B:, :] = tail_rows(shut, b_row[...])
+    copies = [pltpu.make_async_copy(message, driver_out.at[k], sems.at[7 + k]) for k in range(8)]
     for copy in copies:
         copy.start()
     for copy in copies:
@@ -137,34 +136,42 @@
     return (yl + first * (1 - 2 * yl)) * 4 + x
 
 
-def rider_first_body(own_near, own_far, other_near, other_far, driver, out, dzone):
+def block_of(r):
     c = lax.axis_index("c")
+    other = r % 2
+    return 2 * place(r // 8, r // 2 % 4) + c + other * (1 - 2 * c)
+
+
+def rider_part(own, other, driver, rows, left):
     for z in range(DB):
-        dzone[z] = zone_rows(driver[z])
+        left[z * B : (z + 1) * B] = with_zone(driver[z], zone_rows(driver[z]))
 
     def pair(slot, carry):
-        for far, (own, other) in enumerate(((own_near, other_near), (own_far, other_far))):
-            mine, theirs = own[slot], other[slot]
-            right = jnp.concatenate(
-                [with_zone(mine, zone_rows(mine)), with_zone(theirs, zone_rows(theirs))], axis=0
-            )
-            peak = jnp.full((8, 2 * B), -3e38, F32)
-            mass = jnp.zeros((8, 2 * B), F32)
-            for z in range(DB):
-                cost = product(with_zone(driver[z], dzone[z]), right)
-                fresh = jnp.maximum(peak, -fold(cost, jnp.minimum))
-                terms = jnp.exp(-cost - jnp.concatenate([fresh] * 16, axis=0))
-                mass = mass * jnp.exp(peak - fresh) + fold(terms, jnp.add)
-                peak = fresh
-            top = jnp.max(peak, axis=0, keepdims=True)
-            mass = jnp.sum(mass * jnp.exp(peak - top), axis=0, keepdims=True)
-            total = top + jnp.log(mass)
-            p = place(far, slot)
-            out[0, pl.ds(2 * p + c, 1), :] = total[:, :B]
-            out[0, pl.ds(2 * p + 1 - c, 1), :] = total[:, B:]
+        mine, theirs = own[slot], other[slot]
+        right = jnp.concatenate(
+            [with_zone(mine, zone_rows(mine)), with_zone(theirs, zone_rows(theirs))], axis=0
+        )
+        cost = product(left[...], right)
+        pieces = [cost[z * B : (z + 1) * B] for z in range(DB)]
+        low = tree([fold(piece, jnp.minimum) for piece in pieces], jnp.minimum)
+        low = jnp.min(low, axis=0, keepdims=True)
+        mass = tree([fold(jnp.exp(low - piece), jnp.add) for piece in pieces], jnp.add)
+        total = jnp.log(jnp.sum(mass, axis=0, keepdims=True)) - low
+        rows[pl.ds(2 * slot, 1), :] = total[:, :B]
+        rows[pl.ds(2 * slot + 1, 1), :] = total[:, B:]
         return carry
 
-    lax.fori_loop(0, RB // 4, pair, 0)
+    lax.fori_loop(0, 4, pair, 0)
+
+
+def rider_near_body(own, other, driver, rows, left):
+    rider_part(own, other, driver, rows, left)
+
+
+def rider_far_body(own, other, driver, near, out, rows, left):
+    rider_part(own, other, driver, rows, left)
+    for r in range(RB):
+        out[0, pl.ds(block_of(r), 1), :] = (rows if r >= 8 else near)[r % 8 : r % 8 + 1]
     for k in range(1, RPEERS):
         out[k] = out[0]
 
@@ -179,17 +186,12 @@
     return tree([sums[k] for k in range(peers)], jnp.add)
 
 
-def block_of(r):
-    c = lax.axis_index("c")
-    other = r % 2
-    return 2 * place(r // 8, r // 2 % 4) + c + other * (1 - 2 * c)
-
-
-def driver_first_body(sums, own_near, own_far, other_near, other_far, driver, out, kernel, peaks, pots, ucol):
-    own = [own_near[k] for k in range(4)] + [own_far[k] for k in range(4)]
-    other = [other_near[k] for k in range(4)] + [other_far[k] for k in range(4)]
+def driver_first_body(sums, own_near, own_far, other_near, other_far, driver, out, kernel, peaks, pots, ucol, left):
+    riders = ((own_near, other_near), (own_far, other_far))
     for r in range(RB):
-        pots[pl.ds(RB + block_of(r), 1), :] = weight_row((other if r % 2 else own)[r // 2])
+        message = riders[r // 8][r % 2][r // 2 % 4]
+        left[r * B : (r + 1) * B] = with_zone(message, zone_rows(message))
+        pots[pl.ds(RB + block_of(r), 1), :] = weight_row(message)
     pots[0:RB] = pots[RB:] - (log_total(sums, RPEERS) - LOG_DRIVERS)
     for r in range(RB):
         ucol[r * B : (r + 1) * B, :] = column(pots[pl.ds(block_of(r), 1), :])
@@ -200,11 +202,11 @@
             [with_zone(one, zone_rows(one)), with_zone(two, zone_rows(two))], axis=0
         )
         lanes = pl.ds(pl.multiple_of(h * 2 * B, 2 * B), 2 * B)
+        cost = product(left[...], right)
         high = jnp.full((8, 2 * B), FLOOR, F32)
         for r in range(RB):
             u = ucol[r * B : (r + 1) * B, :]
-            left = (other if r % 2 else own)[r // 2]
-            score = jnp.concatenate([u, u], axis=1) - product(with_zone(left, zone_rows(left)), right)
+            score = jnp.concatenate([u, u], axis=1) - cost[r * B : (r + 1) * B]
             kernel[r * B : (r + 1) * B, lanes] = score
             high = jnp.maximum(high, fold(score, jnp.maximum))
         top = jnp.max(high, axis=0, keepdims=True)
@@ -225,15 +227,12 @@
 
 
 def row_sums(kernel, weight, out):
-    def block(r, carry):
-        rows = pl.ds(pl.multiple_of(r * B, B), B)
+    for r in range(RB):
+        rows = slice(r * B, (r + 1) * B)
         acc = kernel[rows, 0:B] * weight[0:1]
         for k in range(1, DB):
             acc = acc + kernel[rows, k * B : (k + 1) * B] * weight[k : k + 1]
         out[0, pl.ds(block_of(r), 1), :] = jnp.sum(acc.T, axis=0, keepdims=True)
-        return carry
-
-    lax.fori_loop(0, RB, block, 0)
     for k in range(1, RPEERS):
         out[k] = out[0]
 
@@ -310,17 +309,24 @@
     return lax.ppermute(value, axis, [(k, partner(k)) for k in range(SIZES[AXES.index(axis)])])
 
 
-def gather_riders(message):
+def gather(message, drivers):
     near = jnp.concatenate([message, swap(message, "yl", lambda k: 1 - k)], axis=0)
+    near, drivers = lax.optimization_barrier((near, drivers))
+    drivers = exchange(drivers, ("z",))
     near = jnp.concatenate([near, swap(near, "x", lambda k: k ^ 1)], axis=0)
     far = swap(near, "x", lambda k: 3 - k)
-    return near, far, swap(near, "c", lambda k: 1 - k), swap(far, "c", lambda k: 1 - k)
+    return near, far, swap(near, "c", lambda k: 1 - k), swap(far, "c", lambda k: 1 - k), drivers
+
+
+def matmul_cost(riders, drivers):
+    return pl.CostEstimate(flops=2 * riders * drivers * 2 * B, transcendentals=riders * drivers,
+                           bytes_accessed=4 * riders * drivers)
 
 
 def per_device(rider_emb, driver_emb, log_a, log_b, rider_zone, driver_zone, zone_table):
     rider_msg, driver_msg = call(
         pack_body,
-        [bf16(1, PAY, B), bf16(8, PAY, B)],
+        [pltpu.VMEM((1, PAY, B), BF16), bf16(8, PAY, B)],
         [FAR] * 7,
         [
             pltpu.VMEM((1, B), F32),
@@ -328,27 +334,32 @@
             pltpu.SMEM((2,), jnp.int32),
             pltpu.SMEM((1,), jnp.int32),
             pltpu.SMEM((16, 16), jnp.int32),
-            pltpu.VMEM((2, PAY, B), BF16),
-            pltpu.SemaphoreType.DMA((16,)),
+            pltpu.VMEM((PAY, B), BF16),
+            pltpu.SemaphoreType.DMA((15,)),
         ],
         limit=60,
-        to=FAR,
+        to=[VM, FAR],
     )(
         rider_emb.reshape(2, B, B), driver_emb, log_a.reshape(2, B), log_b.reshape(1, B),
         rider_zone, driver_zone, zone_table,
     )
-    riders = gather_riders(rider_msg)
-    driver = exchange(driver_msg, ("z",))
+    own_near, own_far, other_near, other_far, driver = gather(rider_msg, driver_msg)
+    riders = own_near, own_far, other_near, other_far
+    half = matmul_cost(RB * B // 2, DB * B)
+    left = pltpu.VMEM((DB * B, 2 * B), BF16)
+    (near_rows,) = call(rider_near_body, [f32(8, B)], [VM] * 3, [left], cost=half)(
+        own_near, other_near, driver
+    )
     (message,) = call(
-        rider_first_body, [f32(RPEERS, RB, B)], [VM] * 5, [pltpu.VMEM((DB, 16, B), BF16)]
-    )(*riders, driver)
+        rider_far_body, [f32(RPEERS, RB, B)], [VM] * 4, [pltpu.VMEM((8, B), F32), left], cost=half
+    )(own_far, other_far, driver, near_rows)
     sums = exchange(message, RGROUP)
     columns = pltpu.VMEM((RB * B, B), F32)
     message, kernel, peaks, pots = call(
         driver_first_body,
         [f32(DPEERS, DB, B), f32(RB * B, DB * B), f32(DB, B), f32(2 * RB, B)],
         [VM] * 6,
-        [columns],
+        [columns, pltpu.VMEM((RB * B, 2 * B), BF16)],
     )(sums, *riders, driver)
     sums = exchange(message, DGROUP)
     weights = [pltpu.VMEM((DB, B), F32)]

time: 122 us -> 116 us (0.951)
  Pallas kernels: 17.7 us -> 14.4 us
  blocking collectives: 77.1 us -> 75.4 us
    all_to_all x1, waiting for transfers between devices: 0.01 us -> 1.82 us  [exchange(): return lax.all_to_all(message, axes, 0, 0, tiled=True)]
    all_to_all x6, blocking collectives: 77.1 us -> 75.4 us  [exchange(): return lax.all_to_all(message, axes, 0, 0, tiled=True)]
    pallas_call x1, Pallas kernels: 5.18 us -> 3.91 us  [per_device(): call(driver_first_body, [f32(DPEERS, DB, B), f32(RB * B, DB * B), f32(DB,...]
    pallas_call x1, Pallas kernels: 1.93 us -> 0.68 us  [per_device(): call(rider_second_body, [f32(RPEERS, RB, B), f32(3 * DB, B)], [VM] * 4, w...]
    pallas_call x1, Pallas kernels: 1.9 us -> 0.65 us  [per_device(): call(rider_next_body, [f32(RPEERS, RB, B)], [VM] * 3, weights)]
    pallas_call x2 -> x3, Pallas kernels: 5.63 us -> 6.09 us  [the longest x1 2.14 us: per_device(): call(rider_far_body, [f32(RPEERS, RB, B)], [VM] * 4, [pltpu.VMEM((8, B),...]
  transfers between devices with their start and end apart: 6 -> 6, of which waited for: 4 -> 4; matrix products, arithmetic and copies ran while one was open for 1% -> 0% of each run, Pallas kernels for 0% -> 2%
where the time goes in v4:
time: 116 us; the launch traced here: 115 us
  blocking collectives  75.4 us (65%)
  Pallas kernels  14.4 us (12%)
  starting transfers between devices  12.3 us (11%)
  waiting for transfers between devices  11.7 us (10%)
  between operations  1.34 us (1%)
    all_to_all x6, blocking collectives, exchange(): return lax.all_to_all(message, axes, 0, 0, tiled=True)  75.4 us
    ppermute x5, waiting for transfers between devices, swap(): lax.ppermute(value, axis, [(k, partner(k)) for k in range(SIZES[AXES.inde...  9.85 us
    all_to_all x1, starting transfers between devices, exchange(): return lax.all_to_all(message, axes, 0, 0, tiled=True)  8.48 us
    pallas_call x1, Pallas kernels, per_device(): call(driver_first_body, [f32(DPEERS, DB, B), f32(RB * B, DB * B), f32(DB,...  3.91 us
    ppermute x5, starting transfers between devices, swap(): lax.ppermute(value, axis, [(k, partner(k)) for k in range(SIZES[AXES.inde...  3.78 us
  transfers between devices with their start and end apart: 6, of which 4 were waited for; matrix products, arithmetic and copies ran while one was open for 0% of the time, Pallas kernels for 2%

profile of v4, /device:TPU:2, one launch (start us, length us, event | category | flops | bytes accessed | tf_op | source)
XLA Modules:
  0.0 115.1 jit_solution(10459877361221839949)
XLA Ops:
  1.3 1.8 %shard_map.86 = (bf16[1,144,128]{2,1,0:T(8,128)(2,1)S(1)}, bf16[8,144,128]{2,1,0:T(8,128)(2,1)}) custom-call(bf16[2,128,128]{2,1,0:T(8,128)(2,1)} %bitcast.5, bf16[128,128]{1,0:T(8,128)(2,1)} %driver.1, f32[2,128]{1,0:T(2,128)} %bitcast.6, f32[1,128]{1,0:T(1,128)} %bitcast.7, s32[2]{0:T(128)} %rzone.1, s32[1]{0:T(128)S(6)} %copy.10.dzone, s32[16,16]{1,0:T(8,128)} %table.1), custom_call_target="tpu_custom_call" | custom-call | tf_op jit(solution)/shard_map/pallas_call | solution.py:327
  3.1 1.7 %collective-permute-start = (bf16[1,144,128]{2,1,0:T(8,128)(2,1)S(1)}, bf16[1,144,128]{2,1,0:T(8,128)(2,1)S(1)}, u32[]{:S(2)}, u32[]{:S(2)}) collective-permute-start(bf16[1,144,128]{2,1,0:T(8,128)(2,1)S(1)} %get-tuple-element.14), channel_id=1, source_target_pairs={{0,16},{16,0},{1,17},{17,1},{2,18},{18,2},{3,19},{19,3},{4,20},{20... | collective-permute-start | bytes 110600 | tf_op jit(solution)/shard_map/ppermute | solution.py:309
  4.8 2.4 %collective-permute-done = bf16[1,144,128]{2,1,0:T(8,128)(2,1)S(1)} collective-permute-done((bf16[1,144,128]{2,1,0:T(8,128)(2,1)S(1)}, bf16[1,144,128]{2,1,0:T(8,128)(2,1)S(1)}, u32[]{:S(2)}, u32[]{:S(2)}) %collective-permute-start) | collective-permute-done | bytes 36896 | tf_op jit(solution)/shard_map/ppermute | solution.py:309
  7.2 8.5 %all-to-all-start = ((bf16[8,144,128]{2,1,0:T(8,128)(2,1)}), bf16[8,144,128]{2,1,0:T(8,128)(2,1)S(1)}, u32[]{:S(2)}, u32[]{:S(2)}) async-start(bf16[8,144,128]{2,1,0:T(8,128)(2,1)} %get-tuple-element.17), calls=%async_computation | async-start | bytes 589824 | tf_op jit(solution)/shard_map/all_to_all | solution.py:305
  15.7 0.5 collective-permute-start.1
  16.2 3.8 %collective-permute-done.1 = bf16[2,144,128]{2,1,0:T(8,128)(2,1)S(1)} collective-permute-done((bf16[2,144,128]{2,1,0:T(8,128)(2,1)S(1)}, bf16[2,144,128]{2,1,0:T(8,128)(2,1)S(1)}, u32[]{:S(2)}, u32[]{:S(2)}) %collective-permute-start.1) | collective-permute-done | bytes 73760 | tf_op jit(solution)/shard_map/ppermute | solution.py:309
  20.0 1.6 %collective-permute-start.2 = (bf16[4,144,128]{2,1,0:T(8,128)(2,1)S(1)}, bf16[4,144,128]{2,1,0:T(8,128)(2,1)S(1)}, u32[]{:S(2)}, u32[]{:S(2)}) collective-permute-start(bf16[4,144,128]{2,1,0:T(8,128)(2,1)S(1)} %constant_dynamic-update-slice_fusion.own.own_near), channel_id=1, source_target_pairs={{0,12},{4,8},{8,4},{12,0},{1,13},{5,9},{9,5},{13,1},{2,14},{6,10},... | collective-permute-start | bytes 442376 | tf_op jit(solution)/shard_map/ppermute | solution.py:309
  21.6 0.0 collective-permute-start.4
  21.6 3.6 %collective-permute-done.2.own.own_far = bf16[4,144,128]{2,1,0:T(8,128)(2,1)S(1)} collective-permute-done((bf16[4,144,128]{2,1,0:T(8,128)(2,1)S(1)}, bf16[4,144,128]{2,1,0:T(8,128)(2,1)S(1)}, u32[]{:S(2)}, u32[]{:S(2)}) %collective-permute-start.2) | collective-permute-done | bytes 147488 | tf_op jit(solution)/shard_map/ppermute | solution.py:309
  25.3 0.0 collective-permute-start.3
  25.3 0.0 collective-permute-done.4.other.other_near
  25.3 1.8 %all-to-all-done.driver = bf16[8,144,128]{2,1,0:T(8,128)(2,1)S(1)} async-done(((bf16[8,144,128]{2,1,0:T(8,128)(2,1)}), bf16[8,144,128]{2,1,0:T(8,128)(2,1)S(1)}, u32[]{:S(2)}, u32[]{:S(2)}) %all-to-all-start) | async-done | bytes 294944 | tf_op jit(solution)/shard_map/all_to_all | solution.py:305
  27.1 2.1 %shard_map.87.near = f32[8,128]{1,0:T(8,128)S(1)} custom-call(bf16[4,144,128]{2,1,0:T(8,128)(2,1)S(1)} %constant_dynamic-update-slice_fusion.own.own_near, bf16[4,144,128]{2,1,0:T(8,128)(2,1)S(1)} %collective-permute-done.4.other.other_near, bf16[8,144,128]{2,1,0:T(8,128)(2,1)S(1)} %all-to-all-done.driver), custom_call_target="tpu_custom_call" | custom-call | flops 536870912 | bytes 4194304 | tf_op jit(solution)/shard_map/pallas_call | solution.py:350
  29.2 0.0 collective-permute-done.3.other.other_far
  29.2 2.1 %shard_map.88 = f32[32,16,128]{2,1,0:T(8,128)S(1)} custom-call(bf16[4,144,128]{2,1,0:T(8,128)(2,1)S(1)} %collective-permute-done.2.own.own_far, bf16[4,144,128]{2,1,0:T(8,128)(2,1)S(1)} %collective-permute-done.3.other.other_far, bf16[8,144,128]{2,1,0:T(8,128)(2,1)S(1)} %all-to-all-done.driver, f32[8,128]{1,0:T(8,128)S(1)} %shard_map.87.near), custom_call_target="tpu_custom_call" | custom-call | flops 536870912 | bytes 4194304 | tf_op jit(solution)/shard_map/pallas_call | solution.py:353
  31.4 15.3 %all_to_all.35.sums = f32[32,16,128]{2,1,0:T(8,128)S(1)} all-to-all(f32[32,16,128]{2,1,0:T(8,128)S(1)} %shard_map.88), channel_id=1, replica_groups=mesh['z'=8,'yl'=2,'x'=4,'yh'=2,'c'=2] {'yl','x','yh','c'}, dimensions={0} | all-to-all | bytes 524288 | tf_op jit(solution)/shard_map/all_to_all | solution.py:305
  46.7 3.9 %shard_map.89 = (f32[8,8,128]{2,1,0:T(8,128)S(1)}, f32[2048,1024]{1,0:T(8,128)S(1)}, f32[8,128]{1,0:T(8,128)S(1)}, f32[32,128]{1,0:T(8,128)S(1)}) custom-call(f32[32,16,128]{2,1,0:T(8,128)S(1)} %all_to_all.35.sums, bf16[4,144,128]{2,1,0:T(8,128)(2,1)S(1)} %constant_dynamic-update-slice_fusion.own.own_near, ...), custom_call_target="tpu_custom_call" | custom-call | tf_op jit(solution)/shard_map/pallas_call | solution.py:358
  50.6 14.3 %all_to_all.36.sums = f32[8,8,128]{2,1,0:T(8,128)S(1)} all-to-all(f32[8,8,128]{2,1,0:T(8,128)S(1)} %get-tuple-element.18), channel_id=1, replica_groups=mesh['z'=8,'yl'=2,'x'=4,'yh'=2,'c'=2] {'z'}, dimensions={0} | all-to-all | bytes 65536 | tf_op jit(solution)/shard_map/all_to_all | solution.py:305
  64.9 0.7 shard_map.90
  65.6 12.5 %all_to_all.37.sums = f32[32,16,128]{2,1,0:T(8,128)S(1)} all-to-all(f32[32,16,128]{2,1,0:T(8,128)S(1)} %get-tuple-element.21), channel_id=1, replica_groups=mesh['z'=8,'yl'=2,'x'=4,'yh'=2,'c'=2] {'yl','x','yh','c'}, dimensions={0} | all-to-all | bytes 524288 | tf_op jit(solution)/shard_map/all_to_all | solution.py:305
  78.1 1.0 shard_map.91
  79.1 10.4 %all_to_all.38.sums = f32[8,8,128]{2,1,0:T(8,128)S(1)} all-to-all(f32[8,8,128]{2,1,0:T(8,128)S(1)} %shard_map.91), channel_id=1, replica_groups=mesh['z'=8,'yl'=2,'x'=4,'yh'=2,'c'=2] {'z'}, dimensions={0} | all-to-all | bytes 65536 | tf_op jit(solution)/shard_map/all_to_all | solution.py:305
  89.5 0.7 shard_map.92
  90.1 12.5 %all_to_all.39.sums = f32[32,16,128]{2,1,0:T(8,128)S(1)} all-to-all(f32[32,16,128]{2,1,0:T(8,128)S(1)} %shard_map.92), channel_id=1, replica_groups=mesh['z'=8,'yl'=2,'x'=4,'yh'=2,'c'=2] {'yl','x','yh','c'}, dimensions={0} | all-to-all | bytes 524288 | tf_op jit(solution)/shard_map/all_to_all | solution.py:305
  102.6 1.5 %shard_map.93 = (f32[8,8,128]{2,1,0:T(8,128)S(1)}, f32[2,128]{1,0:T(2,128)}) custom-call(f32[32,16,128]{2,1,0:T(8,128)S(1)} %all_to_all.39.sums, f32[32,128]{1,0:T(8,128)S(1)} %get-tuple-element.22.pots, f32[24,128]{1,0:T(8,128)S(1)} %get-tuple-element.23.state, f32[2048,1024]{1,0:T(8,128)S(1)} %get-tuple-element.20.kernel), custom_call_target="tpu_custom_call" | custom-call | tf_op jit(solution)/shard_map/pallas_call | solution.py:380
  104.2 10.4 %all_to_all.40.sums = f32[8,8,128]{2,1,0:T(8,128)S(1)} all-to-all(f32[8,8,128]{2,1,0:T(8,128)S(1)} %get-tuple-element.25), channel_id=1, replica_groups=mesh['z'=8,'yl'=2,'x'=4,'yh'=2,'c'=2] {'z'}, dimensions={0} | all-to-all | bytes 65536 | tf_op jit(solution)/shard_map/all_to_all | solution.py:305
  114.6 0.5 shard_map.94
  (3 shorter events, 0.0 us)
Async XLA Ops:
  3.1 4.0 %collective-permute-start = (bf16[1,144,128]{2,1,0:T(8,128)(2,1)S(1)}, bf16[1,144,128]{2,1,0:T(8,128)(2,1)S(1)}, u32[]{:S(2)}, u32[]{:S(2)}) collective-permute-start(bf16[1,144,128]{2,1,0:T(8,128)(2,1)S(1)} %get-tuple-element.14), channel_id=1, source_target_pairs={{0,16},{16,0},{1,17},{17,1},{2,18},{18,2},{3,19},{19,3},{4,20},{20... | collective-permute-start | bytes 110600 | tf_op jit(solution)/shard_map/ppermute | solution.py:309
  7.2 19.9 %all-to-all-start = ((bf16[8,144,128]{2,1,0:T(8,128)(2,1)}), bf16[8,144,128]{2,1,0:T(8,128)(2,1)S(1)}, u32[]{:S(2)}, u32[]{:S(2)}) async-start(bf16[8,144,128]{2,1,0:T(8,128)(2,1)} %get-tuple-element.17), calls=%async_computation | async-start | bytes 589824 | tf_op jit(solution)/shard_map/all_to_all | solution.py:305
  15.7 4.4 %collective-permute-start.1 = (bf16[2,144,128]{2,1,0:T(8,128)(2,1)S(1)}, bf16[2,144,128]{2,1,0:T(8,128)(2,1)S(1)}, u32[]{:S(2)}, u32[]{:S(2)}) collective-permute-start(bf16[2,144,128]{2,1,0:T(8,128)(2,1)S(1)} %pad_maximum_fusion), channel_id=1, source_target_pairs={{0,4},{4,0},{8,12},{12,8},{1,5},{5,1},{9,13},{13,9},{2,6},{6,2},{1... | collective-permute-start | bytes 221192 | tf_op jit(solution)/shard_map/ppermute | solution.py:309
  20.0 5.2 %collective-permute-start.2 = (bf16[4,144,128]{2,1,0:T(8,128)(2,1)S(1)}, bf16[4,144,128]{2,1,0:T(8,128)(2,1)S(1)}, u32[]{:S(2)}, u32[]{:S(2)}) collective-permute-start(bf16[4,144,128]{2,1,0:T(8,128)(2,1)S(1)} %constant_dynamic-update-slice_fusion.own.own_near), channel_id=1, source_target_pairs={{0,12},{4,8},{8,4},{12,0},{1,13},{5,9},{9,5},{13,1},{2,14},{6,10},... | collective-permute-start | bytes 442376 | tf_op jit(solution)/shard_map/ppermute | solution.py:309
  21.6 3.7 %collective-permute-start.4 = (bf16[4,144,128]{2,1,0:T(8,128)(2,1)S(1)}, bf16[4,144,128]{2,1,0:T(8,128)(2,1)S(1)}, u32[]{:S(2)}, u32[]{:S(2)}) collective-permute-start(bf16[4,144,128]{2,1,0:T(8,128)(2,1)S(1)} %constant_dynamic-update-slice_fusion.own.own_near), channel_id=1, source_target_pairs={{0,1},{1,0},{2,3},{3,2},{4,5},{5,4},{6,7},{7,6},{8,9},{9,8},{10,11... | collective-permute-start | bytes 442376 | tf_op jit(solution)/shard_map/ppermute | solution.py:309
  25.3 3.9 %collective-permute-start.3 = (bf16[4,144,128]{2,1,0:T(8,128)(2,1)S(1)}, bf16[4,144,128]{2,1,0:T(8,128)(2,1)S(1)}, u32[]{:S(2)}, u32[]{:S(2)}) collective-permute-start(bf16[4,144,128]{2,1,0:T(8,128)(2,1)S(1)} %collective-permute-done.2.own.own_far), channel_id=1, source_target_pairs={{0,1},{1,0},{2,3},{3,2},{4,5},{5,4},{6,7},{7,6},{8,9},{9,8},{10,11... | collective-permute-start | bytes 442376 | tf_op jit(solution)/shard_map/ppermute | solution.py:309

commit v5 on v4

v5 whole, which is shorter than its diff:
```python
import math

import jax
import jax.numpy as jnp
from jax import lax
from jax.experimental import pallas as pl
from jax.experimental.pallas import tpu as pltpu
from jax.sharding import Mesh, PartitionSpec as P

AXES = ("z", "yl", "x", "yh", "c")
SIZES = (8, 2, 4, 2, 2)

B = 128
RB = 16
DB = 8
PAY = B + 16
ITERS = 3
LOG_DRIVERS = math.log(32768)
LOG_RIDERS = math.log(16384)
PENALTY = 1e30
FLOOR = -1e29
TINY = 1e-37

F32 = jnp.float32
BF16 = jnp.bfloat16
VM = pl.BlockSpec(memory_space=pltpu.VMEM)
FAR = pl.BlockSpec(memory_space=pltpu.HBM)


def call(body, outs, ins, scratch=(), limit=40, cost=None):
    return pl.pallas_call(
        body,
        out_shape=outs,
        in_specs=ins,
        out_specs=[VM] * len(outs),
        cost_estimate=cost,
        scratch_shapes=list(scratch),
        compiler_params=pltpu.CompilerParams(vmem_limit_bytes=limit * 2**20),
    )


def f32(*shape):
    return jax.ShapeDtypeStruct(shape, F32)


def bf16(*shape):
    return jax.ShapeDtypeStruct(shape, BF16)


def product(left, right):
    return lax.dot_general(left, right, (((1,), (1,)), ((), ())), preferred_element_type=F32)


def tree(parts, op):
    while len(parts) > 1:
        parts = [op(parts[2 * k], parts[2 * k + 1]) for k in range(len(parts) // 2)]
    return parts[0]


def fold(block, op):
    return tree([block[8 * k : 8 * k + 8] for k in range(B // 8)], op)


def column(row):
    return jnp.broadcast_to(row, (B, B)).T


def three_parts(value):
    high = value.astype(BF16)
    rest = value - high.astype(F32)
    middle = rest.astype(BF16)
    return high, middle, (rest - middle.astype(F32)).astype(BF16)


def zone_rows(message):
    return jnp.broadcast_to(message[B : B + 1].astype(F32), (16, B)).astype(BF16)


def weight_row(message):
    tail = message[B:].astype(F32)
    return (tail[1:2] + tail[2:3]) + tail[3:4]


def with_zone(message, zone):
    return jnp.concatenate([message[:B], jnp.concatenate([zone] * (B // 16), axis=0)], axis=1)


def tail_rows(zone_row, log_row):
    row = lax.broadcasted_iota(jnp.int32, (16, B), 0)
    tail = jnp.where(row == 0, zone_row, 0.0)
    for k, part in enumerate(three_parts(log_row)):
        tail = jnp.where(row == k + 1, part.astype(F32), tail)
    return tail.astype(BF16)


def pack_body(rider, driver, log_a, log_b, rzone, dzone, table, rider_out, driver_out,
              a_row, b_row, rz, dz, tab, sems):
    c = lax.axis_index("c")
    copies = [
        pltpu.make_async_copy(rider.at[c], rider_out.at[0, pl.ds(0, B)], sems.at[0]),
        pltpu.make_async_copy(driver, driver_out.at[0, pl.ds(0, B)], sems.at[1]),
        pltpu.make_async_copy(log_a.at[pl.ds(c, 1)], a_row, sems.at[2]),
        pltpu.make_async_copy(log_b, b_row, sems.at[3]),
        pltpu.make_async_copy(rzone, rz, sems.at[4]),
        pltpu.make_async_copy(dzone, dz, sems.at[5]),
        pltpu.make_async_copy(table, tab, sems.at[6]),
    ]
    for copy in copies:
        copy.start()
    for copy in copies:
        copy.wait()
    lane = lax.broadcasted_iota(jnp.int32, (16, B), 1)
    hot = jnp.where(lane == rz[c], 1.0, 0.0)
    zone = dz[0]
    shut = jnp.zeros((16, B), F32)
    for k in range(16):
        shut = jnp.where((lane == k) & (tab[k, zone] != 1), PENALTY, shut)
    rider_out[0, B:, :] = tail_rows(hot, a_row[...])
    driver_out[0, B:, :] = tail_rows(shut, b_row[...])


def place(far, slot):
    yl, x = lax.axis_index("yl"), lax.axis_index("x")
    first, second = slot % 2, slot // 2
    x = x + far * (3 - 2 * x)
    x = x + second * (1 - 2 * (x % 2))
    return (yl + first * (1 - 2 * yl)) * 4 + x


def block_of(r):
    c = lax.axis_index("c")
    other = r % 2
    return 2 * place(r // 8, r // 2 % 4) + c + other * (1 - 2 * c)


def ring(j):
    return (lax.axis_index("z") + j) % DB


def widen(messages, wide):
    for k, message in enumerate(messages):
        wide[k * B : (k + 1) * B] = with_zone(message, zone_rows(message))


def rider_part(own, other, drivers, rows, left):
    widen([driver[0] for driver in drivers], left)

    def pair(slot, carry):
        mine, theirs = own[slot], other[slot]
        right = jnp.concatenate(
            [with_zone(mine, zone_rows(mine)), with_zone(theirs, zone_rows(theirs))], axis=0
        )
        cost = product(left[...], right)
        pieces = [cost[z * B : (z + 1) * B] for z in range(DB)]
        low = tree([fold(piece, jnp.minimum) for piece in pieces], jnp.minimum)
        low = jnp.min(low, axis=0, keepdims=True)
        mass = tree([fold(jnp.exp(low - piece), jnp.add) for piece in pieces], jnp.add)
        total = jnp.log(jnp.sum(mass, axis=0, keepdims=True)) - low
        rows[pl.ds(2 * slot, 1), :] = total[:, :B]
        rows[pl.ds(2 * slot + 1, 1), :] = total[:, B:]
        return carry

    lax.fori_loop(0, 4, pair, 0)


def rider_near_body(own, other, *rest):
    *drivers, rows, left = rest
    rider_part(own, other, drivers, rows, left)


def rider_far_body(own, other, near, *rest):
    *drivers, out, rows, left = rest
    rider_part(own, other, drivers, rows, left)
    for r in range(RB):
        out[pl.ds(block_of(r), 1), :] = (rows if r >= 8 else near)[r % 8 : r % 8 + 1]


def log_total(sums):
    parts = [sums[k] for k in range(DB)]
    peak = tree(parts, jnp.maximum)
    return peak + jnp.log(tree([jnp.exp(part - peak) for part in parts], jnp.add))


def total_of(sums):
    return tree([sums[k] for k in range(DB)], jnp.add)


def driver_first_body(sums, own_near, own_far, other_near, other_far, *rest):
    *drivers, out, kernel, peaks, pots, ucol, left, right = rest
    riders = ((own_near, other_near), (own_far, other_far))
    messages = [riders[r // 8][r % 2][r // 2 % 4] for r in range(RB)]
    widen(messages, left)
    widen([driver[0] for driver in drivers], right)
    for r in range(RB):
        pots[pl.ds(RB + block_of(r), 1), :] = weight_row(messages[r])
    for j in range(DB):
        peaks[pl.ds(DB + ring(j), 1), :] = weight_row(drivers[j][0])
    pots[0:RB] = pots[RB:] - (sums[...] - LOG_DRIVERS)
    for r in range(RB):
        ucol[r * B : (r + 1) * B, :] = column(pots[pl.ds(block_of(r), 1), :])

    def pair(h, carry):
        lanes = pl.ds(pl.multiple_of(h * 2 * B, 2 * B), 2 * B)
        cost = product(left[...], right[lanes, :])
        high = jnp.full((8, 2 * B), FLOOR, F32)
        for r in range(RB):
            u = ucol[r * B : (r + 1) * B, :]
            score = jnp.concatenate([u, u], axis=1) - cost[r * B : (r + 1) * B]
            kernel[r * B : (r + 1) * B, lanes] = score
            high = jnp.maximum(high, fold(score, jnp.maximum))
        top = jnp.max(high, axis=0, keepdims=True)
        total = jnp.zeros((8, 2 * B), F32)
        for r in range(RB):
            term = jnp.exp(kernel[r * B : (r + 1) * B, lanes] - top)
            kernel[r * B : (r + 1) * B, lanes] = term
            total = total + fold(term, jnp.add)
        total = top + jnp.log(jnp.maximum(jnp.sum(total, axis=0, keepdims=True), TINY))
        for k in range(2):
            peaks[pl.ds(ring(2 * h + k), 1), :] = top[:, k * B : (k + 1) * B]
            out[0, pl.ds(ring(2 * h + k), 1), :] = total[:, k * B : (k + 1) * B]
        return carry

    lax.fori_loop(0, DB // 2, pair, 0)
    for k in range(1, DB):
        out[k] = out[0]


def row_sums(kernel, scale, out):
    weight = [scale[pl.ds(ring(j), 1), :] for j in range(DB)]
    for r in range(RB):
        rows = slice(r * B, (r + 1) * B)
        acc = kernel[rows, 0:B] * weight[0]
        for k in range(1, DB):
            acc = acc + kernel[rows, k * B : (k + 1) * B] * weight[k]
        out[pl.ds(block_of(r), 1), :] = jnp.sum(acc.T, axis=0, keepdims=True)


def column_sums(kernel, f, state, fcol, hold):
    hold[...] = f
    for r in range(RB):
        fcol[r * B : (r + 1) * B, :] = column(hold[pl.ds(block_of(r), 1), :])

    def block(r, acc):
        for k in range(B // 8):
            rows = pl.ds(pl.multiple_of(r * B + 8 * k, 8), 8)
            f = fcol[rows, :]
            acc = tuple(a + kernel[rows, j * B : (j + 1) * B] * f for j, a in enumerate(acc))
        return acc

    acc = lax.fori_loop(0, RB, block, tuple(jnp.zeros((8, B), F32) for _ in range(DB)))
    for j in range(DB):
        hold[pl.ds(ring(j), 1), :] = jnp.sum(acc[j], axis=0, keepdims=True)
    return hold[0:DB] * state[2 * DB : 3 * DB]


def rider_second_body(sums, peaks, kernel, out, state):
    log_b = peaks[DB:]
    pot = log_b - (log_total(sums) - LOG_RIDERS)
    state[0:DB] = pot
    state[DB : 2 * DB] = log_b
    state[2 * DB :] = jnp.exp(pot + peaks[0:DB])
    row_sums(kernel, state.at[pl.ds(2 * DB, DB)], out)


def driver_next_body(sums, pots, state, kernel, out, fcol, hold):
    rows = column_sums(kernel, jnp.exp(pots[RB:] + LOG_DRIVERS) / sums[...], state, fcol, hold)
    for k in range(DB):
        out[k] = rows


def rider_next_body(sums, state, kernel, out, scale):
    scale[...] = state[2 * DB :] * (jnp.exp(state[DB : 2 * DB] + LOG_RIDERS) / total_of(sums))
    row_sums(kernel, scale, out)


def driver_last_body(sums, pots, state, kernel, out, rider_pot, fcol, hold):
    log_a = pots[RB:]
    hold[...] = pots[0:RB] + (log_a + LOG_DRIVERS - jnp.log(sums[...]))
    block = lax.axis_index("yl") * 4 + lax.axis_index("x")
    rider_pot[0:1] = hold[pl.ds(2 * block, 1), :]
    rider_pot[1:2] = hold[pl.ds(2 * block + 1, 1), :]
    rows = column_sums(kernel, jnp.exp(log_a + LOG_DRIVERS) / sums[...], state, fcol, hold)
    for k in range(DB):
        out[k] = jnp.broadcast_to(rows[k : k + 1], (8, B))


def finish_body(sums, state, driver_pot):
    z = lax.axis_index("z")
    pot = state[pl.ds(z, 1), :]
    log_b = state[pl.ds(DB + z, 1), :]
    driver_pot[...] = pot + (log_b + LOG_RIDERS - jnp.log(total_of(sums)[0:1]))


def exchange(message):
    return lax.all_to_all(message, "z", 0, 0, tiled=True)


def swap(value, axes, partner):
    count = math.prod(SIZES[AXES.index(axis)] for axis in axes)
    return lax.ppermute(value, axes, [(k, partner(k)) for k in range(count)])


def gather(rider, driver):
    held = {0: driver, DB: driver}
    near, far, other = rider, None, None
    for k in range(1, DB // 2 + 1):
        held[k] = swap(held[k - 1], ("z",), lambda i: (i - 1) % DB)
        if k < DB // 2:
            held[DB - k] = swap(held[DB - k + 1], ("z",), lambda i: (i + 1) % DB)
        if k == 1:
            near = jnp.concatenate([near, swap(near, ("yl",), lambda i: 1 - i)], axis=0)
        elif k == 2:
            near = jnp.concatenate([near, swap(near, ("x",), lambda i: i ^ 1)], axis=0)
        elif k == 3:
            far = swap(near, ("x",), lambda i: 3 - i)
            other = swap(near, ("c",), lambda i: 1 - i)
        if k < 3:
            near, held[k], held[DB - k] = lax.optimization_barrier((near, held[k], held[DB - k]))
        elif k == 3:
            far, held[k], held[DB - k] = lax.optimization_barrier((far, held[k], held[DB - k]))
    return (near, far, other, swap(far, ("c",), lambda i: 1 - i)), [held[k] for k in range(DB)]


def log_add(a, b):
    peak = jnp.maximum(a, b)
    return peak + jnp.log(jnp.exp(a - peak) + jnp.exp(b - peak))


def close(value, op):
    for axes, partner in (
        (("c",), lambda k: 1 - k),
        (("x",), lambda k: k ^ 1),
        (("x",), lambda k: 3 - k),
        (("yl",), lambda k: 1 - k),
        (("yl", "yh"), lambda k: 3 - k),
    ):
        value = op(value, swap(value, axes, partner))
    return value


def matmul_cost(riders, drivers):
    return pl.CostEstimate(flops=2 * riders * drivers * 2 * B, transcendentals=riders * drivers,
                           bytes_accessed=4 * riders * drivers)


def per_device(rider_emb, driver_emb, log_a, log_b, rider_zone, driver_zone, zone_table):
    message = pltpu.VMEM((1, PAY, B), BF16)
    rider_msg, driver_msg = call(
        pack_body,
        [message, message],
        [FAR] * 7,
        [
            pltpu.VMEM((1, B), F32),
            pltpu.VMEM((1, B), F32),
            pltpu.SMEM((2,), jnp.int32),
            pltpu.SMEM((1,), jnp.int32),
            pltpu.SMEM((16, 16), jnp.int32),
            pltpu.SemaphoreType.DMA((7,)),
        ],
        limit=60,
    )(
        rider_emb.reshape(2, B, B), driver_emb, log_a.reshape(2, B), log_b.reshape(1, B),
        rider_zone, driver_zone, zone_table,
    )
    riders, drivers = gather(rider_msg, driver_msg)
    own_near, own_far, other_near, other_far = riders
    half = matmul_cost(RB * B // 2, DB * B)
    left = pltpu.VMEM((DB * B, 2 * B), BF16)
    (near,) = call(rider_near_body, [f32(8, B)], [VM] * 10, [left], cost=half)(
        own_near, other_near, *drivers
    )
    (sums,) = call(
        rider_far_body, [f32(RB, B)], [VM] * 11, [pltpu.VMEM((8, B), F32), left], cost=half
    )(own_far, other_far, near, *drivers)
    sums = close(sums, log_add)
    columns = pltpu.VMEM((RB * B, B), F32)
    sums, kernel, peaks, pots = call(
        driver_first_body,
        [f32(DB, DB, B), f32(RB * B, DB * B), f32(2 * DB, B), f32(2 * RB, B)],
        [VM] * 13,
        [columns, pltpu.VMEM((RB * B, 2 * B), BF16), left],
    )(sums, *riders, *drivers)
    sums = exchange(sums)
    columns = [columns, pltpu.VMEM((RB, B), F32)]
    sums, state = call(rider_second_body, [f32(RB, B), f32(3 * DB, B)], [VM] * 3)(
        sums, peaks, kernel
    )
    sums = close(sums, jnp.add)
    for _ in range(ITERS - 2):
        (sums,) = call(driver_next_body, [f32(DB, DB, B)], [VM] * 4, columns)(
            sums, pots, state, kernel
        )
        sums = exchange(sums)
        (sums,) = call(rider_next_body, [f32(RB, B)], [VM] * 3, [pltpu.VMEM((DB, B), F32)])(
            sums, state, kernel
        )
        sums = close(sums, jnp.add)
    sums, rider_pot = call(driver_last_body, [f32(DB, 8, B), f32(2, B)], [VM] * 4, columns)(
        sums, pots, state, kernel
    )
    sums = exchange(sums)
    (driver_pot,) = call(finish_body, [f32(1, B)], [VM] * 2)(sums, state)
    return rider_pot.reshape(2 * B), driver_pot.reshape(B)


def solution(mesh):
    fine = Mesh(mesh.devices.reshape(SIZES), AXES)
    row, every = ("z", "yl", "x"), AXES
    placed = (
        P(row, None),
        P(every, None),
        P(row),
        P(every),
        P(row),
        P(every),
        P(),
    )
    return jax.shard_map(
        per_device,
        mesh=fine,
        in_specs=placed,
        out_specs=(P(row), P(every)),
        check_vma=False,
    )
```

time: 116 us -> 135 us (1.16); the launches traced: 115 us -> 133 us
  blocking collectives: 75.4 us -> 34.4 us
  waiting for transfers between devices: 11.7 us -> 51.1 us
  starting transfers between devices: 12.3 us -> 32.1 us
    ppermute x5 -> x27, waiting for transfers between devices: 9.85 us -> 51.1 us  [swap(): return lax.ppermute(value, axes, [(k, partner(k)) for k in range(count)])]
    all_to_all x6 -> x3, blocking collectives: 75.4 us -> 34.4 us  [exchange(): return lax.all_to_all(message, 'z', 0, 0, tiled=True)]
    ppermute x5 -> x27, starting transfers between devices: 3.78 us -> 32.1 us  [swap(): return lax.ppermute(value, axes, [(k, partner(k)) for k in range(count)])]
    all_to_all x1 -> x0, starting transfers between devices: 8.48 us -> none  [exchange(): return lax.all_to_all(message, axes, 0, 0, tiled=True)]
    all_to_all x1 -> x0, waiting for transfers between devices: 1.82 us -> none  [exchange(): return lax.all_to_all(message, axes, 0, 0, tiled=True)]
  transfers between devices with their start and end apart: 6 -> 27, of which waited for: 4 -> 22; matrix products, arithmetic and copies ran while one was open for 0% -> 0% of each run, Pallas kernels for 2% -> 2%
where the time goes in v5:
time: 135 us; the launch traced here: 133 us
  waiting for transfers between devices  51.1 us (38%)
  blocking collectives  34.4 us (25%)
  starting transfers between devices  32.1 us (24%)
  Pallas kernels  13.6 us (10%)
  between operations  1.39 us (1%)
    ppermute x27, waiting for transfers between devices, swap(): return lax.ppermute(value, axes, [(k, partner(k)) for k in range(count)])  51.1 us
    all_to_all x3, blocking collectives, exchange(): return lax.all_to_all(message, 'z', 0, 0, tiled=True)  34.4 us
    ppermute x27, starting transfers between devices, swap(): return lax.ppermute(value, axes, [(k, partner(k)) for k in range(count)])  32.1 us
    pallas_call x1, Pallas kernels, per_device(): call(driver_first_body, [f32(DB, DB, B), f32(RB * B, DB * B), f32(2 * DB,...  3.86 us
  transfers between devices with their start and end apart: 27, of which 22 were waited for; matrix products, arithmetic and copies ran while one was open for 0% of the time, Pallas kernels for 2%

profile of v5, /device:TPU:2, one launch (start us, length us, event | category | flops | bytes accessed | tf_op | source)
XLA Modules:
  0.0 132.7 jit_solution(807609600300154041)
XLA Ops:
  2.3 1.7 %collective-permute-start = (bf16[1,144,128]{2,1,0:T(8,128)(2,1)S(1)}, bf16[1,144,128]{2,1,0:T(8,128)(2,1)S(1)}, u32[]{:S(2)}, u32[]{:S(2)}) collective-permute-start(bf16[1,144,128]{2,1,0:T(8,128)(2,1)S(1)} %get-tuple-element.21), channel_id=1, source_target_pairs={{0,16},{16,0},{1,17},{17,1},{2,18},{18,2},{3,19},{19,3},{4,20},{20... | collective-permute-start | bytes 110600 | tf_op jit(solution)/shard_map/ppermute | solution.py:300
  4.0 1.9 %collective-permute-start.2 = (bf16[1,144,128]{2,1,0:T(8,128)(2,1)S(1)}, bf16[1,144,128]{2,1,0:T(8,128)(2,1)S(1)}, u32[]{:S(2)}, u32[]{:S(2)}) collective-permute-start(bf16[1,144,128]{2,1,0:T(8,128)(2,1)S(1)} %get-tuple-element.22.rest_0_), channel_id=1, source_target_pairs={{0,32},{32,64},{64,96},{96,128},{128,160},{160,192},{192,224},{224... | collective-permute-start | bytes 110600 | tf_op jit(solution)/shard_map/ppermute | solution.py:300
  5.9 3.9 %collective-permute-start.1 = (bf16[1,144,128]{2,1,0:T(8,128)(2,1)S(1)}, bf16[1,144,128]{2,1,0:T(8,128)(2,1)S(1)}, u32[]{:S(2)}, u32[]{:S(2)}) collective-permute-start(bf16[1,144,128]{2,1,0:T(8,128)(2,1)S(1)} %get-tuple-element.22.rest_0_), channel_id=1, source_target_pairs={{0,224},{32,0},{64,32},{96,64},{128,96},{160,128},{192,160},{224,1... | collective-permute-start | bytes 110600 | tf_op jit(solution)/shard_map/ppermute | solution.py:300
  9.9 1.9 %collective-permute-done.2.rest_7_ = bf16[1,144,128]{2,1,0:T(8,128)(2,1)S(1)} collective-permute-done((bf16[1,144,128]{2,1,0:T(8,128)(2,1)S(1)}, bf16[1,144,128]{2,1,0:T(8,128)(2,1)S(1)}, u32[]{:S(2)}, u32[]{:S(2)}) %collective-permute-start.2) | collective-permute-done | bytes 36896 | tf_op jit(solution)/shard_map/ppermute | solution.py:300
  12.3 3.2 %collective-permute-start.4 = (bf16[1,144,128]{2,1,0:T(8,128)(2,1)S(1)}, bf16[1,144,128]{2,1,0:T(8,128)(2,1)S(1)}, u32[]{:S(2)}, u32[]{:S(2)}) collective-permute-start(bf16[1,144,128]{2,1,0:T(8,128)(2,1)S(1)} %collective-permute-done.1.rest_1_), channel_id=1, source_target_pairs={{0,224},{32,0},{64,32},{96,64},{128,96},{160,128},{192,160},{224,1... | collective-permute-start | bytes 110600 | tf_op jit(solution)/shard_map/ppermute | solution.py:300
  17.2 3.5 %collective-permute-done.5.rest_6_ = bf16[1,144,128]{2,1,0:T(8,128)(2,1)S(1)} collective-permute-done((bf16[1,144,128]{2,1,0:T(8,128)(2,1)S(1)}, bf16[1,144,128]{2,1,0:T(8,128)(2,1)S(1)}, u32[]{:S(2)}, u32[]{:S(2)}) %collective-permute-start.5) | collective-permute-done | bytes 36896 | tf_op jit(solution)/shard_map/ppermute | solution.py:300
  20.7 2.2 %collective-permute-start.6 = (bf16[4,144,128]{2,1,0:T(8,128)(2,1)S(1)}, bf16[4,144,128]{2,1,0:T(8,128)(2,1)S(1)}, u32[]{:S(2)}, u32[]{:S(2)}) collective-permute-start(bf16[4,144,128]{2,1,0:T(8,128)(2,1)S(1)} %pad_maximum_fusion.own.own_near), channel_id=1, source_target_pairs={{0,12},{4,8},{8,4},{12,0},{1,13},{5,9},{9,5},{13,1},{2,14},{6,10},... | collective-permute-start | bytes 442376 | tf_op jit(solution)/shard_map/ppermute | solution.py:300
  22.9 2.0 %collective-permute-start.8 = (bf16[1,144,128]{2,1,0:T(8,128)(2,1)S(1)}, bf16[1,144,128]{2,1,0:T(8,128)(2,1)S(1)}, u32[]{:S(2)}, u32[]{:S(2)}) collective-permute-start(bf16[1,144,128]{2,1,0:T(8,128)(2,1)S(1)} %collective-permute-done.5.rest_6_), channel_id=1, source_target_pairs={{0,32},{32,64},{64,96},{96,128},{128,160},{160,192},{192,224},{224... | collective-permute-start | bytes 110600 | tf_op jit(solution)/shard_map/ppermute | solution.py:300
  24.9 1.9 %collective-permute-done.7.rest_3_ = bf16[1,144,128]{2,1,0:T(8,128)(2,1)S(1)} collective-permute-done((bf16[1,144,128]{2,1,0:T(8,128)(2,1)S(1)}, bf16[1,144,128]{2,1,0:T(8,128)(2,1)S(1)}, u32[]{:S(2)}, u32[]{:S(2)}) %collective-permute-start.7) | collective-permute-done | bytes 36896 | tf_op jit(solution)/shard_map/ppermute | solution.py:300
  28.4 3.7 %collective-permute-done.11.rest_4_ = bf16[1,144,128]{2,1,0:T(8,128)(2,1)S(1)} collective-permute-done((bf16[1,144,128]{2,1,0:T(8,128)(2,1)S(1)}, bf16[1,144,128]{2,1,0:T(8,128)(2,1)S(1)}, u32[]{:S(2)}, u32[]{:S(2)}) %collective-permute-start.11) | collective-permute-done | bytes 36896 | tf_op jit(solution)/shard_map/ppermute | solution.py:300
  32.0 2.1 %shard_map.87.near = f32[8,128]{1,0:T(8,128)S(1)} custom-call(bf16[4,144,128]{2,1,0:T(8,128)(2,1)S(1)} %pad_maximum_fusion.own.own_near, bf16[4,144,128]{2,1,0:T(8,128)(2,1)S(1)} %collective-permute-done.10.other.other_near, bf16[1,144,128]{2,1,0:T(8,128)(2,1)S(1)} %get-tuple-element.22.rest_0_, bf16[1,144,128]{2,1,0:T(8,128)(2,1)S(1)} %collective-permute-done.1.rest_1_, ...), custom_call_target="tpu_custom_call" | custom-call | flops 536870912 | bytes 4194304 | tf_op jit(solution)/shard_map/pallas_call | solution.py:369
  34.2 2.1 %shard_map.88 = f32[16,128]{1,0:T(8,128)S(1)} custom-call(bf16[4,144,128]{2,1,0:T(8,128)(2,1)S(1)} %collective-permute-done.6.own.own_far, bf16[4,144,128]{2,1,0:T(8,128)(2,1)S(1)} %collective-permute-done.9.other.other_far, f32[8,128]{1,0:T(8,128)S(1)} %shard_map.87.near, bf16[1,144,128]{2,1,0:T(8,128)(2,1)S(1)} %get-tuple-element.22.rest_0_, ...), custom_call_target="tpu_custom_call" | custom-call | flops 536870912 | bytes 4194304 | tf_op jit(solution)/shard_map/pallas_call | solution.py:372
  39.1 2.3 %collective-permute-done.13 = f32[16,128]{1,0:T(8,128)S(1)} collective-permute-done((f32[16,128]{1,0:T(8,128)S(1)}, f32[16,128]{1,0:T(8,128)S(1)}, u32[]{:S(2)}, u32[]{:S(2)}) %collective-permute-start.13) | collective-permute-done | bytes 8224 | tf_op jit(solution)/shard_map/ppermute | solution.py:300
  41.5 3.6 %collective-permute-done.14 = f32[16,128]{1,0:T(8,128)S(1)} collective-permute-done((f32[16,128]{1,0:T(8,128)S(1)}, f32[16,128]{1,0:T(8,128)S(1)}, u32[]{:S(2)}, u32[]{:S(2)}) %collective-permute-start.14) | collective-permute-done | bytes 8224 | tf_op jit(solution)/shard_map/ppermute | solution.py:300
  45.6 3.2 %collective-permute-done.15 = f32[16,128]{1,0:T(8,128)S(1)} collective-permute-done((f32[16,128]{1,0:T(8,128)S(1)}, f32[16,128]{1,0:T(8,128)S(1)}, u32[]{:S(2)}, u32[]{:S(2)}) %collective-permute-start.15) | collective-permute-done | bytes 8224 | tf_op jit(solution)/shard_map/ppermute | solution.py:300
  48.9 2.4 %collective-permute-start.16 = (f32[16,128]{1,0:T(8,128)S(1)}, f32[16,128]{1,0:T(8,128)S(1)}, u32[]{:S(2)}, u32[]{:S(2)}) collective-permute-start(f32[16,128]{1,0:T(8,128)S(1)} %log_add_fusion.1), channel_id=1, source_target_pairs={{0,18},{2,16},{16,2},{18,0},{1,19},{3,17},{17,3},{19,1},{4,22},{6,... | collective-permute-start | bytes 24584 | tf_op jit(solution)/shard_map/ppermute | solution.py:300
  51.3 2.7 %collective-permute-done.16 = f32[16,128]{1,0:T(8,128)S(1)} collective-permute-done((f32[16,128]{1,0:T(8,128)S(1)}, f32[16,128]{1,0:T(8,128)S(1)}, u32[]{:S(2)}, u32[]{:S(2)}) %collective-permute-start.16) | collective-permute-done | bytes 8224 | tf_op jit(solution)/shard_map/ppermute | solution.py:300
  54.0 3.9 %shard_map.89 = (f32[8,8,128]{2,1,0:T(8,128)S(1)}, f32[2048,1024]{1,0:T(8,128)S(1)}, f32[16,128]{1,0:T(8,128)S(1)}, f32[32,128]{1,0:T(8,128)S(1)}) custom-call(f32[16,128]{1,0:T(8,128)S(1)} %log_add_fusion.sums, bf16[4,144,128]{2,1,0:T(8,128)(2,1)S(1)} %pad_maximum_fusion.own.own_near, bf16[4,144,128]{2,1,0:T(8,128)(2,1)S(1)} %collective-permute-done.6.own.own_far, ...), custom_call_target="tpu_custom_call" | custom-call | tf_op jit(solution)/shard_map/pallas_call | solution.py:377
  57.9 13.7 %all_to_all.15.sums = f32[8,8,128]{2,1,0:T(8,128)S(1)} all-to-all(f32[8,8,128]{2,1,0:T(8,128)S(1)} %get-tuple-element.32), channel_id=1, replica_groups=mesh['z'=8,'yl'=2,'x'=4,'yh'=2,'c'=2] {'z'}, dimensions={0} | all-to-all | bytes 65536 | tf_op jit(solution)/shard_map/all_to_all | solution.py:295
  73.5 2.6 %collective-permute-start.18 = (f32[16,128]{1,0:T(8,128)S(1)}, f32[16,128]{1,0:T(8,128)S(1)}, u32[]{:S(2)}, u32[]{:S(2)}) collective-permute-start(f32[16,128]{1,0:T(8,128)S(1)} %add.70), channel_id=1, source_target_pairs={{0,4},{4,0},{8,12},{12,8},{1,5},{5,1},{9,13},{13,9},{2,6},{6,2},{1... | collective-permute-start | bytes 24584 | tf_op jit(solution)/shard_map/ppermute | solution.py:300
  76.1 1.6 %collective-permute-done.18 = f32[16,128]{1,0:T(8,128)S(1)} collective-permute-done((f32[16,128]{1,0:T(8,128)S(1)}, f32[16,128]{1,0:T(8,128)S(1)}, u32[]{:S(2)}, u32[]{:S(2)}) %collective-permute-start.18) | collective-permute-done | bytes 8224 | tf_op jit(solution)/shard_map/ppermute | solution.py:300
  78.3 3.1 %collective-permute-done.19 = f32[16,128]{1,0:T(8,128)S(1)} collective-permute-done((f32[16,128]{1,0:T(8,128)S(1)}, f32[16,128]{1,0:T(8,128)S(1)}, u32[]{:S(2)}, u32[]{:S(2)}) %collective-permute-start.19) | collective-permute-done | bytes 8224 | tf_op jit(solution)/shard_map/ppermute | solution.py:300
  81.4 3.6 %collective-permute-done.20 = f32[16,128]{1,0:T(8,128)S(1)} collective-permute-done((f32[16,128]{1,0:T(8,128)S(1)}, f32[16,128]{1,0:T(8,128)S(1)}, u32[]{:S(2)}, u32[]{:S(2)}) %collective-permute-start.20) | collective-permute-done | bytes 8224 | tf_op jit(solution)/shard_map/ppermute | solution.py:300
  85.1 2.2 %collective-permute-start.21 = (f32[16,128]{1,0:T(8,128)S(1)}, f32[16,128]{1,0:T(8,128)S(1)}, u32[]{:S(2)}, u32[]{:S(2)}) collective-permute-start(f32[16,128]{1,0:T(8,128)S(1)} %add.73), channel_id=1, source_target_pairs={{0,18},{2,16},{16,2},{18,0},{1,19},{3,17},{17,3},{19,1},{4,22},{6,... | collective-permute-start | bytes 24584 | tf_op jit(solution)/shard_map/ppermute | solution.py:300
  87.3 2.7 %collective-permute-done.21 = f32[16,128]{1,0:T(8,128)S(1)} collective-permute-done((f32[16,128]{1,0:T(8,128)S(1)}, f32[16,128]{1,0:T(8,128)S(1)}, u32[]{:S(2)}, u32[]{:S(2)}) %collective-permute-start.21) | collective-permute-done | bytes 8224 | tf_op jit(solution)/shard_map/ppermute | solution.py:300
  90.9 10.4 %all_to_all.16.sums = f32[8,8,128]{2,1,0:T(8,128)S(1)} all-to-all(f32[8,8,128]{2,1,0:T(8,128)S(1)} %shard_map.91), channel_id=1, replica_groups=mesh['z'=8,'yl'=2,'x'=4,'yh'=2,'c'=2] {'z'}, dimensions={0} | all-to-all | bytes 65536 | tf_op jit(solution)/shard_map/all_to_all | solution.py:295
  103.2 3.2 %collective-permute-start.23 = (f32[16,128]{1,0:T(8,128)S(1)}, f32[16,128]{1,0:T(8,128)S(1)}, u32[]{:S(2)}, u32[]{:S(2)}) collective-permute-start(f32[16,128]{1,0:T(8,128)S(1)} %add.75), channel_id=1, source_target_pairs={{0,4},{4,0},{8,12},{12,8},{1,5},{5,1},{9,13},{13,9},{2,6},{6,2},{1... | collective-permute-start | bytes 24584 | tf_op jit(solution)/shard_map/ppermute | solution.py:300
  108.7 3.1 %collective-permute-done.24 = f32[16,128]{1,0:T(8,128)S(1)} collective-permute-done((f32[16,128]{1,0:T(8,128)S(1)}, f32[16,128]{1,0:T(8,128)S(1)}, u32[]{:S(2)}, u32[]{:S(2)}) %collective-permute-start.24) | collective-permute-done | bytes 8224 | tf_op jit(solution)/shard_map/ppermute | solution.py:300
  111.8 3.6 %collective-permute-done.25 = f32[16,128]{1,0:T(8,128)S(1)} collective-permute-done((f32[16,128]{1,0:T(8,128)S(1)}, f32[16,128]{1,0:T(8,128)S(1)}, u32[]{:S(2)}, u32[]{:S(2)}) %collective-permute-start.25) | collective-permute-done | bytes 8224 | tf_op jit(solution)/shard_map/ppermute | solution.py:300
  115.4 2.2 %collective-permute-start.26 = (f32[16,128]{1,0:T(8,128)S(1)}, f32[16,128]{1,0:T(8,128)S(1)}, u32[]{:S(2)}, u32[]{:S(2)}) collective-permute-start(f32[16,128]{1,0:T(8,128)S(1)} %add.78), channel_id=1, source_target_pairs={{0,18},{2,16},{16,2},{18,0},{1,19},{3,17},{17,3},{19,1},{4,22},{6,... | collective-permute-start | bytes 24584 | tf_op jit(solution)/shard_map/ppermute | solution.py:300
  117.6 2.7 %collective-permute-done.26 = f32[16,128]{1,0:T(8,128)S(1)} collective-permute-done((f32[16,128]{1,0:T(8,128)S(1)}, f32[16,128]{1,0:T(8,128)S(1)}, u32[]{:S(2)}, u32[]{:S(2)}) %collective-permute-start.26) | collective-permute-done | bytes 8224 | tf_op jit(solution)/shard_map/ppermute | solution.py:300
  121.8 10.4 %all_to_all.17.sums = f32[8,8,128]{2,1,0:T(8,128)S(1)} all-to-all(f32[8,8,128]{2,1,0:T(8,128)S(1)} %get-tuple-element.39), channel_id=1, replica_groups=mesh['z'=8,'yl'=2,'x'=4,'yh'=2,'c'=2] {'z'}, dimensions={0} | all-to-all | bytes 65536 | tf_op jit(solution)/shard_map/all_to_all | solution.py:295
  (51 shorter events, 18.0 us)
Async XLA Ops:
  2.3 7.5 %collective-permute-start = (bf16[1,144,128]{2,1,0:T(8,128)(2,1)S(1)}, bf16[1,144,128]{2,1,0:T(8,128)(2,1)S(1)}, u32[]{:S(2)}, u32[]{:S(2)}) collective-permute-start(bf16[1,144,128]{2,1,0:T(8,128)(2,1)S(1)} %get-tuple-element.21), channel_id=1, source_target_pairs={{0,16},{16,0},{1,17},{17,1},{2,18},{18,2},{3,19},{19,3},{4,20},{20... | collective-permute-start | bytes 110600 | tf_op jit(solution)/shard_map/ppermute | solution.py:300
  4.0 7.8 %collective-permute-start.2 = (bf16[1,144,128]{2,1,0:T(8,128)(2,1)S(1)}, bf16[1,144,128]{2,1,0:T(8,128)(2,1)S(1)}, u32[]{:S(2)}, u32[]{:S(2)}) collective-permute-start(bf16[1,144,128]{2,1,0:T(8,128)(2,1)S(1)} %get-tuple-element.22.rest_0_), channel_id=1, source_target_pairs={{0,32},{32,64},{64,96},{96,128},{128,160},{160,192},{192,224},{224... | collective-permute-start | bytes 110600 | tf_op jit(solution)/shard_map/ppermute | solution.py:300
  5.9 5.9 %collective-permute-start.1 = (bf16[1,144,128]{2,1,0:T(8,128)(2,1)S(1)}, bf16[1,144,128]{2,1,0:T(8,128)(2,1)S(1)}, u32[]{:S(2)}, u32[]{:S(2)}) collective-permute-start(bf16[1,144,128]{2,1,0:T(8,128)(2,1)S(1)} %get-tuple-element.22.rest_0_), channel_id=1, source_target_pairs={{0,224},{32,0},{64,32},{96,64},{128,96},{160,128},{192,160},{224,1... | collective-permute-start | bytes 110600 | tf_op jit(solution)/shard_map/ppermute | solution.py:300
  11.8 4.4 %collective-permute-start.3 = (bf16[2,144,128]{2,1,0:T(8,128)(2,1)S(1)}, bf16[2,144,128]{2,1,0:T(8,128)(2,1)S(1)}, u32[]{:S(2)}, u32[]{:S(2)}) collective-permute-start(bf16[2,144,128]{2,1,0:T(8,128)(2,1)S(1)} %pad_maximum_fusion.1), channel_id=1, source_target_pairs={{0,4},{4,0},{8,12},{12,8},{1,5},{5,1},{9,13},{13,9},{2,6},{6,2},{1... | collective-permute-start | bytes 221192 | tf_op jit(solution)/shard_map/ppermute | solution.py:300
  12.3 4.9 %collective-permute-start.4 = (bf16[1,144,128]{2,1,0:T(8,128)(2,1)S(1)}, bf16[1,144,128]{2,1,0:T(8,128)(2,1)S(1)}, u32[]{:S(2)}, u32[]{:S(2)}) collective-permute-start(bf16[1,144,128]{2,1,0:T(8,128)(2,1)S(1)} %collective-permute-done.1.rest_1_), channel_id=1, source_target_pairs={{0,224},{32,0},{64,32},{96,64},{128,96},{160,128},{192,160},{224,1... | collective-permute-start | bytes 110600 | tf_op jit(solution)/shard_map/ppermute | solution.py:300
  15.6 5.2 %collective-permute-start.5 = (bf16[1,144,128]{2,1,0:T(8,128)(2,1)S(1)}, bf16[1,144,128]{2,1,0:T(8,128)(2,1)S(1)}, u32[]{:S(2)}, u32[]{:S(2)}) collective-permute-start(bf16[1,144,128]{2,1,0:T(8,128)(2,1)S(1)} %collective-permute-done.2.rest_7_), channel_id=1, source_target_pairs={{0,32},{32,64},{64,96},{96,128},{128,160},{160,192},{192,224},{224... | collective-permute-start | bytes 110600 | tf_op jit(solution)/shard_map/ppermute | solution.py:300
  20.7 7.3 %collective-permute-start.6 = (bf16[4,144,128]{2,1,0:T(8,128)(2,1)S(1)}, bf16[4,144,128]{2,1,0:T(8,128)(2,1)S(1)}, u32[]{:S(2)}, u32[]{:S(2)}) collective-permute-start(bf16[4,144,128]{2,1,0:T(8,128)(2,1)S(1)} %pad_maximum_fusion.own.own_near), channel_id=1, source_target_pairs={{0,12},{4,8},{8,4},{12,0},{1,13},{5,9},{9,5},{13,1},{2,14},{6,10},... | collective-permute-start | bytes 442376 | tf_op jit(solution)/shard_map/ppermute | solution.py:300
  22.9 5.5 %collective-permute-start.10 = (bf16[4,144,128]{2,1,0:T(8,128)(2,1)S(1)}, bf16[4,144,128]{2,1,0:T(8,128)(2,1)S(1)}, u32[]{:S(2)}, u32[]{:S(2)}) collective-permute-start(bf16[4,144,128]{2,1,0:T(8,128)(2,1)S(1)} %pad_maximum_fusion.own.own_near), channel_id=1, source_target_pairs={{0,1},{1,0},{2,3},{3,2},{4,5},{5,4},{6,7},{7,6},{8,9},{9,8},{10,11... | collective-permute-start | bytes 442376 | tf_op jit(solution)/shard_map/ppermute | solution.py:300
  22.9 4.0 %collective-permute-start.7 = (bf16[1,144,128]{2,1,0:T(8,128)(2,1)S(1)}, bf16[1,144,128]{2,1,0:T(8,128)(2,1)S(1)}, u32[]{:S(2)}, u32[]{:S(2)}) collective-permute-start(bf16[1,144,128]{2,1,0:T(8,128)(2,1)S(1)} %collective-permute-done.4.rest_2_), channel_id=1, source_target_pairs={{0,224},{32,0},{64,32},{96,64},{128,96},{160,128},{192,160},{224,1... | collective-permute-start | bytes 110600 | tf_op jit(solution)/shard_map/ppermute | solution.py:300
  22.9 5.2 %collective-permute-start.8 = (bf16[1,144,128]{2,1,0:T(8,128)(2,1)S(1)}, bf16[1,144,128]{2,1,0:T(8,128)(2,1)S(1)}, u32[]{:S(2)}, u32[]{:S(2)}) collective-permute-start(bf16[1,144,128]{2,1,0:T(8,128)(2,1)S(1)} %collective-permute-done.5.rest_6_), channel_id=1, source_target_pairs={{0,32},{32,64},{64,96},{96,128},{128,160},{160,192},{192,224},{224... | collective-permute-start | bytes 110600 | tf_op jit(solution)/shard_map/ppermute | solution.py:300
  28.1 6.1 %collective-permute-start.9 = (bf16[4,144,128]{2,1,0:T(8,128)(2,1)S(1)}, bf16[4,144,128]{2,1,0:T(8,128)(2,1)S(1)}, u32[]{:S(2)}, u32[]{:S(2)}) collective-permute-start(bf16[4,144,128]{2,1,0:T(8,128)(2,1)S(1)} %collective-permute-done.6.own.own_far), channel_id=1, source_target_pairs={{0,1},{1,0},{2,3},{3,2},{4,5},{5,4},{6,7},{7,6},{8,9},{9,8},{10,11... | collective-permute-start | bytes 442376 | tf_op jit(solution)/shard_map/ppermute | solution.py:300
  28.1 4.0 %collective-permute-start.11 = (bf16[1,144,128]{2,1,0:T(8,128)(2,1)S(1)}, bf16[1,144,128]{2,1,0:T(8,128)(2,1)S(1)}, u32[]{:S(2)}, u32[]{:S(2)}) collective-permute-start(bf16[1,144,128]{2,1,0:T(8,128)(2,1)S(1)} %collective-permute-done.7.rest_3_), channel_id=1, source_target_pairs={{0,224},{32,0},{64,32},{96,64},{128,96},{160,128},{192,160},{224,1... | collective-permute-start | bytes 110600 | tf_op jit(solution)/shard_map/ppermute | solution.py:300
  36.3 1.3 collective-permute-start.12
  37.6 3.7 %collective-permute-start.13 = (f32[16,128]{1,0:T(8,128)S(1)}, f32[16,128]{1,0:T(8,128)S(1)}, u32[]{:S(2)}, u32[]{:S(2)}) collective-permute-start(f32[16,128]{1,0:T(8,128)S(1)} %log_add_fusion.4), channel_id=1, source_target_pairs={{0,4},{4,0},{8,12},{12,8},{1,5},{5,1},{9,13},{13,9},{2,6},{6,2},{1... | collective-permute-start | bytes 24584 | tf_op jit(solution)/shard_map/ppermute | solution.py:300
  41.3 3.7 %collective-permute-start.14 = (f32[16,128]{1,0:T(8,128)S(1)}, f32[16,128]{1,0:T(8,128)S(1)}, u32[]{:S(2)}, u32[]{:S(2)}) collective-permute-start(f32[16,128]{1,0:T(8,128)S(1)} %log_add_fusion.3), channel_id=1, source_target_pairs={{0,12},{4,8},{8,4},{12,0},{1,13},{5,9},{9,5},{13,1},{2,14},{6,10},... | collective-permute-start | bytes 24584 | tf_op jit(solution)/shard_map/ppermute | solution.py:300
  45.1 3.7 %collective-permute-start.15 = (f32[16,128]{1,0:T(8,128)S(1)}, f32[16,128]{1,0:T(8,128)S(1)}, u32[]{:S(2)}, u32[]{:S(2)}) collective-permute-start(f32[16,128]{1,0:T(8,128)S(1)} %log_add_fusion.2), channel_id=1, source_target_pairs={{0,16},{16,0},{1,17},{17,1},{2,18},{18,2},{3,19},{19,3},{4,20},{20... | collective-permute-start | bytes 24584 | tf_op jit(solution)/shard_map/ppermute | solution.py:300
  48.9 5.1 %collective-permute-start.16 = (f32[16,128]{1,0:T(8,128)S(1)}, f32[16,128]{1,0:T(8,128)S(1)}, u32[]{:S(2)}, u32[]{:S(2)}) collective-permute-start(f32[16,128]{1,0:T(8,128)S(1)} %log_add_fusion.1), channel_id=1, source_target_pairs={{0,18},{2,16},{16,2},{18,0},{1,19},{3,17},{17,3},{19,1},{4,22},{6,... | collective-permute-start | bytes 24584 | tf_op jit(solution)/shard_map/ppermute | solution.py:300
  72.2 1.3 collective-permute-start.17
  73.5 4.2 %collective-permute-start.18 = (f32[16,128]{1,0:T(8,128)S(1)}, f32[16,128]{1,0:T(8,128)S(1)}, u32[]{:S(2)}, u32[]{:S(2)}) collective-permute-start(f32[16,128]{1,0:T(8,128)S(1)} %add.70), channel_id=1, source_target_pairs={{0,4},{4,0},{8,12},{12,8},{1,5},{5,1},{9,13},{13,9},{2,6},{6,2},{1... | collective-permute-start | bytes 24584 | tf_op jit(solution)/shard_map/ppermute | solution.py:300
  77.7 3.7 %collective-permute-start.19 = (f32[16,128]{1,0:T(8,128)S(1)}, f32[16,128]{1,0:T(8,128)S(1)}, u32[]{:S(2)}, u32[]{:S(2)}) collective-permute-start(f32[16,128]{1,0:T(8,128)S(1)} %add.71), channel_id=1, source_target_pairs={{0,12},{4,8},{8,4},{12,0},{1,13},{5,9},{9,5},{13,1},{2,14},{6,10},... | collective-permute-start | bytes 24584 | tf_op jit(solution)/shard_map/ppermute | solution.py:300
  81.4 3.7 %collective-permute-start.20 = (f32[16,128]{1,0:T(8,128)S(1)}, f32[16,128]{1,0:T(8,128)S(1)}, u32[]{:S(2)}, u32[]{:S(2)}) collective-permute-start(f32[16,128]{1,0:T(8,128)S(1)} %add.72), channel_id=1, source_target_pairs={{0,16},{16,0},{1,17},{17,1},{2,18},{18,2},{3,19},{19,3},{4,20},{20... | collective-permute-start | bytes 24584 | tf_op jit(solution)/shard_map/ppermute | solution.py:300
  85.1 4.9 %collective-permute-start.21 = (f32[16,128]{1,0:T(8,128)S(1)}, f32[16,128]{1,0:T(8,128)S(1)}, u32[]{:S(2)}, u32[]{:S(2)}) collective-permute-start(f32[16,128]{1,0:T(8,128)S(1)} %add.73), channel_id=1, source_target_pairs={{0,18},{2,16},{16,2},{18,0},{1,19},{3,17},{17,3},{19,1},{4,22},{6,... | collective-permute-start | bytes 24584 | tf_op jit(solution)/shard_map/ppermute | solution.py:300
  102.0 1.3 collective-permute-start.22
  103.2 4.9 %collective-permute-start.23 = (f32[16,128]{1,0:T(8,128)S(1)}, f32[16,128]{1,0:T(8,128)S(1)}, u32[]{:S(2)}, u32[]{:S(2)}) collective-permute-start(f32[16,128]{1,0:T(8,128)S(1)} %add.75), channel_id=1, source_target_pairs={{0,4},{4,0},{8,12},{12,8},{1,5},{5,1},{9,13},{13,9},{2,6},{6,2},{1... | collective-permute-start | bytes 24584 | tf_op jit(solution)/shard_map/ppermute | solution.py:300
  108.1 3.7 %collective-permute-start.24 = (f32[16,128]{1,0:T(8,128)S(1)}, f32[16,128]{1,0:T(8,128)S(1)}, u32[]{:S(2)}, u32[]{:S(2)}) collective-permute-start(f32[16,128]{1,0:T(8,128)S(1)} %add.76), channel_id=1, source_target_pairs={{0,12},{4,8},{8,4},{12,0},{1,13},{5,9},{9,5},{13,1},{2,14},{6,10},... | collective-permute-start | bytes 24584 | tf_op jit(solution)/shard_map/ppermute | solution.py:300
  111.8 3.7 %collective-permute-start.25 = (f32[16,128]{1,0:T(8,128)S(1)}, f32[16,128]{1,0:T(8,128)S(1)}, u32[]{:S(2)}, u32[]{:S(2)}) collective-permute-start(f32[16,128]{1,0:T(8,128)S(1)} %add.77), channel_id=1, source_target_pairs={{0,16},{16,0},{1,17},{17,1},{2,18},{18,2},{3,19},{19,3},{4,20},{20... | collective-permute-start | bytes 24584 | tf_op jit(solution)/shard_map/ppermute | solution.py:300
  115.4 4.9 %collective-permute-start.26 = (f32[16,128]{1,0:T(8,128)S(1)}, f32[16,128]{1,0:T(8,128)S(1)}, u32[]{:S(2)}, u32[]{:S(2)}) collective-permute-start(f32[16,128]{1,0:T(8,128)S(1)} %add.78), channel_id=1, source_target_pairs={{0,18},{2,16},{16,2},{18,0},{1,19},{3,17},{17,3},{19,1},{4,22},{6,... | collective-permute-start | bytes 24584 | tf_op jit(solution)/shard_map/ppermute | solution.py:300

commit v6 on v5

--- a/solution.py
+++ b/solution.py
@@ -9,6 +9,8 @@
 
 AXES = ("z", "yl", "x", "yh", "c")
 SIZES = (8, 2, 4, 2, 2)
+PLANE = ("yl", "x", "yh")
+PEERS = 16
 
 B = 128
 RB = 16
@@ -117,6 +119,8 @@
         shut = jnp.where((lane == k) & (tab[k, zone] != 1), PENALTY, shut)
     rider_out[0, B:, :] = tail_rows(hot, a_row[...])
     driver_out[0, B:, :] = tail_rows(shut, b_row[...])
+    for k in range(1, DB):
+        driver_out[k] = driver_out[0]
 
 
 def place(far, slot):
@@ -133,8 +137,10 @@
     return 2 * place(r // 8, r // 2 % 4) + c + other * (1 - 2 * c)
 
 
-def ring(j):
-    return (lax.axis_index("z") + j) % DB
+def block_of(r):
+    c = lax.axis_index("c")
+    other = r % 2
+    return 2 * place(r // 8, r // 2 % 4) + c + other * (1 - 2 * c)
 
 
 def widen(messages, wide):
@@ -142,60 +148,66 @@
         wide[k * B : (k + 1) * B] = with_zone(message, zone_rows(message))
 
 
-def rider_part(own, other, drivers, rows, left):
-    widen([driver[0] for driver in drivers], left)
-
-    def pair(slot, carry):
-        mine, theirs = own[slot], other[slot]
+def rider_rows(riders, drivers, rows, first):
+    def pair(h, carry):
+        one, two = riders[2 * h], riders[2 * h + 1]
         right = jnp.concatenate(
-            [with_zone(mine, zone_rows(mine)), with_zone(theirs, zone_rows(theirs))], axis=0
+            [with_zone(one, zone_rows(one)), with_zone(two, zone_rows(two))], axis=0
         )
-        cost = product(left[...], right)
+        cost = product(drivers[...], right)
         pieces = [cost[z * B : (z + 1) * B] for z in range(DB)]
         low = tree([fold(piece, jnp.minimum) for piece in pieces], jnp.minimum)
         low = jnp.min(low, axis=0, keepdims=True)
         mass = tree([fold(jnp.exp(low - piece), jnp.add) for piece in pieces], jnp.add)
         total = jnp.log(jnp.sum(mass, axis=0, keepdims=True)) - low
-        rows[pl.ds(2 * slot, 1), :] = total[:, :B]
-        rows[pl.ds(2 * slot + 1, 1), :] = total[:, B:]
+        rows[pl.ds(first + 2 * h, 1), :] = total[:, :B]
+        rows[pl.ds(first + 2 * h + 1, 1), :] = total[:, B:]
         return carry
 
-    lax.fori_loop(0, 4, pair, 0)
-
-
-def rider_near_body(own, other, *rest):
-    *drivers, rows, left = rest
-    rider_part(own, other, drivers, rows, left)
-
-
-def rider_far_body(own, other, near, *rest):
-    *drivers, out, rows, left = rest
-    rider_part(own, other, drivers, rows, left)
+    lax.fori_loop(0, 2, pair, 0)
+
+
+def rider_near_body(near, driver, rows, wide):
+    widen([driver[z] for z in range(DB)], wide)
+    rider_rows(near, wide, rows, 0)
+
+
+def rider_far_body(far, wide, rows):
+    rider_rows(far, wide, rows, 0)
+
+
+def rider_other_body(near, far, wide, own_near, own_far, out, rows):
+    rider_rows(near, wide, rows, 0)
+    rider_rows(far, wide, rows, 4)
     for r in range(RB):
-        out[pl.ds(block_of(r), 1), :] = (rows if r >= 8 else near)[r % 8 : r % 8 + 1]
+        slot = r // 2 % 4
+        if r % 2:
+            row = rows[4 * (r // 8) + slot : 4 * (r // 8) + slot + 1]
+        else:
+            row = (own_far if r >= 8 else own_near)[slot : slot + 1]
+        out[pl.ds(block_of(r), 1), :] = row
 
 
 def log_total(sums):
-    parts = [sums[k] for k in range(DB)]
+    parts = [sums[k] for k in range(sums.shape[0])]
     peak = tree(parts, jnp.maximum)
     return peak + jnp.log(tree([jnp.exp(part - peak) for part in parts], jnp.add))
 
 
 def total_of(sums):
-    return tree([sums[k] for k in range(DB)], jnp.add)
-
-
-def driver_first_body(sums, own_near, own_far, other_near, other_far, *rest):
-    *drivers, out, kernel, peaks, pots, ucol, left, right = rest
+    return tree([sums[k] for k in range(sums.shape[0])], jnp.add)
+
+
+def driver_first_body(sums, own_near, own_far, other_near, other_far, driver, right,
+                      out, kernel, peaks, pots, ucol, left):
     riders = ((own_near, other_near), (own_far, other_far))
     messages = [riders[r // 8][r % 2][r // 2 % 4] for r in range(RB)]
     widen(messages, left)
-    widen([driver[0] for driver in drivers], right)
     for r in range(RB):
         pots[pl.ds(RB + block_of(r), 1), :] = weight_row(messages[r])
     for j in range(DB):
-        peaks[pl.ds(DB + ring(j), 1), :] = weight_row(drivers[j][0])
-    pots[0:RB] = pots[RB:] - (sums[...] - LOG_DRIVERS)
+        peaks[DB + j : DB + j + 1, :] = weight_row(driver[j])
+    pots[0:RB] = pots[RB:] - (log_total(sums) - LOG_DRIVERS)
     for r in range(RB):
         ucol[r * B : (r + 1) * B, :] = column(pots[pl.ds(block_of(r), 1), :])
 
@@ -216,8 +228,8 @@
             total = total + fold(term, jnp.add)
         total = top + jnp.log(jnp.maximum(jnp.sum(total, axis=0, keepdims=True), TINY))
         for k in range(2):
-            peaks[pl.ds(ring(2 * h + k), 1), :] = top[:, k * B : (k + 1) * B]
-            out[0, pl.ds(ring(2 * h + k), 1), :] = total[:, k * B : (k + 1) * B]
+            peaks[pl.ds(2 * h + k, 1), :] = top[:, k * B : (k + 1) * B]
+            out[0, pl.ds(2 * h + k, 1), :] = total[:, k * B : (k + 1) * B]
         return carry
 
     lax.fori_loop(0, DB // 2, pair, 0)
@@ -226,12 +238,11 @@
 
 
 def row_sums(kernel, scale, out):
-    weight = [scale[pl.ds(ring(j), 1), :] for j in range(DB)]
     for r in range(RB):
         rows = slice(r * B, (r + 1) * B)
-        acc = kernel[rows, 0:B] * weight[0]
+        acc = kernel[rows, 0:B] * scale[0:1]
         for k in range(1, DB):
-            acc = acc + kernel[rows, k * B : (k + 1) * B] * weight[k]
+            acc = acc + kernel[rows, k * B : (k + 1) * B] * scale[k : k + 1]
         out[pl.ds(block_of(r), 1), :] = jnp.sum(acc.T, axis=0, keepdims=True)
 
 
@@ -249,7 +260,7 @@
 
     acc = lax.fori_loop(0, RB, block, tuple(jnp.zeros((8, B), F32) for _ in range(DB)))
     for j in range(DB):
-        hold[pl.ds(ring(j), 1), :] = jnp.sum(acc[j], axis=0, keepdims=True)
+        hold[j : j + 1, :] = jnp.sum(acc[j], axis=0, keepdims=True)
     return hold[0:DB] * state[2 * DB : 3 * DB]
 
 
@@ -263,7 +274,7 @@
 
 
 def driver_next_body(sums, pots, state, kernel, out, fcol, hold):
-    rows = column_sums(kernel, jnp.exp(pots[RB:] + LOG_DRIVERS) / sums[...], state, fcol, hold)
+    rows = column_sums(kernel, jnp.exp(pots[RB:] + LOG_DRIVERS) / total_of(sums), state, fcol, hold)
     for k in range(DB):
         out[k] = rows
 
@@ -273,52 +284,30 @@
     row_sums(kernel, scale, out)
 
 
-def driver_last_body(sums, pots, state, kernel, out, rider_pot, fcol, hold):
-    log_a = pots[RB:]
-    hold[...] = pots[0:RB] + (log_a + LOG_DRIVERS - jnp.log(sums[...]))
-    block = lax.axis_index("yl") * 4 + lax.axis_index("x")
-    rider_pot[0:1] = hold[pl.ds(2 * block, 1), :]
-    rider_pot[1:2] = hold[pl.ds(2 * block + 1, 1), :]
-    rows = column_sums(kernel, jnp.exp(log_a + LOG_DRIVERS) / sums[...], state, fcol, hold)
+def driver_last_body(sums, pots, state, kernel, out, fcol, hold):
+    f = jnp.exp(pots[RB:] + LOG_DRIVERS) / total_of(sums)
+    rows = column_sums(kernel, f, state, fcol, hold)
     for k in range(DB):
         out[k] = jnp.broadcast_to(rows[k : k + 1], (8, B))
 
 
-def finish_body(sums, state, driver_pot):
+def finish_body(sums, state, rider_sums, pots, rider_pot, driver_pot, hold):
     z = lax.axis_index("z")
     pot = state[pl.ds(z, 1), :]
     log_b = state[pl.ds(DB + z, 1), :]
     driver_pot[...] = pot + (log_b + LOG_RIDERS - jnp.log(total_of(sums)[0:1]))
-
-
-def exchange(message):
-    return lax.all_to_all(message, "z", 0, 0, tiled=True)
-
-
-def swap(value, axes, partner):
-    count = math.prod(SIZES[AXES.index(axis)] for axis in axes)
-    return lax.ppermute(value, axes, [(k, partner(k)) for k in range(count)])
-
-
-def gather(rider, driver):
-    held = {0: driver, DB: driver}
-    near, far, other = rider, None, None
-    for k in range(1, DB // 2 + 1):
-        held[k] = swap(held[k - 1], ("z",), lambda i: (i - 1) % DB)
-        if k < DB // 2:
-            held[DB - k] = swap(held[DB - k + 1], ("z",), lambda i: (i + 1) % DB)
-        if k == 1:
-            near = jnp.concatenate([near, swap(near, ("yl",), lambda i: 1 - i)], axis=0)
-        elif k == 2:
-            near = jnp.concatenate([near, swap(near, ("x",), lambda i: i ^ 1)], axis=0)
-        elif k == 3:
-            far = swap(near, ("x",), lambda i: 3 - i)
-            other = swap(near, ("c",), lambda i: 1 - i)
-        if k < 3:
-            near, held[k], held[DB - k] = lax.optimization_barrier((near, held[k], held[DB - k]))
-        elif k == 3:
-            far, held[k], held[DB - k] = lax.optimization_barrier((far, held[k], held[DB - k]))
-    return (near, far, other, swap(far, ("c",), lambda i: 1 - i)), [held[k] for k in range(DB)]
+    hold[...] = pots[0:RB] + (pots[RB:] + LOG_DRIVERS - jnp.log(total_of(rider_sums)))
+    block = lax.axis_index("yl") * 4 + lax.axis_index("x")
+    rider_pot[0:1] = hold[pl.ds(2 * block, 1), :]
+    rider_pot[1:2] = hold[pl.ds(2 * block + 1, 1), :]
+
+
+def exchange(message, axes):
+    return lax.all_to_all(message, axes, 0, 0, tiled=True)
+
+
+def swap(value, axis, partner):
+    return lax.ppermute(value, axis, [(k, partner(k)) for k in range(SIZES[AXES.index(axis)])])
 
 
 def log_add(a, b):
@@ -327,27 +316,33 @@
 
 
 def close(value, op):
-    for axes, partner in (
-        (("c",), lambda k: 1 - k),
-        (("x",), lambda k: k ^ 1),
-        (("x",), lambda k: 3 - k),
-        (("yl",), lambda k: 1 - k),
-        (("yl", "yh"), lambda k: 3 - k),
-    ):
-        value = op(value, swap(value, axes, partner))
-    return value
-
-
-def matmul_cost(riders, drivers):
-    return pl.CostEstimate(flops=2 * riders * drivers * 2 * B, transcendentals=riders * drivers,
-                           bytes_accessed=4 * riders * drivers)
+    value = op(value, swap(value, "c", lambda k: 1 - k))
+    return exchange(jnp.broadcast_to(value[None], (PEERS, RB, B)), PLANE)
+
+
+def rider_first(message, drivers):
+    near = jnp.concatenate([message, swap(message, "yl", lambda k: 1 - k)], axis=0)
+    near, drivers = lax.optimization_barrier((near, drivers))
+    drivers = exchange(drivers, "z")
+    near = jnp.concatenate([near, swap(near, "x", lambda k: k ^ 1)], axis=0)
+    far = swap(near, "x", lambda k: 3 - k)
+    quarter = pl.CostEstimate(flops=2**30, transcendentals=2**19, bytes_accessed=2**21)
+    near_rows, wide = call(
+        rider_near_body, [f32(4, B), bf16(DB * B, 2 * B)], [VM] * 2, cost=quarter
+    )(near, drivers)
+    near, far, near_rows = lax.optimization_barrier((near, far, near_rows))
+    other_near, other_far = (swap(value, "c", lambda k: 1 - k) for value in (near, far))
+    (far_rows,) = call(rider_far_body, [f32(4, B)], [VM] * 2, cost=quarter)(far, wide)
+    (sums,) = call(rider_other_body, [f32(RB, B)], [VM] * 5, [pltpu.VMEM((8, B), F32)])(
+        other_near, other_far, wide, near_rows, far_rows
+    )
+    return sums, (near, far, other_near, other_far, drivers, wide)
 
 
 def per_device(rider_emb, driver_emb, log_a, log_b, rider_zone, driver_zone, zone_table):
-    message = pltpu.VMEM((1, PAY, B), BF16)
     rider_msg, driver_msg = call(
         pack_body,
-        [message, message],
+        [pltpu.VMEM((1, PAY, B), BF16), pltpu.VMEM((DB, PAY, B), BF16)],
         [FAR] * 7,
         [
             pltpu.VMEM((1, B), F32),
@@ -362,25 +357,16 @@
         rider_emb.reshape(2, B, B), driver_emb, log_a.reshape(2, B), log_b.reshape(1, B),
         rider_zone, driver_zone, zone_table,
     )
-    riders, drivers = gather(rider_msg, driver_msg)
-    own_near, own_far, other_near, other_far = riders
-    half = matmul_cost(RB * B // 2, DB * B)
-    left = pltpu.VMEM((DB * B, 2 * B), BF16)
-    (near,) = call(rider_near_body, [f32(8, B)], [VM] * 10, [left], cost=half)(
-        own_near, other_near, *drivers
-    )
-    (sums,) = call(
-        rider_far_body, [f32(RB, B)], [VM] * 11, [pltpu.VMEM((8, B), F32), left], cost=half
-    )(own_far, other_far, near, *drivers)
+    sums, gathered = rider_first(rider_msg, driver_msg)
     sums = close(sums, log_add)
     columns = pltpu.VMEM((RB * B, B), F32)
     sums, kernel, peaks, pots = call(
         driver_first_body,
         [f32(DB, DB, B), f32(RB * B, DB * B), f32(2 * DB, B), f32(2 * RB, B)],
-        [VM] * 13,
-        [columns, pltpu.VMEM((RB * B, 2 * B), BF16), left],
-    )(sums, *riders, *drivers)
-    sums = exchange(sums)
+        [VM] * 7,
+        [columns, pltpu.VMEM((RB * B, 2 * B), BF16)],
+    )(sums, *gathered)
+    sums = exchange(sums, "z")
     columns = [columns, pltpu.VMEM((RB, B), F32)]
     sums, state = call(rider_second_body, [f32(RB, B), f32(3 * DB, B)], [VM] * 3)(
         sums, peaks, kernel
@@ -390,16 +376,19 @@
         (sums,) = call(driver_next_body, [f32(DB, DB, B)], [VM] * 4, columns)(
             sums, pots, state, kernel
         )
-        sums = exchange(sums)
+        sums = exchange(sums, "z")
         (sums,) = call(rider_next_body, [f32(RB, B)], [VM] * 3, [pltpu.VMEM((DB, B), F32)])(
             sums, state, kernel
         )
         sums = close(sums, jnp.add)
-    sums, rider_pot = call(driver_last_body, [f32(DB, 8, B), f32(2, B)], [VM] * 4, columns)(
-        sums, pots, state, kernel
-    )
-    sums = exchange(sums)
-    (driver_pot,) = call(finish_body, [f32(1, B)], [VM] * 2)(sums, state)
+    rider_sums = sums
+    (sums,) = call(driver_last_body, [f32(DB, 8, B)], [VM] * 4, columns)(
+        rider_sums, pots, state, kernel
+    )
+    sums = exchange(sums, "z")
+    rider_pot, driver_pot = call(
+        finish_body, [f32(2, B), f32(1, B)], [VM] * 4, [pltpu.VMEM((RB, B), F32)]
+    )(sums, state, rider_sums, pots)
     return rider_pot.reshape(2 * B), driver_pot.reshape(B)
 
 

time: 135 us -> 114 us (0.84); the launches traced: 133 us -> 114 us
  waiting for transfers between devices: 51.1 us -> 14.9 us
  blocking collectives: 34.4 us -> 70.3 us
  starting transfers between devices: 32.1 us -> 13.4 us
    ppermute x27 -> x8, waiting for transfers between devices: 51.1 us -> 9.43 us  [swap(): lax.ppermute(value, axis, [(k, partner(k)) for k in range(SIZES[AXES.inde...]
    all_to_all x3 -> x6, blocking collectives: 34.4 us -> 70.3 us  [exchange(): return lax.all_to_all(message, axes, 0, 0, tiled=True)]
    ppermute x27 -> x8, starting transfers between devices: 32.1 us -> 4.94 us  [swap(): lax.ppermute(value, axis, [(k, partner(k)) for k in range(SIZES[AXES.inde...]
    all_to_all x0 -> x1, starting transfers between devices: none -> 8.48 us  [exchange(): return lax.all_to_all(message, axes, 0, 0, tiled=True)]
    all_to_all x0 -> x1, waiting for transfers between devices: none -> 5.48 us  [exchange(): return lax.all_to_all(message, axes, 0, 0, tiled=True)]
    pallas_call x5 -> x6, Pallas kernels: 7.37 us -> 7.58 us  [the longest x1 2.09 us: rider_first(): call(rider_other_body, [f32(RB, B)], [VM] * 5, [pltpu.VMEM((8, B), F32)])]
  transfers between devices with their start and end apart: 27 -> 9, of which waited for: 22 -> 6; matrix products, arithmetic and copies ran while one was open for 0% -> 0% of each run, Pallas kernels for 2% -> 2%
where the time goes in v6:
time: 114 us
  blocking collectives  70.3 us (62%)
  waiting for transfers between devices  14.9 us (13%)
  Pallas kernels  13.8 us (12%)
  starting transfers between devices  13.4 us (12%)
  between operations  1.38 us (1%)
    all_to_all x6, blocking collectives, exchange(): return lax.all_to_all(message, axes, 0, 0, tiled=True)  70.3 us
    ppermute x8, waiting for transfers between devices, swap(): lax.ppermute(value, axis, [(k, partner(k)) for k in range(SIZES[AXES.inde...  9.43 us
    all_to_all x1, starting transfers between devices, exchange(): return lax.all_to_all(message, axes, 0, 0, tiled=True)  8.48 us
    all_to_all x1, waiting for transfers between devices, exchange(): return lax.all_to_all(message, axes, 0, 0, tiled=True)  5.48 us
    ppermute x8, starting transfers between devices, swap(): lax.ppermute(value, axis, [(k, partner(k)) for k in range(SIZES[AXES.inde...  4.94 us
    pallas_call x1, Pallas kernels, per_device(): call(driver_first_body, [f32(DB, DB, B), f32(RB * B, DB * B), f32(2 * DB,...  3.86 us
  transfers between devices with their start and end apart: 9, of which 6 were waited for; matrix products, arithmetic and copies ran while one was open for 0% of the time, Pallas kernels for 2%

profile of v6, /device:TPU:2, one launch (start us, length us, event | category | flops | bytes accessed | tf_op | source)
XLA Modules:
  0.0 113.9 jit_solution(16631500700503034671)
XLA Ops:
  1.3 1.8 %shard_map.86 = (bf16[1,144,128]{2,1,0:T(8,128)(2,1)S(1)}, bf16[8,144,128]{2,1,0:T(8,128)(2,1)}) custom-call(bf16[2,128,128]{2,1,0:T(8,128)(2,1)} %bitcast.5, bf16[128,128]{1,0:T(8,128)(2,1)} %driver.1, f32[2,128]{1,0:T(2,128)} %bitcast.6, f32[1,128]{1,0:T(1,128)} %bitcast.7, s32[2]{0:T(128)} %rzone.1, s32[1]{0:T(128)S(6)} %copy.10.dzone, s32[16,16]{1,0:T(8,128)} %table.1), custom_call_target="tpu_custom_call" | custom-call | tf_op jit(solution)/shard_map/pallas_call | solution.py:343
  3.1 1.7 %collective-permute-start = (bf16[1,144,128]{2,1,0:T(8,128)(2,1)S(1)}, bf16[1,144,128]{2,1,0:T(8,128)(2,1)S(1)}, u32[]{:S(2)}, u32[]{:S(2)}) collective-permute-start(bf16[1,144,128]{2,1,0:T(8,128)(2,1)S(1)} %get-tuple-element.19), channel_id=1, source_target_pairs={{0,16},{16,0},{1,17},{17,1},{2,18},{18,2},{3,19},{19,3},{4,20},{20... | collective-permute-start | bytes 110600 | tf_op jit(solution)/shard_map/ppermute | solution.py:310
  4.7 2.4 %collective-permute-done = bf16[1,144,128]{2,1,0:T(8,128)(2,1)S(1)} collective-permute-done((bf16[1,144,128]{2,1,0:T(8,128)(2,1)S(1)}, bf16[1,144,128]{2,1,0:T(8,128)(2,1)S(1)}, u32[]{:S(2)}, u32[]{:S(2)}) %collective-permute-start) | collective-permute-done | bytes 36896 | tf_op jit(solution)/shard_map/ppermute | solution.py:310
  7.1 8.5 %all-to-all-start = ((bf16[8,144,128]{2,1,0:T(8,128)(2,1)}), bf16[8,144,128]{2,1,0:T(8,128)(2,1)S(1)}, u32[]{:S(2)}, u32[]{:S(2)}) async-start(bf16[8,144,128]{2,1,0:T(8,128)(2,1)} %get-tuple-element.22), calls=%async_computation | async-start | bytes 589824 | tf_op jit(solution)/shard_map/all_to_all | solution.py:306
  15.6 0.5 collective-permute-start.1
  16.1 3.8 %collective-permute-done.1 = bf16[2,144,128]{2,1,0:T(8,128)(2,1)S(1)} collective-permute-done((bf16[2,144,128]{2,1,0:T(8,128)(2,1)S(1)}, bf16[2,144,128]{2,1,0:T(8,128)(2,1)S(1)}, u32[]{:S(2)}, u32[]{:S(2)}) %collective-permute-start.1) | collective-permute-done | bytes 73760 | tf_op jit(solution)/shard_map/ppermute | solution.py:310
  20.0 1.6 %collective-permute-start.2 = (bf16[4,144,128]{2,1,0:T(8,128)(2,1)S(1)}, bf16[4,144,128]{2,1,0:T(8,128)(2,1)S(1)}, u32[]{:S(2)}, u32[]{:S(2)}) collective-permute-start(bf16[4,144,128]{2,1,0:T(8,128)(2,1)S(1)} %constant_dynamic-update-slice_fusion.near.own_near), channel_id=1, source_target_pairs={{0,12},{4,8},{8,4},{12,0},{1,13},{5,9},{9,5},{13,1},{2,14},{6,10},... | collective-permute-start | bytes 442376 | tf_op jit(solution)/shard_map/ppermute | solution.py:310
  21.6 5.5 %all-to-all-done.driver = bf16[8,144,128]{2,1,0:T(8,128)(2,1)S(1)} async-done(((bf16[8,144,128]{2,1,0:T(8,128)(2,1)}), bf16[8,144,128]{2,1,0:T(8,128)(2,1)S(1)}, u32[]{:S(2)}, u32[]{:S(2)}) %all-to-all-start) | async-done | bytes 294944 | tf_op jit(solution)/shard_map/all_to_all | solution.py:306
  27.0 1.1 shard_map.87
  28.1 0.1 collective-permute-start.3
  28.2 0.5 collective-permute-start.4
  28.7 1.0 shard_map.88.own_far
  29.8 0.0 collective-permute-done.4.far.other_far
  29.8 2.1 %shard_map.89 = f32[16,128]{1,0:T(8,128)S(1)} custom-call(bf16[4,144,128]{2,1,0:T(8,128)(2,1)S(1)} %collective-permute-done.3.near.other_near, bf16[4,144,128]{2,1,0:T(8,128)(2,1)S(1)} %collective-permute-done.4.far.other_far, bf16[1024,256]{1,0:T(8,128)(2,1)S(1)} %get-tuple-element.26.wide.right, f32[4,128]{1,0:T(4,128)S(1)} %get-tuple-element.27.own_near, ...), custom_call_target="tpu_custom_call" | custom-call | tf_op jit(solution)/shard_map/pallas_call | solution.py:336
  31.9 0.4 collective-permute-start.5
  32.3 0.9 collective-permute-done.5
  33.2 14.1 %all_to_all.35.sums = f32[16,16,128]{2,1,0:T(8,128)S(1)} all-to-all(f32[16,16,128]{2,1,0:T(8,128)S(1)} %broadcast_in_dim.6), channel_id=1, replica_groups=mesh['z'=8,'yl'=2,'x'=4,'yh'=2,'c'=2] {'yl','x','yh'}, dimensions={0} | all-to-all | bytes 262144 | tf_op jit(solution)/shard_map/all_to_all | solution.py:306
  47.3 3.9 %shard_map.90 = (f32[8,8,128]{2,1,0:T(8,128)S(1)}, f32[2048,1024]{1,0:T(8,128)S(1)}, f32[16,128]{1,0:T(8,128)S(1)}, f32[32,128]{1,0:T(8,128)S(1)}) custom-call(f32[16,16,128]{2,1,0:T(8,128)S(1)} %all_to_all.35.sums, bf16[4,144,128]{2,1,0:T(8,128)(2,1)S(1)} %constant_dynamic-update-slice_fusion.near.own_near, ...), custom_call_target="tpu_custom_call" | custom-call | tf_op jit(solution)/shard_map/pallas_call | solution.py:363
  51.1 13.0 %all_to_all.36.sums = f32[8,8,128]{2,1,0:T(8,128)S(1)} all-to-all(f32[8,8,128]{2,1,0:T(8,128)S(1)} %get-tuple-element.28), channel_id=1, replica_groups=mesh['z'=8,'yl'=2,'x'=4,'yh'=2,'c'=2] {'z'}, dimensions={0} | all-to-all | bytes 65536 | tf_op jit(solution)/shard_map/all_to_all | solution.py:306
  64.1 0.7 shard_map.91
  64.8 0.1 collective-permute-start.6
  64.9 1.2 %collective-permute-done.6 = f32[16,128]{1,0:T(8,128)S(1)} collective-permute-done((f32[16,128]{1,0:T(8,128)S(1)}, f32[16,128]{1,0:T(8,128)S(1)}, u32[]{:S(2)}, u32[]{:S(2)}) %collective-permute-start.6) | collective-permute-done | bytes 8224 | tf_op jit(solution)/shard_map/ppermute | solution.py:310
  66.1 11.2 %all_to_all.37.sums = f32[16,16,128]{2,1,0:T(8,128)S(1)} all-to-all(f32[16,16,128]{2,1,0:T(8,128)S(1)} %broadcast_in_dim.7), channel_id=1, replica_groups=mesh['z'=8,'yl'=2,'x'=4,'yh'=2,'c'=2] {'yl','x','yh'}, dimensions={0} | all-to-all | bytes 262144 | tf_op jit(solution)/shard_map/all_to_all | solution.py:306
  77.3 1.0 shard_map.92
  78.3 10.4 %all_to_all.38.sums = f32[8,8,128]{2,1,0:T(8,128)S(1)} all-to-all(f32[8,8,128]{2,1,0:T(8,128)S(1)} %shard_map.92), channel_id=1, replica_groups=mesh['z'=8,'yl'=2,'x'=4,'yh'=2,'c'=2] {'z'}, dimensions={0} | all-to-all | bytes 65536 | tf_op jit(solution)/shard_map/all_to_all | solution.py:306
  88.7 0.7 shard_map.93
  89.4 0.1 collective-permute-start.7
  89.5 1.2 %collective-permute-done.7 = f32[16,128]{1,0:T(8,128)S(1)} collective-permute-done((f32[16,128]{1,0:T(8,128)S(1)}, f32[16,128]{1,0:T(8,128)S(1)}, u32[]{:S(2)}, u32[]{:S(2)}) %collective-permute-start.7) | collective-permute-done | bytes 8224 | tf_op jit(solution)/shard_map/ppermute | solution.py:310
  90.7 11.2 %all_to_all.39.sums.rider_sums = f32[16,16,128]{2,1,0:T(8,128)S(1)} all-to-all(f32[16,16,128]{2,1,0:T(8,128)S(1)} %broadcast_in_dim.8), channel_id=1, replica_groups=mesh['z'=8,'yl'=2,'x'=4,'yh'=2,'c'=2] {'yl','x','yh'}, dimensions={0} | all-to-all | bytes 262144 | tf_op jit(solution)/shard_map/all_to_all | solution.py:306
  101.9 1.0 shard_map.94
  102.9 10.4 %all_to_all.40.sums = f32[8,8,128]{2,1,0:T(8,128)S(1)} all-to-all(f32[8,8,128]{2,1,0:T(8,128)S(1)} %shard_map.94), channel_id=1, replica_groups=mesh['z'=8,'yl'=2,'x'=4,'yh'=2,'c'=2] {'z'}, dimensions={0} | all-to-all | bytes 65536 | tf_op jit(solution)/shard_map/all_to_all | solution.py:306
  113.3 0.6 shard_map.95
  (11 shorter events, 0.1 us)
Async XLA Ops:
  3.1 4.0 %collective-permute-start = (bf16[1,144,128]{2,1,0:T(8,128)(2,1)S(1)}, bf16[1,144,128]{2,1,0:T(8,128)(2,1)S(1)}, u32[]{:S(2)}, u32[]{:S(2)}) collective-permute-start(bf16[1,144,128]{2,1,0:T(8,128)(2,1)S(1)} %get-tuple-element.19), channel_id=1, source_target_pairs={{0,16},{16,0},{1,17},{17,1},{2,18},{18,2},{3,19},{19,3},{4,20},{20... | collective-permute-start | bytes 110600 | tf_op jit(solution)/shard_map/ppermute | solution.py:310
  7.1 19.9 %all-to-all-start = ((bf16[8,144,128]{2,1,0:T(8,128)(2,1)}), bf16[8,144,128]{2,1,0:T(8,128)(2,1)S(1)}, u32[]{:S(2)}, u32[]{:S(2)}) async-start(bf16[8,144,128]{2,1,0:T(8,128)(2,1)} %get-tuple-element.22), calls=%async_computation | async-start | bytes 589824 | tf_op jit(solution)/shard_map/all_to_all | solution.py:306
  15.6 4.4 %collective-permute-start.1 = (bf16[2,144,128]{2,1,0:T(8,128)(2,1)S(1)}, bf16[2,144,128]{2,1,0:T(8,128)(2,1)S(1)}, u32[]{:S(2)}, u32[]{:S(2)}) collective-permute-start(bf16[2,144,128]{2,1,0:T(8,128)(2,1)S(1)} %pad_maximum_fusion), channel_id=1, source_target_pairs={{0,4},{4,0},{8,12},{12,8},{1,5},{5,1},{9,13},{13,9},{2,6},{6,2},{1... | collective-permute-start | bytes 221192 | tf_op jit(solution)/shard_map/ppermute | solution.py:310
  20.0 8.1 %collective-permute-start.2 = (bf16[4,144,128]{2,1,0:T(8,128)(2,1)S(1)}, bf16[4,144,128]{2,1,0:T(8,128)(2,1)S(1)}, u32[]{:S(2)}, u32[]{:S(2)}) collective-permute-start(bf16[4,144,128]{2,1,0:T(8,128)(2,1)S(1)} %constant_dynamic-update-slice_fusion.near.own_near), channel_id=1, source_target_pairs={{0,12},{4,8},{8,4},{12,0},{1,13},{5,9},{9,5},{13,1},{2,14},{6,10},... | collective-permute-start | bytes 442376 | tf_op jit(solution)/shard_map/ppermute | solution.py:310
  28.1 1.6 %collective-permute-start.3 = (bf16[4,144,128]{2,1,0:T(8,128)(2,1)S(1)}, bf16[4,144,128]{2,1,0:T(8,128)(2,1)S(1)}, u32[]{:S(2)}, u32[]{:S(2)}) collective-permute-start(bf16[4,144,128]{2,1,0:T(8,128)(2,1)S(1)} %constant_dynamic-update-slice_fusion.near.own_near), channel_id=1, source_target_pairs={{0,1},{1,0},{2,3},{3,2},{4,5},{5,4},{6,7},{7,6},{8,9},{9,8},{10,11... | collective-permute-start | bytes 442376 | tf_op jit(solution)/shard_map/ppermute | solution.py:310
  28.2 1.6 %collective-permute-start.4 = (bf16[4,144,128]{2,1,0:T(8,128)(2,1)S(1)}, bf16[4,144,128]{2,1,0:T(8,128)(2,1)S(1)}, u32[]{:S(2)}, u32[]{:S(2)}) collective-permute-start(bf16[4,144,128]{2,1,0:T(8,128)(2,1)S(1)} %collective-permute-done.2.far.own_far), channel_id=1, source_target_pairs={{0,1},{1,0},{2,3},{3,2},{4,5},{5,4},{6,7},{7,6},{8,9},{9,8},{10,11... | collective-permute-start | bytes 442376 | tf_op jit(solution)/shard_map/ppermute | solution.py:310
  31.9 1.3 %collective-permute-start.5 = (f32[16,128]{1,0:T(8,128)S(1)}, f32[16,128]{1,0:T(8,128)S(1)}, u32[]{:S(2)}, u32[]{:S(2)}) collective-permute-start(f32[16,128]{1,0:T(8,128)S(1)} %shard_map.89), channel_id=1, source_target_pairs={{0,1},{1,0},{2,3},{3,2},{4,5},{5,4},{6,7},{7,6},{8,9},{9,8},{10,11... | collective-permute-start | bytes 24584 | tf_op jit(solution)/shard_map/ppermute | solution.py:310
  64.8 1.3 %collective-permute-start.6 = (f32[16,128]{1,0:T(8,128)S(1)}, f32[16,128]{1,0:T(8,128)S(1)}, u32[]{:S(2)}, u32[]{:S(2)}) collective-permute-start(f32[16,128]{1,0:T(8,128)S(1)} %get-tuple-element.31), channel_id=1, source_target_pairs={{0,1},{1,0},{2,3},{3,2},{4,5},{5,4},{6,7},{7,6},{8,9},{9,8},{10,11... | collective-permute-start | bytes 24584 | tf_op jit(solution)/shard_map/ppermute | solution.py:310
  89.4 1.3 %collective-permute-start.7 = (f32[16,128]{1,0:T(8,128)S(1)}, f32[16,128]{1,0:T(8,128)S(1)}, u32[]{:S(2)}, u32[]{:S(2)}) collective-permute-start(f32[16,128]{1,0:T(8,128)S(1)} %shard_map.93), channel_id=1, source_target_pairs={{0,1},{1,0},{2,3},{3,2},{4,5},{5,4},{6,7},{7,6},{8,9},{9,8},{10,11... | collective-permute-start | bytes 24584 | tf_op jit(solution)/shard_map/ppermute | solution.py:310

commit v7 on v6

--- a/solution.py
+++ b/solution.py
@@ -211,28 +211,28 @@
     for r in range(RB):
         ucol[r * B : (r + 1) * B, :] = column(pots[pl.ds(block_of(r), 1), :])
 
-    def pair(h, carry):
-        lanes = pl.ds(pl.multiple_of(h * 2 * B, 2 * B), 2 * B)
+    def four(h, carry):
+        lanes = pl.ds(pl.multiple_of(h * 4 * B, 4 * B), 4 * B)
         cost = product(left[...], right[lanes, :])
-        high = jnp.full((8, 2 * B), FLOOR, F32)
+        high = jnp.full((8, 4 * B), FLOOR, F32)
         for r in range(RB):
             u = ucol[r * B : (r + 1) * B, :]
-            score = jnp.concatenate([u, u], axis=1) - cost[r * B : (r + 1) * B]
+            score = jnp.concatenate([u] * 4, axis=1) - cost[r * B : (r + 1) * B]
             kernel[r * B : (r + 1) * B, lanes] = score
             high = jnp.maximum(high, fold(score, jnp.maximum))
         top = jnp.max(high, axis=0, keepdims=True)
-        total = jnp.zeros((8, 2 * B), F32)
+        total = jnp.zeros((8, 4 * B), F32)
         for r in range(RB):
             term = jnp.exp(kernel[r * B : (r + 1) * B, lanes] - top)
             kernel[r * B : (r + 1) * B, lanes] = term
             total = total + fold(term, jnp.add)
         total = top + jnp.log(jnp.maximum(jnp.sum(total, axis=0, keepdims=True), TINY))
-        for k in range(2):
-            peaks[pl.ds(2 * h + k, 1), :] = top[:, k * B : (k + 1) * B]
-            out[0, pl.ds(2 * h + k, 1), :] = total[:, k * B : (k + 1) * B]
+        for k in range(4):
+            peaks[pl.ds(4 * h + k, 1), :] = top[:, k * B : (k + 1) * B]
+            out[0, pl.ds(4 * h + k, 1), :] = total[:, k * B : (k + 1) * B]
         return carry
 
-    lax.fori_loop(0, DB // 2, pair, 0)
+    lax.fori_loop(0, DB // 4, four, 0)
     for k in range(1, DB):
         out[k] = out[0]
 
@@ -322,7 +322,6 @@
 
 def rider_first(message, drivers):
     near = jnp.concatenate([message, swap(message, "yl", lambda k: 1 - k)], axis=0)
-    near, drivers = lax.optimization_barrier((near, drivers))
     drivers = exchange(drivers, "z")
     near = jnp.concatenate([near, swap(near, "x", lambda k: k ^ 1)], axis=0)
     far = swap(near, "x", lambda k: 3 - k)

time: 114 us -> 114 us (level)
  blocking collectives: 70.3 us -> 73.2 us
  waiting for transfers between devices: 14.9 us -> 12 us
    all_to_all x6, blocking collectives: 70.3 us -> 73.2 us  [exchange(): return lax.all_to_all(message, axes, 0, 0, tiled=True)]
    all_to_all x1, waiting for transfers between devices: 5.48 us -> 2.57 us  [exchange(): return lax.all_to_all(message, axes, 0, 0, tiled=True)]
where the time goes in v7:
time: 114 us; the launch traced here: 113 us
  blocking collectives  73.2 us (64%)
  starting transfers between devices  13.4 us (12%)
  Pallas kernels  13.2 us (12%)
  waiting for transfers between devices  12 us (11%)
  between operations  1.38 us (1%)
    all_to_all x6, blocking collectives, exchange(): return lax.all_to_all(message, axes, 0, 0, tiled=True)  73.2 us
    ppermute x8, waiting for transfers between devices, swap(): lax.ppermute(value, axis, [(k, partner(k)) for k in range(SIZES[AXES.inde...  9.42 us
    all_to_all x1, starting transfers between devices, exchange(): return lax.all_to_all(message, axes, 0, 0, tiled=True)  8.48 us
    ppermute x8, starting transfers between devices, swap(): lax.ppermute(value, axis, [(k, partner(k)) for k in range(SIZES[AXES.inde...  4.94 us
    pallas_call x1, Pallas kernels, per_device(): call(driver_first_body, [f32(DB, DB, B), f32(RB * B, DB * B), f32(2 * DB,...  3.31 us
    all_to_all x1, waiting for transfers between devices, exchange(): return lax.all_to_all(message, axes, 0, 0, tiled=True)  2.57 us
  transfers between devices with their start and end apart: 9, of which 6 were waited for; matrix products, arithmetic and copies ran while one was open for 0% of the time, Pallas kernels for 2%

profile of v7, /device:TPU:2, one launch (start us, length us, event | category | flops | bytes accessed | tf_op | source)
XLA Modules:
  0.0 113.4 jit_solution(7294050788159434543)
XLA Ops:
  1.3 1.8 %shard_map.86 = (bf16[1,144,128]{2,1,0:T(8,128)(2,1)S(1)}, bf16[8,144,128]{2,1,0:T(8,128)(2,1)}) custom-call(bf16[2,128,128]{2,1,0:T(8,128)(2,1)} %bitcast.5, bf16[128,128]{1,0:T(8,128)(2,1)} %driver.1, f32[2,128]{1,0:T(2,128)} %bitcast.6, f32[1,128]{1,0:T(1,128)} %bitcast.7, s32[2]{0:T(128)} %rzone.1, s32[1]{0:T(128)S(6)} %copy.11.dzone, s32[16,16]{1,0:T(8,128)} %table.1), custom_call_target="tpu_custom_call" | custom-call | tf_op jit(solution)/shard_map/pallas_call | solution.py:342
  3.1 8.5 %all-to-all-start = ((bf16[8,144,128]{2,1,0:T(8,128)(2,1)}), bf16[8,144,128]{2,1,0:T(8,128)(2,1)S(1)}, u32[]{:S(2)}, u32[]{:S(2)}) async-start(bf16[8,144,128]{2,1,0:T(8,128)(2,1)} %get-tuple-element.18), calls=%async_computation | async-start | bytes 589824 | tf_op jit(solution)/shard_map/all_to_all | solution.py:306
  11.5 1.6 %collective-permute-start = (bf16[1,144,128]{2,1,0:T(8,128)(2,1)S(1)}, bf16[1,144,128]{2,1,0:T(8,128)(2,1)S(1)}, u32[]{:S(2)}, u32[]{:S(2)}) collective-permute-start(bf16[1,144,128]{2,1,0:T(8,128)(2,1)S(1)} %get-tuple-element.17), channel_id=1, source_target_pairs={{0,16},{16,0},{1,17},{17,1},{2,18},{18,2},{3,19},{19,3},{4,20},{20... | collective-permute-start | bytes 110600 | tf_op jit(solution)/shard_map/ppermute | solution.py:310
  13.1 2.4 %collective-permute-done = bf16[1,144,128]{2,1,0:T(8,128)(2,1)S(1)} collective-permute-done((bf16[1,144,128]{2,1,0:T(8,128)(2,1)S(1)}, bf16[1,144,128]{2,1,0:T(8,128)(2,1)S(1)}, u32[]{:S(2)}, u32[]{:S(2)}) %collective-permute-start) | collective-permute-done | bytes 36896 | tf_op jit(solution)/shard_map/ppermute | solution.py:310
  15.5 0.6 collective-permute-start.1
  16.1 3.8 %collective-permute-done.1 = bf16[2,144,128]{2,1,0:T(8,128)(2,1)S(1)} collective-permute-done((bf16[2,144,128]{2,1,0:T(8,128)(2,1)S(1)}, bf16[2,144,128]{2,1,0:T(8,128)(2,1)S(1)}, u32[]{:S(2)}, u32[]{:S(2)}) %collective-permute-start.1) | collective-permute-done | bytes 73760 | tf_op jit(solution)/shard_map/ppermute | solution.py:310
  20.0 1.6 %collective-permute-start.2 = (bf16[4,144,128]{2,1,0:T(8,128)(2,1)S(1)}, bf16[4,144,128]{2,1,0:T(8,128)(2,1)S(1)}, u32[]{:S(2)}, u32[]{:S(2)}) collective-permute-start(bf16[4,144,128]{2,1,0:T(8,128)(2,1)S(1)} %constant_dynamic-update-slice_fusion.near.own_near), channel_id=1, source_target_pairs={{0,12},{4,8},{8,4},{12,0},{1,13},{5,9},{9,5},{13,1},{2,14},{6,10},... | collective-permute-start | bytes 442376 | tf_op jit(solution)/shard_map/ppermute | solution.py:310
  21.6 2.6 %all-to-all-done.driver = bf16[8,144,128]{2,1,0:T(8,128)(2,1)S(1)} async-done(((bf16[8,144,128]{2,1,0:T(8,128)(2,1)}), bf16[8,144,128]{2,1,0:T(8,128)(2,1)S(1)}, u32[]{:S(2)}, u32[]{:S(2)}) %all-to-all-start) | async-done | bytes 294944 | tf_op jit(solution)/shard_map/all_to_all | solution.py:306
  24.1 1.1 shard_map.87
  25.2 0.1 collective-permute-start.3
  25.3 0.5 collective-permute-start.4
  25.8 1.0 shard_map.88.own_far
  26.8 0.0 collective-permute-done.4.far.other_far
  26.9 2.1 %shard_map.89 = f32[16,128]{1,0:T(8,128)S(1)} custom-call(bf16[4,144,128]{2,1,0:T(8,128)(2,1)S(1)} %collective-permute-done.3.near.other_near, bf16[4,144,128]{2,1,0:T(8,128)(2,1)S(1)} %collective-permute-done.4.far.other_far, bf16[1024,256]{1,0:T(8,128)(2,1)S(1)} %get-tuple-element.22.wide.right, f32[4,128]{1,0:T(4,128)S(1)} %get-tuple-element.23.own_near, ...), custom_call_target="tpu_custom_call" | custom-call | tf_op jit(solution)/shard_map/pallas_call | solution.py:335
  29.0 0.4 collective-permute-start.5
  29.4 0.9 collective-permute-done.5
  30.3 14.9 %all_to_all.35.sums = f32[16,16,128]{2,1,0:T(8,128)S(1)} all-to-all(f32[16,16,128]{2,1,0:T(8,128)S(1)} %broadcast_in_dim.6), channel_id=1, replica_groups=mesh['z'=8,'yl'=2,'x'=4,'yh'=2,'c'=2] {'yl','x','yh'}, dimensions={0} | all-to-all | bytes 262144 | tf_op jit(solution)/shard_map/all_to_all | solution.py:306
  45.2 3.3 %shard_map.90 = (f32[8,8,128]{2,1,0:T(8,128)S(1)}, f32[2048,1024]{1,0:T(8,128)S(1)}, f32[16,128]{1,0:T(8,128)S(1)}, f32[32,128]{1,0:T(8,128)S(1)}) custom-call(f32[16,16,128]{2,1,0:T(8,128)S(1)} %all_to_all.35.sums, bf16[4,144,128]{2,1,0:T(8,128)(2,1)S(1)} %constant_dynamic-update-slice_fusion.near.own_near, ...), custom_call_target="tpu_custom_call" | custom-call | tf_op jit(solution)/shard_map/pallas_call | solution.py:362
  48.5 15.0 %all_to_all.36.sums = f32[8,8,128]{2,1,0:T(8,128)S(1)} all-to-all(f32[8,8,128]{2,1,0:T(8,128)S(1)} %get-tuple-element.24), channel_id=1, replica_groups=mesh['z'=8,'yl'=2,'x'=4,'yh'=2,'c'=2] {'z'}, dimensions={0} | all-to-all | bytes 65536 | tf_op jit(solution)/shard_map/all_to_all | solution.py:306
  63.6 0.7 shard_map.91
  64.2 0.1 collective-permute-start.6
  64.3 1.2 %collective-permute-done.6 = f32[16,128]{1,0:T(8,128)S(1)} collective-permute-done((f32[16,128]{1,0:T(8,128)S(1)}, f32[16,128]{1,0:T(8,128)S(1)}, u32[]{:S(2)}, u32[]{:S(2)}) %collective-permute-start.6) | collective-permute-done | bytes 8224 | tf_op jit(solution)/shard_map/ppermute | solution.py:310
  65.5 11.2 %all_to_all.37.sums = f32[16,16,128]{2,1,0:T(8,128)S(1)} all-to-all(f32[16,16,128]{2,1,0:T(8,128)S(1)} %broadcast_in_dim.7), channel_id=1, replica_groups=mesh['z'=8,'yl'=2,'x'=4,'yh'=2,'c'=2] {'yl','x','yh'}, dimensions={0} | all-to-all | bytes 262144 | tf_op jit(solution)/shard_map/all_to_all | solution.py:306
  76.8 1.0 shard_map.92
  77.8 10.4 %all_to_all.38.sums = f32[8,8,128]{2,1,0:T(8,128)S(1)} all-to-all(f32[8,8,128]{2,1,0:T(8,128)S(1)} %shard_map.92), channel_id=1, replica_groups=mesh['z'=8,'yl'=2,'x'=4,'yh'=2,'c'=2] {'z'}, dimensions={0} | all-to-all | bytes 65536 | tf_op jit(solution)/shard_map/all_to_all | solution.py:306
  88.2 0.7 shard_map.93
  88.8 0.1 collective-permute-start.7
  88.9 1.2 %collective-permute-done.7 = f32[16,128]{1,0:T(8,128)S(1)} collective-permute-done((f32[16,128]{1,0:T(8,128)S(1)}, f32[16,128]{1,0:T(8,128)S(1)}, u32[]{:S(2)}, u32[]{:S(2)}) %collective-permute-start.7) | collective-permute-done | bytes 8224 | tf_op jit(solution)/shard_map/ppermute | solution.py:310
  90.1 11.2 %all_to_all.39.sums.rider_sums = f32[16,16,128]{2,1,0:T(8,128)S(1)} all-to-all(f32[16,16,128]{2,1,0:T(8,128)S(1)} %broadcast_in_dim.8), channel_id=1, replica_groups=mesh['z'=8,'yl'=2,'x'=4,'yh'=2,'c'=2] {'yl','x','yh'}, dimensions={0} | all-to-all | bytes 262144 | tf_op jit(solution)/shard_map/all_to_all | solution.py:306
  101.4 1.0 shard_map.94
  102.4 10.4 %all_to_all.40.sums = f32[8,8,128]{2,1,0:T(8,128)S(1)} all-to-all(f32[8,8,128]{2,1,0:T(8,128)S(1)} %shard_map.94), channel_id=1, replica_groups=mesh['z'=8,'yl'=2,'x'=4,'yh'=2,'c'=2] {'z'}, dimensions={0} | all-to-all | bytes 65536 | tf_op jit(solution)/shard_map/all_to_all | solution.py:306
  112.8 0.6 shard_map.95
  (12 shorter events, 0.1 us)
Async XLA Ops:
  3.1 21.1 %all-to-all-start = ((bf16[8,144,128]{2,1,0:T(8,128)(2,1)}), bf16[8,144,128]{2,1,0:T(8,128)(2,1)S(1)}, u32[]{:S(2)}, u32[]{:S(2)}) async-start(bf16[8,144,128]{2,1,0:T(8,128)(2,1)} %get-tuple-element.18), calls=%async_computation | async-start | bytes 589824 | tf_op jit(solution)/shard_map/all_to_all | solution.py:306
  11.5 4.0 %collective-permute-start = (bf16[1,144,128]{2,1,0:T(8,128)(2,1)S(1)}, bf16[1,144,128]{2,1,0:T(8,128)(2,1)S(1)}, u32[]{:S(2)}, u32[]{:S(2)}) collective-permute-start(bf16[1,144,128]{2,1,0:T(8,128)(2,1)S(1)} %get-tuple-element.17), channel_id=1, source_target_pairs={{0,16},{16,0},{1,17},{17,1},{2,18},{18,2},{3,19},{19,3},{4,20},{20... | collective-permute-start | bytes 110600 | tf_op jit(solution)/shard_map/ppermute | solution.py:310
  15.5 4.4 %collective-permute-start.1 = (bf16[2,144,128]{2,1,0:T(8,128)(2,1)S(1)}, bf16[2,144,128]{2,1,0:T(8,128)(2,1)S(1)}, u32[]{:S(2)}, u32[]{:S(2)}) collective-permute-start(bf16[2,144,128]{2,1,0:T(8,128)(2,1)S(1)} %pad_maximum_fusion), channel_id=1, source_target_pairs={{0,4},{4,0},{8,12},{12,8},{1,5},{5,1},{9,13},{13,9},{2,6},{6,2},{1... | collective-permute-start | bytes 221192 | tf_op jit(solution)/shard_map/ppermute | solution.py:310
  20.0 5.2 %collective-permute-start.2 = (bf16[4,144,128]{2,1,0:T(8,128)(2,1)S(1)}, bf16[4,144,128]{2,1,0:T(8,128)(2,1)S(1)}, u32[]{:S(2)}, u32[]{:S(2)}) collective-permute-start(bf16[4,144,128]{2,1,0:T(8,128)(2,1)S(1)} %constant_dynamic-update-slice_fusion.near.own_near), channel_id=1, source_target_pairs={{0,12},{4,8},{8,4},{12,0},{1,13},{5,9},{9,5},{13,1},{2,14},{6,10},... | collective-permute-start | bytes 442376 | tf_op jit(solution)/shard_map/ppermute | solution.py:310
  25.2 1.6 %collective-permute-start.3 = (bf16[4,144,128]{2,1,0:T(8,128)(2,1)S(1)}, bf16[4,144,128]{2,1,0:T(8,128)(2,1)S(1)}, u32[]{:S(2)}, u32[]{:S(2)}) collective-permute-start(bf16[4,144,128]{2,1,0:T(8,128)(2,1)S(1)} %constant_dynamic-update-slice_fusion.near.own_near), channel_id=1, source_target_pairs={{0,1},{1,0},{2,3},{3,2},{4,5},{5,4},{6,7},{7,6},{8,9},{9,8},{10,11... | collective-permute-start | bytes 442376 | tf_op jit(solution)/shard_map/ppermute | solution.py:310
  25.3 1.6 %collective-permute-start.4 = (bf16[4,144,128]{2,1,0:T(8,128)(2,1)S(1)}, bf16[4,144,128]{2,1,0:T(8,128)(2,1)S(1)}, u32[]{:S(2)}, u32[]{:S(2)}) collective-permute-start(bf16[4,144,128]{2,1,0:T(8,128)(2,1)S(1)} %collective-permute-done.2.far.own_far), channel_id=1, source_target_pairs={{0,1},{1,0},{2,3},{3,2},{4,5},{5,4},{6,7},{7,6},{8,9},{9,8},{10,11... | collective-permute-start | bytes 442376 | tf_op jit(solution)/shard_map/ppermute | solution.py:310
  29.0 1.3 %collective-permute-start.5 = (f32[16,128]{1,0:T(8,128)S(1)}, f32[16,128]{1,0:T(8,128)S(1)}, u32[]{:S(2)}, u32[]{:S(2)}) collective-permute-start(f32[16,128]{1,0:T(8,128)S(1)} %shard_map.89), channel_id=1, source_target_pairs={{0,1},{1,0},{2,3},{3,2},{4,5},{5,4},{6,7},{7,6},{8,9},{9,8},{10,11... | collective-permute-start | bytes 24584 | tf_op jit(solution)/shard_map/ppermute | solution.py:310
  64.2 1.3 %collective-permute-start.6 = (f32[16,128]{1,0:T(8,128)S(1)}, f32[16,128]{1,0:T(8,128)S(1)}, u32[]{:S(2)}, u32[]{:S(2)}) collective-permute-start(f32[16,128]{1,0:T(8,128)S(1)} %get-tuple-element.27), channel_id=1, source_target_pairs={{0,1},{1,0},{2,3},{3,2},{4,5},{5,4},{6,7},{7,6},{8,9},{9,8},{10,11... | collective-permute-start | bytes 24584 | tf_op jit(solution)/shard_map/ppermute | solution.py:310
  88.8 1.3 %collective-permute-start.7 = (f32[16,128]{1,0:T(8,128)S(1)}, f32[16,128]{1,0:T(8,128)S(1)}, u32[]{:S(2)}, u32[]{:S(2)}) collective-permute-start(f32[16,128]{1,0:T(8,128)S(1)} %shard_map.93), channel_id=1, source_target_pairs={{0,1},{1,0},{2,3},{3,2},{4,5},{5,4},{6,7},{7,6},{8,9},{9,8},{10,11... | collective-permute-start | bytes 24584 | tf_op jit(solution)/shard_map/ppermute | solution.py:310

commit v8 on v7

--- a/solution.py
+++ b/solution.py
@@ -29,7 +29,7 @@
 FAR = pl.BlockSpec(memory_space=pltpu.HBM)
 
 
-def call(body, outs, ins, scratch=(), limit=40, cost=None):
+def call(body, outs, ins, scratch=(), limit=20, cost=None):
     return pl.pallas_call(
         body,
         out_shape=outs,
@@ -133,14 +133,7 @@
 
 def block_of(r):
     c = lax.axis_index("c")
-    other = r % 2
-    return 2 * place(r // 8, r // 2 % 4) + c + other * (1 - 2 * c)
-
-
-def block_of(r):
-    c = lax.axis_index("c")
-    other = r % 2
-    return 2 * place(r // 8, r // 2 % 4) + c + other * (1 - 2 * c)
+    return 2 * place(r // 4 % 2, r % 4) + c + r // 8 * (1 - 2 * c)
 
 
 def widen(messages, wide):
@@ -148,44 +141,37 @@
         wide[k * B : (k + 1) * B] = with_zone(message, zone_rows(message))
 
 
-def rider_rows(riders, drivers, rows, first):
-    def pair(h, carry):
-        one, two = riders[2 * h], riders[2 * h + 1]
-        right = jnp.concatenate(
-            [with_zone(one, zone_rows(one)), with_zone(two, zone_rows(two))], axis=0
-        )
-        cost = product(drivers[...], right)
-        pieces = [cost[z * B : (z + 1) * B] for z in range(DB)]
-        low = tree([fold(piece, jnp.minimum) for piece in pieces], jnp.minimum)
-        low = jnp.min(low, axis=0, keepdims=True)
-        mass = tree([fold(jnp.exp(low - piece), jnp.add) for piece in pieces], jnp.add)
-        total = jnp.log(jnp.sum(mass, axis=0, keepdims=True)) - low
-        rows[pl.ds(first + 2 * h, 1), :] = total[:, :B]
-        rows[pl.ds(first + 2 * h + 1, 1), :] = total[:, B:]
-        return carry
-
-    lax.fori_loop(0, 2, pair, 0)
-
-
-def rider_near_body(near, driver, rows, wide):
+def rider_rows(riders, drivers, cost, rows, first, left):
+    widen([riders[k] for k in range(4)], left)
+    for h in range(DB // 2):
+        lanes = slice(2 * h * B, 2 * (h + 1) * B)
+        cost[:, lanes] = product(left[...], drivers[lanes, :])
+    for k in range(4):
+        pieces = [cost[k * B : (k + 1) * B, j * B : (j + 1) * B] for j in range(DB)]
+        low = tree(pieces, jnp.minimum)
+        mass = tree([jnp.exp(low - piece) for piece in pieces], jnp.add).T
+        low = low.T
+        least = jnp.min(low, axis=0, keepdims=True)
+        mass = jnp.sum(mass * jnp.exp(least - low), axis=0, keepdims=True)
+        rows[first + k : first + k + 1, :] = jnp.log(mass) - least
+
+
+def rider_near_body(near, driver, cost, rows, wide, left):
     widen([driver[z] for z in range(DB)], wide)
-    rider_rows(near, wide, rows, 0)
-
-
-def rider_far_body(far, wide, rows):
-    rider_rows(far, wide, rows, 0)
-
-
-def rider_other_body(near, far, wide, own_near, own_far, out, rows):
-    rider_rows(near, wide, rows, 0)
-    rider_rows(far, wide, rows, 4)
-    for r in range(RB):
-        slot = r // 2 % 4
-        if r % 2:
-            row = rows[4 * (r // 8) + slot : 4 * (r // 8) + slot + 1]
-        else:
-            row = (own_far if r >= 8 else own_near)[slot : slot + 1]
-        out[pl.ds(block_of(r), 1), :] = row
+    rider_rows(near, wide, cost, rows, 0, left)
+
+
+def rider_far_body(far, wide, cost, rows, left):
+    rider_rows(far, wide, cost, rows, 0, left)
+
+
+def rider_other_body(near, far, wide, own_near, own_far, near_cost, far_cost, out, rows, left):
+    rows[0:4] = own_near[...]
+    rows[4:8] = own_far[...]
+    rider_rows(near, wide, near_cost, rows, 8, left)
+    rider_rows(far, wide, far_cost, rows, 12, left)
+    for r in range(RB):
+        out[pl.ds(block_of(r), 1), :] = rows[r : r + 1]
 
 
 def log_total(sums):
@@ -198,41 +184,36 @@
     return tree([sums[k] for k in range(sums.shape[0])], jnp.add)
 
 
-def driver_first_body(sums, own_near, own_far, other_near, other_far, driver, right,
-                      out, kernel, peaks, pots, ucol, left):
-    riders = ((own_near, other_near), (own_far, other_far))
-    messages = [riders[r // 8][r % 2][r // 2 % 4] for r in range(RB)]
-    widen(messages, left)
-    for r in range(RB):
-        pots[pl.ds(RB + block_of(r), 1), :] = weight_row(messages[r])
+def driver_first_body(sums, own_near, own_far, other_near, other_far, driver, *rest):
+    *costs, out, kernel, peaks, pots, ucol = rest
+    messages = (own_near, own_far, other_near, other_far)
+    for r in range(RB):
+        pots[pl.ds(RB + block_of(r), 1), :] = weight_row(messages[r // 4][r % 4])
     for j in range(DB):
         peaks[DB + j : DB + j + 1, :] = weight_row(driver[j])
     pots[0:RB] = pots[RB:] - (log_total(sums) - LOG_DRIVERS)
     for r in range(RB):
         ucol[r * B : (r + 1) * B, :] = column(pots[pl.ds(block_of(r), 1), :])
 
-    def four(h, carry):
-        lanes = pl.ds(pl.multiple_of(h * 4 * B, 4 * B), 4 * B)
-        cost = product(left[...], right[lanes, :])
-        high = jnp.full((8, 4 * B), FLOOR, F32)
-        for r in range(RB):
-            u = ucol[r * B : (r + 1) * B, :]
-            score = jnp.concatenate([u] * 4, axis=1) - cost[r * B : (r + 1) * B]
-            kernel[r * B : (r + 1) * B, lanes] = score
-            high = jnp.maximum(high, fold(score, jnp.maximum))
-        top = jnp.max(high, axis=0, keepdims=True)
-        total = jnp.zeros((8, 4 * B), F32)
-        for r in range(RB):
-            term = jnp.exp(kernel[r * B : (r + 1) * B, lanes] - top)
-            kernel[r * B : (r + 1) * B, lanes] = term
-            total = total + fold(term, jnp.add)
-        total = top + jnp.log(jnp.maximum(jnp.sum(total, axis=0, keepdims=True), TINY))
-        for k in range(4):
-            peaks[pl.ds(4 * h + k, 1), :] = top[:, k * B : (k + 1) * B]
-            out[0, pl.ds(4 * h + k, 1), :] = total[:, k * B : (k + 1) * B]
-        return carry
-
-    lax.fori_loop(0, DB // 4, four, 0)
+    def scores(r):
+        u = ucol[r * B : (r + 1) * B, :]
+        rows = slice(r % 4 * B, (r % 4 + 1) * B)
+        return [u - costs[r // 4][rows, j * B : (j + 1) * B] for j in range(DB)]
+
+    high = [jnp.full((8, B), FLOOR, F32)] * DB
+    for r in range(RB):
+        high = [jnp.maximum(h, fold(score, jnp.maximum)) for h, score in zip(high, scores(r))]
+    top = [jnp.max(h, axis=0, keepdims=True) for h in high]
+    total = [jnp.zeros((8, B), F32)] * DB
+    for r in range(RB):
+        for j, score in enumerate(scores(r)):
+            term = jnp.exp(score - top[j])
+            kernel[r * B : (r + 1) * B, j * B : (j + 1) * B] = term
+            total[j] = total[j] + fold(term, jnp.add)
+    for j in range(DB):
+        mass = jnp.maximum(jnp.sum(total[j], axis=0, keepdims=True), TINY)
+        peaks[j : j + 1] = top[j]
+        out[0, j : j + 1] = top[j] + jnp.log(mass)
     for k in range(1, DB):
         out[k] = out[0]
 
@@ -326,16 +307,18 @@
     near = jnp.concatenate([near, swap(near, "x", lambda k: k ^ 1)], axis=0)
     far = swap(near, "x", lambda k: 3 - k)
     quarter = pl.CostEstimate(flops=2**30, transcendentals=2**19, bytes_accessed=2**21)
-    near_rows, wide = call(
-        rider_near_body, [f32(4, B), bf16(DB * B, 2 * B)], [VM] * 2, cost=quarter
+    cost, rows, left = f32(4 * B, DB * B), f32(4, B), pltpu.VMEM((4 * B, 2 * B), BF16)
+    own_near_cost, near_rows, wide = call(
+        rider_near_body, [cost, rows, bf16(DB * B, 2 * B)], [VM] * 2, [left], cost=quarter
     )(near, drivers)
     near, far, near_rows = lax.optimization_barrier((near, far, near_rows))
     other_near, other_far = (swap(value, "c", lambda k: 1 - k) for value in (near, far))
-    (far_rows,) = call(rider_far_body, [f32(4, B)], [VM] * 2, cost=quarter)(far, wide)
-    (sums,) = call(rider_other_body, [f32(RB, B)], [VM] * 5, [pltpu.VMEM((8, B), F32)])(
-        other_near, other_far, wide, near_rows, far_rows
-    )
-    return sums, (near, far, other_near, other_far, drivers, wide)
+    own_far_cost, far_rows = call(rider_far_body, [cost, rows], [VM] * 2, [left], cost=quarter)(far, wide)
+    other_near_cost, other_far_cost, sums = call(
+        rider_other_body, [cost, cost, f32(RB, B)], [VM] * 5, [pltpu.VMEM((RB, B), F32), left]
+    )(other_near, other_far, wide, near_rows, far_rows)
+    costs = own_near_cost, own_far_cost, other_near_cost, other_far_cost
+    return sums, (near, far, other_near, other_far, drivers, *costs)
 
 
 def per_device(rider_emb, driver_emb, log_a, log_b, rider_zone, driver_zone, zone_table):
@@ -362,8 +345,8 @@
     sums, kernel, peaks, pots = call(
         driver_first_body,
         [f32(DB, DB, B), f32(RB * B, DB * B), f32(2 * DB, B), f32(2 * RB, B)],
-        [VM] * 7,
-        [columns, pltpu.VMEM((RB * B, 2 * B), BF16)],
+        [VM] * 10,
+        [columns],
     )(sums, *gathered)
     sums = exchange(sums, "z")
     columns = [columns, pltpu.VMEM((RB, B), F32)]

time: 114 us -> 112 us (0.982)
  Pallas kernels: 13.2 us -> 10.5 us
    pallas_call x3, Pallas kernels: 4.19 us -> 2.82 us  [the longest x1 1.27 us: rider_first(): call(rider_other_body, [cost, cost, f32(RB, B)], [VM] * 5, [pltpu.VMEM((R...]
    pallas_call x1, Pallas kernels: 3.31 us -> 2.02 us  [per_device(): call(driver_first_body, [f32(DB, DB, B), f32(RB * B, DB * B), f32(2 * DB,...]
  transfers between devices with their start and end apart: 9 -> 9, of which waited for: 6 -> 9; matrix products, arithmetic and copies ran while one was open for 0% -> 0% of each run, Pallas kernels for 2% -> 1%
where the time goes in v8:
time: 112 us; the launch traced here: 111 us
  blocking collectives  73.3 us (65%)
  starting transfers between devices  13.3 us (12%)
  waiting for transfers between devices  12.5 us (11%)
  Pallas kernels  10.5 us (9%)
  between operations  1.35 us (1%)
    all_to_all x6, blocking collectives, exchange(): return lax.all_to_all(message, axes, 0, 0, tiled=True)  73.3 us
    ppermute x8, waiting for transfers between devices, swap(): lax.ppermute(value, axis, [(k, partner(k)) for k in range(SIZES[AXES.inde...  9.97 us
    all_to_all x1, starting transfers between devices, exchange(): return lax.all_to_all(message, axes, 0, 0, tiled=True)  8.48 us
    ppermute x8, starting transfers between devices, swap(): lax.ppermute(value, axis, [(k, partner(k)) for k in range(SIZES[AXES.inde...  4.86 us
    all_to_all x1, waiting for transfers between devices, exchange(): return lax.all_to_all(message, axes, 0, 0, tiled=True)  2.57 us
  transfers between devices with their start and end apart: 9, of which 9 were waited for; matrix products, arithmetic and copies ran while one was open for 0% of the time, Pallas kernels for 1%

profile of v8, /device:TPU:2, one launch (start us, length us, event | category | flops | bytes accessed | tf_op | source)
XLA Modules:
  0.0 111.2 jit_solution(6486646396726381353)
XLA Ops:
  1.3 1.8 %shard_map.86 = (bf16[1,144,128]{2,1,0:T(8,128)(2,1)S(1)}, bf16[8,144,128]{2,1,0:T(8,128)(2,1)}) custom-call(bf16[2,128,128]{2,1,0:T(8,128)(2,1)} %bitcast.5, bf16[128,128]{1,0:T(8,128)(2,1)} %driver.1, f32[2,128]{1,0:T(2,128)} %bitcast.6, f32[1,128]{1,0:T(1,128)} %bitcast.7, s32[2]{0:T(128)} %rzone.1, s32[1]{0:T(128)S(6)} %copy.11.dzone, s32[16,16]{1,0:T(8,128)} %table.1), custom_call_target="tpu_custom_call" | custom-call | tf_op jit(solution)/shard_map/pallas_call | solution.py:325
  3.1 8.5 %all-to-all-start = ((bf16[8,144,128]{2,1,0:T(8,128)(2,1)}), bf16[8,144,128]{2,1,0:T(8,128)(2,1)S(1)}, u32[]{:S(2)}, u32[]{:S(2)}) async-start(bf16[8,144,128]{2,1,0:T(8,128)(2,1)} %get-tuple-element.24), calls=%async_computation | async-start | bytes 589824 | tf_op jit(solution)/shard_map/all_to_all | solution.py:287
  11.6 1.6 %collective-permute-start = (bf16[1,144,128]{2,1,0:T(8,128)(2,1)S(1)}, bf16[1,144,128]{2,1,0:T(8,128)(2,1)S(1)}, u32[]{:S(2)}, u32[]{:S(2)}) collective-permute-start(bf16[1,144,128]{2,1,0:T(8,128)(2,1)S(1)} %get-tuple-element.23), channel_id=1, source_target_pairs={{0,16},{16,0},{1,17},{17,1},{2,18},{18,2},{3,19},{19,3},{4,20},{20... | collective-permute-start | bytes 110600 | tf_op jit(solution)/shard_map/ppermute | solution.py:291
  13.1 2.4 %collective-permute-done = bf16[1,144,128]{2,1,0:T(8,128)(2,1)S(1)} collective-permute-done((bf16[1,144,128]{2,1,0:T(8,128)(2,1)S(1)}, bf16[1,144,128]{2,1,0:T(8,128)(2,1)S(1)}, u32[]{:S(2)}, u32[]{:S(2)}) %collective-permute-start) | collective-permute-done | bytes 36896 | tf_op jit(solution)/shard_map/ppermute | solution.py:291
  15.5 0.6 collective-permute-start.1
  16.2 3.8 %collective-permute-done.1 = bf16[2,144,128]{2,1,0:T(8,128)(2,1)S(1)} collective-permute-done((bf16[2,144,128]{2,1,0:T(8,128)(2,1)S(1)}, bf16[2,144,128]{2,1,0:T(8,128)(2,1)S(1)}, u32[]{:S(2)}, u32[]{:S(2)}) %collective-permute-start.1) | collective-permute-done | bytes 73760 | tf_op jit(solution)/shard_map/ppermute | solution.py:291
  20.0 1.6 %collective-permute-start.2 = (bf16[4,144,128]{2,1,0:T(8,128)(2,1)S(1)}, bf16[4,144,128]{2,1,0:T(8,128)(2,1)S(1)}, u32[]{:S(2)}, u32[]{:S(2)}) collective-permute-start(bf16[4,144,128]{2,1,0:T(8,128)(2,1)S(1)} %constant_dynamic-update-slice_fusion.near.own_near), channel_id=1, source_target_pairs={{0,12},{4,8},{8,4},{12,0},{1,13},{5,9},{9,5},{13,1},{2,14},{6,10},... | collective-permute-start | bytes 442376 | tf_op jit(solution)/shard_map/ppermute | solution.py:291
  21.6 2.6 %all-to-all-done.driver = bf16[8,144,128]{2,1,0:T(8,128)(2,1)S(1)} async-done(((bf16[8,144,128]{2,1,0:T(8,128)(2,1)}), bf16[8,144,128]{2,1,0:T(8,128)(2,1)S(1)}, u32[]{:S(2)}, u32[]{:S(2)}) %all-to-all-start) | async-done | bytes 294944 | tf_op jit(solution)/shard_map/all_to_all | solution.py:287
  24.1 0.8 shard_map.87
  24.9 0.3 collective-permute-done.2.far.own_far
  25.2 0.5 collective-permute-start.4
  25.7 0.8 shard_map.88
  26.6 0.2 collective-permute-done.4.far.other_far
  26.8 1.3 %shard_map.89 = (f32[512,1024]{1,0:T(8,128)S(1)}, f32[512,1024]{1,0:T(8,128)S(1)}, f32[16,128]{1,0:T(8,128)S(1)}) custom-call(bf16[4,144,128]{2,1,0:T(8,128)(2,1)S(1)} %collective-permute-done.3.near.other_near, bf16[4,144,128]{2,1,0:T(8,128)(2,1)S(1)} %collective-permute-done.4.far.other_far, bf16[1024,256]{1,0:T(8,128)(2,1)S(1)} %get-tuple-element.28.wide, ...), custom_call_target="tpu_custom_call" | custom-call | tf_op jit(solution)/shard_map/pallas_call | solution.py:317
  28.1 0.4 collective-permute-start.5
  28.4 0.9 collective-permute-done.5
  29.4 15.1 %all_to_all.35.sums = f32[16,16,128]{2,1,0:T(8,128)S(1)} all-to-all(f32[16,16,128]{2,1,0:T(8,128)S(1)} %broadcast_in_dim.6), channel_id=1, replica_groups=mesh['z'=8,'yl'=2,'x'=4,'yh'=2,'c'=2] {'yl','x','yh'}, dimensions={0} | all-to-all | bytes 262144 | tf_op jit(solution)/shard_map/all_to_all | solution.py:287
  44.4 2.0 %shard_map.90 = (f32[8,8,128]{2,1,0:T(8,128)S(1)}, f32[2048,1024]{1,0:T(8,128)S(1)}, f32[16,128]{1,0:T(8,128)S(1)}, f32[32,128]{1,0:T(8,128)S(1)}) custom-call(f32[16,16,128]{2,1,0:T(8,128)S(1)} %all_to_all.35.sums, bf16[4,144,128]{2,1,0:T(8,128)(2,1)S(1)} %constant_dynamic-update-slice_fusion.near.own_near, ...), custom_call_target="tpu_custom_call" | custom-call | tf_op jit(solution)/shard_map/pallas_call | solution.py:345
  46.4 15.0 %all_to_all.36.sums = f32[8,8,128]{2,1,0:T(8,128)S(1)} all-to-all(f32[8,8,128]{2,1,0:T(8,128)S(1)} %get-tuple-element.36), channel_id=1, replica_groups=mesh['z'=8,'yl'=2,'x'=4,'yh'=2,'c'=2] {'z'}, dimensions={0} | all-to-all | bytes 65536 | tf_op jit(solution)/shard_map/all_to_all | solution.py:287
  61.5 0.7 shard_map.91
  62.1 0.1 collective-permute-start.6
  62.2 1.2 %collective-permute-done.6 = f32[16,128]{1,0:T(8,128)S(1)} collective-permute-done((f32[16,128]{1,0:T(8,128)S(1)}, f32[16,128]{1,0:T(8,128)S(1)}, u32[]{:S(2)}, u32[]{:S(2)}) %collective-permute-start.6) | collective-permute-done | bytes 8224 | tf_op jit(solution)/shard_map/ppermute | solution.py:291
  63.4 11.2 %all_to_all.37.sums = f32[16,16,128]{2,1,0:T(8,128)S(1)} all-to-all(f32[16,16,128]{2,1,0:T(8,128)S(1)} %broadcast_in_dim.7), channel_id=1, replica_groups=mesh['z'=8,'yl'=2,'x'=4,'yh'=2,'c'=2] {'yl','x','yh'}, dimensions={0} | all-to-all | bytes 262144 | tf_op jit(solution)/shard_map/all_to_all | solution.py:287
  74.6 1.0 shard_map.92
  75.6 10.4 %all_to_all.38.sums = f32[8,8,128]{2,1,0:T(8,128)S(1)} all-to-all(f32[8,8,128]{2,1,0:T(8,128)S(1)} %shard_map.92), channel_id=1, replica_groups=mesh['z'=8,'yl'=2,'x'=4,'yh'=2,'c'=2] {'z'}, dimensions={0} | all-to-all | bytes 65536 | tf_op jit(solution)/shard_map/all_to_all | solution.py:287
  86.0 0.6 shard_map.93
  86.7 0.1 collective-permute-start.7
  86.8 1.2 %collective-permute-done.7 = f32[16,128]{1,0:T(8,128)S(1)} collective-permute-done((f32[16,128]{1,0:T(8,128)S(1)}, f32[16,128]{1,0:T(8,128)S(1)}, u32[]{:S(2)}, u32[]{:S(2)}) %collective-permute-start.7) | collective-permute-done | bytes 8224 | tf_op jit(solution)/shard_map/ppermute | solution.py:291
  87.9 11.2 %all_to_all.39.sums.rider_sums = f32[16,16,128]{2,1,0:T(8,128)S(1)} all-to-all(f32[16,16,128]{2,1,0:T(8,128)S(1)} %broadcast_in_dim.8), channel_id=1, replica_groups=mesh['z'=8,'yl'=2,'x'=4,'yh'=2,'c'=2] {'yl','x','yh'}, dimensions={0} | all-to-all | bytes 262144 | tf_op jit(solution)/shard_map/all_to_all | solution.py:287
  99.2 1.0 shard_map.94
  100.2 10.4 %all_to_all.40.sums = f32[8,8,128]{2,1,0:T(8,128)S(1)} all-to-all(f32[8,8,128]{2,1,0:T(8,128)S(1)} %shard_map.94), channel_id=1, replica_groups=mesh['z'=8,'yl'=2,'x'=4,'yh'=2,'c'=2] {'z'}, dimensions={0} | all-to-all | bytes 65536 | tf_op jit(solution)/shard_map/all_to_all | solution.py:287
  110.6 0.6 shard_map.95
  (12 shorter events, 0.2 us)
Async XLA Ops:
  3.1 21.1 %all-to-all-start = ((bf16[8,144,128]{2,1,0:T(8,128)(2,1)}), bf16[8,144,128]{2,1,0:T(8,128)(2,1)S(1)}, u32[]{:S(2)}, u32[]{:S(2)}) async-start(bf16[8,144,128]{2,1,0:T(8,128)(2,1)} %get-tuple-element.24), calls=%async_computation | async-start | bytes 589824 | tf_op jit(solution)/shard_map/all_to_all | solution.py:287
  11.6 4.0 %collective-permute-start = (bf16[1,144,128]{2,1,0:T(8,128)(2,1)S(1)}, bf16[1,144,128]{2,1,0:T(8,128)(2,1)S(1)}, u32[]{:S(2)}, u32[]{:S(2)}) collective-permute-start(bf16[1,144,128]{2,1,0:T(8,128)(2,1)S(1)} %get-tuple-element.23), channel_id=1, source_target_pairs={{0,16},{16,0},{1,17},{17,1},{2,18},{18,2},{3,19},{19,3},{4,20},{20... | collective-permute-start | bytes 110600 | tf_op jit(solution)/shard_map/ppermute | solution.py:291
  15.5 4.4 %collective-permute-start.1 = (bf16[2,144,128]{2,1,0:T(8,128)(2,1)S(1)}, bf16[2,144,128]{2,1,0:T(8,128)(2,1)S(1)}, u32[]{:S(2)}, u32[]{:S(2)}) collective-permute-start(bf16[2,144,128]{2,1,0:T(8,128)(2,1)S(1)} %pad_maximum_fusion), channel_id=1, source_target_pairs={{0,4},{4,0},{8,12},{12,8},{1,5},{5,1},{9,13},{13,9},{2,6},{6,2},{1... | collective-permute-start | bytes 221192 | tf_op jit(solution)/shard_map/ppermute | solution.py:291
  20.0 5.2 %collective-permute-start.2 = (bf16[4,144,128]{2,1,0:T(8,128)(2,1)S(1)}, bf16[4,144,128]{2,1,0:T(8,128)(2,1)S(1)}, u32[]{:S(2)}, u32[]{:S(2)}) collective-permute-start(bf16[4,144,128]{2,1,0:T(8,128)(2,1)S(1)} %constant_dynamic-update-slice_fusion.near.own_near), channel_id=1, source_target_pairs={{0,12},{4,8},{8,4},{12,0},{1,13},{5,9},{9,5},{13,1},{2,14},{6,10},... | collective-permute-start | bytes 442376 | tf_op jit(solution)/shard_map/ppermute | solution.py:291
  25.2 1.4 %collective-permute-start.3 = (bf16[4,144,128]{2,1,0:T(8,128)(2,1)S(1)}, bf16[4,144,128]{2,1,0:T(8,128)(2,1)S(1)}, u32[]{:S(2)}, u32[]{:S(2)}) collective-permute-start(bf16[4,144,128]{2,1,0:T(8,128)(2,1)S(1)} %constant_dynamic-update-slice_fusion.near.own_near), channel_id=1, source_target_pairs={{0,1},{1,0},{2,3},{3,2},{4,5},{5,4},{6,7},{7,6},{8,9},{9,8},{10,11... | collective-permute-start | bytes 442376 | tf_op jit(solution)/shard_map/ppermute | solution.py:291
  25.2 1.6 %collective-permute-start.4 = (bf16[4,144,128]{2,1,0:T(8,128)(2,1)S(1)}, bf16[4,144,128]{2,1,0:T(8,128)(2,1)S(1)}, u32[]{:S(2)}, u32[]{:S(2)}) collective-permute-start(bf16[4,144,128]{2,1,0:T(8,128)(2,1)S(1)} %collective-permute-done.2.far.own_far), channel_id=1, source_target_pairs={{0,1},{1,0},{2,3},{3,2},{4,5},{5,4},{6,7},{7,6},{8,9},{9,8},{10,11... | collective-permute-start | bytes 442376 | tf_op jit(solution)/shard_map/ppermute | solution.py:291
  28.1 1.3 %collective-permute-start.5 = (f32[16,128]{1,0:T(8,128)S(1)}, f32[16,128]{1,0:T(8,128)S(1)}, u32[]{:S(2)}, u32[]{:S(2)}) collective-permute-start(f32[16,128]{1,0:T(8,128)S(1)} %get-tuple-element.31), channel_id=1, source_target_pairs={{0,1},{1,0},{2,3},{3,2},{4,5},{5,4},{6,7},{7,6},{8,9},{9,8},{10,11... | collective-permute-start | bytes 24584 | tf_op jit(solution)/shard_map/ppermute | solution.py:291
  62.1 1.3 %collective-permute-start.6 = (f32[16,128]{1,0:T(8,128)S(1)}, f32[16,128]{1,0:T(8,128)S(1)}, u32[]{:S(2)}, u32[]{:S(2)}) collective-permute-start(f32[16,128]{1,0:T(8,128)S(1)} %get-tuple-element.39), channel_id=1, source_target_pairs={{0,1},{1,0},{2,3},{3,2},{4,5},{5,4},{6,7},{7,6},{8,9},{9,8},{10,11... | collective-permute-start | bytes 24584 | tf_op jit(solution)/shard_map/ppermute | solution.py:291
  86.7 1.3 %collective-permute-start.7 = (f32[16,128]{1,0:T(8,128)S(1)}, f32[16,128]{1,0:T(8,128)S(1)}, u32[]{:S(2)}, u32[]{:S(2)}) collective-permute-start(f32[16,128]{1,0:T(8,128)S(1)} %shard_map.93), channel_id=1, source_target_pairs={{0,1},{1,0},{2,3},{3,2},{4,5},{5,4},{6,7},{7,6},{8,9},{9,8},{10,11... | collective-permute-start | bytes 24584 | tf_op jit(solution)/shard_map/ppermute | solution.py:291

commit v9 on v8

--- a/solution.py
+++ b/solution.py
@@ -125,10 +125,9 @@
 
 def place(far, slot):
     yl, x = lax.axis_index("yl"), lax.axis_index("x")
-    first, second = slot % 2, slot // 2
-    x = x + far * (3 - 2 * x)
-    x = x + second * (1 - 2 * (x % 2))
-    return (yl + first * (1 - 2 * yl)) * 4 + x
+    x = x + slot // 2 * (3 - 2 * x)
+    x = x + slot % 2 * (1 - 2 * (x % 2))
+    return (yl + far * (1 - 2 * yl)) * 4 + x
 
 
 def block_of(r):
@@ -291,6 +290,13 @@
     return lax.ppermute(value, axis, [(k, partner(k)) for k in range(SIZES[AXES.index(axis)])])
 
 
+def from_y(value, step):
+    place_of = lambda y: y % 2 * 2 + y // 2
+    return lax.ppermute(
+        value, ("yl", "yh"), [(place_of(y), place_of((y - step) % 4)) for y in range(4)]
+    )
+
+
 def log_add(a, b):
     peak = jnp.maximum(a, b)
     return peak + jnp.log(jnp.exp(a - peak) + jnp.exp(b - peak))
@@ -302,10 +308,12 @@
 
 
 def rider_first(message, drivers):
-    near = jnp.concatenate([message, swap(message, "yl", lambda k: 1 - k)], axis=0)
+    two = jnp.concatenate([message, swap(message, "x", lambda k: k ^ 1)], axis=0)
+    two, drivers = lax.optimization_barrier((two, drivers))
     drivers = exchange(drivers, "z")
-    near = jnp.concatenate([near, swap(near, "x", lambda k: k ^ 1)], axis=0)
-    far = swap(near, "x", lambda k: 3 - k)
+    mirror = swap(two, "x", lambda k: 3 - k)
+    near = jnp.concatenate([two, mirror], axis=0)
+    far = jnp.concatenate([from_y(two, 1), from_y(mirror, -1)], axis=0)
     quarter = pl.CostEstimate(flops=2**30, transcendentals=2**19, bytes_accessed=2**21)
     cost, rows, left = f32(4 * B, DB * B), f32(4, B), pltpu.VMEM((4 * B, 2 * B), BF16)
     own_near_cost, near_rows, wide = call(

time: 112 us -> 113 us (level)
  starting transfers between devices: 13.3 us -> 16.3 us
  blocking collectives: 73.3 us -> 70.7 us
  waiting for transfers between devices: 12.5 us -> 13.8 us
    ppermute x0 -> x2, waiting for transfers between devices: none -> 5.54 us  [from_y(): lax.ppermute(value, ('yl', 'yh'), [(place_of(y), place_of((y - step) % 4)...]
    ppermute x0 -> x2, starting transfers between devices: none -> 3.02 us  [from_y(): lax.ppermute(value, ('yl', 'yh'), [(place_of(y), place_of((y - step) % 4)...]
    all_to_all x6, blocking collectives: 73.3 us -> 70.7 us  [exchange(): return lax.all_to_all(message, axes, 0, 0, tiled=True)]
    all_to_all x1, waiting for transfers between devices: 2.57 us -> 0.01 us  [exchange(): return lax.all_to_all(message, axes, 0, 0, tiled=True)]
    ppermute x8 -> x7, waiting for transfers between devices: 9.97 us -> 8.28 us  [swap(): lax.ppermute(value, axis, [(k, partner(k)) for k in range(SIZES[AXES.inde...]
    ppermute x8 -> x7, starting transfers between devices: 4.86 us -> 5.01 us  [swap(): lax.ppermute(value, axis, [(k, partner(k)) for k in range(SIZES[AXES.inde...]
  transfers between devices with their start and end apart: 9 -> 10, of which waited for: 9 -> 8; matrix products, arithmetic and copies ran while one was open for 0% -> 0% of each run, Pallas kernels for 1% -> 1%
where the time goes in v9:
time: 113 us
  blocking collectives  70.7 us (63%)
  starting transfers between devices  16.3 us (14%)
  waiting for transfers between devices  13.8 us (12%)
  Pallas kernels  10.5 us (9%)
  between operations  1.38 us (1%)
    all_to_all x6, blocking collectives, exchange(): return lax.all_to_all(message, axes, 0, 0, tiled=True)  70.7 us
    ppermute x7, waiting for transfers between devices, swap(): lax.ppermute(value, axis, [(k, partner(k)) for k in range(SIZES[AXES.inde...  8.28 us
    all_to_all x1, starting transfers between devices, exchange(): return lax.all_to_all(message, axes, 0, 0, tiled=True)  8.23 us
    ppermute x2, waiting for transfers between devices, from_y(): lax.ppermute(value, ('yl', 'yh'), [(place_of(y), place_of((y - step) % 4)...  5.54 us
    ppermute x7, starting transfers between devices, swap(): lax.ppermute(value, axis, [(k, partner(k)) for k in range(SIZES[AXES.inde...  5.01 us
    ppermute x2, starting transfers between devices, from_y(): lax.ppermute(value, ('yl', 'yh'), [(place_of(y), place_of((y - step) % 4)...  3.02 us
  transfers between devices with their start and end apart: 10, of which 8 were waited for; matrix products, arithmetic and copies ran while one was open for 0% of the time, Pallas kernels for 1%

profile of v9, /device:TPU:2, one launch (start us, length us, event | category | flops | bytes accessed | tf_op | source)
XLA Modules:
  0.0 112.8 jit_solution(9620664094980433623)
XLA Ops:
  1.3 1.8 %shard_map.86 = (bf16[1,144,128]{2,1,0:T(8,128)(2,1)S(1)}, bf16[8,144,128]{2,1,0:T(8,128)(2,1)}) custom-call(bf16[2,128,128]{2,1,0:T(8,128)(2,1)} %bitcast.5, bf16[128,128]{1,0:T(8,128)(2,1)} %driver.1, f32[2,128]{1,0:T(2,128)} %bitcast.6, f32[1,128]{1,0:T(1,128)} %bitcast.7, s32[2]{0:T(128)} %rzone.1, s32[1]{0:T(128)S(6)} %copy.10.dzone, s32[16,16]{1,0:T(8,128)} %table.1), custom_call_target="tpu_custom_call" | custom-call | tf_op jit(solution)/shard_map/pallas_call | solution.py:333
  3.1 2.4 %collective-permute-start = (bf16[1,144,128]{2,1,0:T(8,128)(2,1)S(1)}, bf16[1,144,128]{2,1,0:T(8,128)(2,1)S(1)}, u32[]{:S(2)}, u32[]{:S(2)}) collective-permute-start(bf16[1,144,128]{2,1,0:T(8,128)(2,1)S(1)} %get-tuple-element.25), channel_id=1, source_target_pairs={{0,4},{4,0},{8,12},{12,8},{1,5},{5,1},{9,13},{13,9},{2,6},{6,2},{1... | collective-permute-start | bytes 110600 | tf_op jit(solution)/shard_map/ppermute | solution.py:290
  5.4 1.9 %collective-permute-done = bf16[1,144,128]{2,1,0:T(8,128)(2,1)S(1)} collective-permute-done((bf16[1,144,128]{2,1,0:T(8,128)(2,1)S(1)}, bf16[1,144,128]{2,1,0:T(8,128)(2,1)S(1)}, u32[]{:S(2)}, u32[]{:S(2)}) %collective-permute-start) | collective-permute-done | bytes 36896 | tf_op jit(solution)/shard_map/ppermute | solution.py:290
  7.4 8.2 %all-to-all-start = ((bf16[8,144,128]{2,1,0:T(8,128)(2,1)}), bf16[8,144,128]{2,1,0:T(8,128)(2,1)S(1)}, u32[]{:S(2)}, u32[]{:S(2)}) async-start(bf16[8,144,128]{2,1,0:T(8,128)(2,1)} %get-tuple-element.28), calls=%async_computation | async-start | bytes 589824 | tf_op jit(solution)/shard_map/all_to_all | solution.py:286
  15.6 3.0 %collective-permute-start.2 = (bf16[2,144,128]{2,1,0:T(8,128)(2,1)S(1)}, bf16[2,144,128]{2,1,0:T(8,128)(2,1)S(1)}, u32[]{:S(2)}, u32[]{:S(2)}) collective-permute-start(bf16[2,144,128]{2,1,0:T(8,128)(2,1)S(1)} %pad_maximum_fusion.1), channel_id=1, source_target_pairs={{0,18},{16,0},{2,16},{18,2},{1,19},{17,1},{3,17},{19,3},{4,22},{20... | collective-permute-start | bytes 221192 | tf_op jit(solution)/shard_map/ppermute | solution.py:295
  18.6 1.5 %collective-permute-start.1 = (bf16[2,144,128]{2,1,0:T(8,128)(2,1)S(1)}, bf16[2,144,128]{2,1,0:T(8,128)(2,1)S(1)}, u32[]{:S(2)}, u32[]{:S(2)}) collective-permute-start(bf16[2,144,128]{2,1,0:T(8,128)(2,1)S(1)} %pad_maximum_fusion.1), channel_id=1, source_target_pairs={{0,12},{4,8},{8,4},{12,0},{1,13},{5,9},{9,5},{13,1},{2,14},{6,10},... | collective-permute-start | bytes 221192 | tf_op jit(solution)/shard_map/ppermute | solution.py:290
  20.1 2.9 %collective-permute-done.1 = bf16[2,144,128]{2,1,0:T(8,128)(2,1)S(1)} collective-permute-done((bf16[2,144,128]{2,1,0:T(8,128)(2,1)S(1)}, bf16[2,144,128]{2,1,0:T(8,128)(2,1)S(1)}, u32[]{:S(2)}, u32[]{:S(2)}) %collective-permute-start.1) | collective-permute-done | bytes 73760 | tf_op jit(solution)/shard_map/ppermute | solution.py:290
  23.0 5.5 %collective-permute-done.3 = bf16[2,144,128]{2,1,0:T(8,128)(2,1)S(1)} collective-permute-done((bf16[2,144,128]{2,1,0:T(8,128)(2,1)S(1)}, bf16[2,144,128]{2,1,0:T(8,128)(2,1)S(1)}, u32[]{:S(2)}, u32[]{:S(2)}) %collective-permute-start.3) | collective-permute-done | bytes 73760 | tf_op jit(solution)/shard_map/ppermute | solution.py:295
  28.6 0.8 shard_map.87
  29.4 0.1 collective-permute-start.4
  29.5 0.5 collective-permute-start.5
  30.0 0.8 shard_map.88
  30.8 0.2 collective-permute-done.5.far.other_far
  31.0 1.3 %shard_map.89 = (f32[512,1024]{1,0:T(8,128)S(1)}, f32[512,1024]{1,0:T(8,128)S(1)}, f32[16,128]{1,0:T(8,128)S(1)}) custom-call(bf16[4,144,128]{2,1,0:T(8,128)(2,1)S(1)} %collective-permute-done.4.near.other_near, bf16[4,144,128]{2,1,0:T(8,128)(2,1)S(1)} %collective-permute-done.5.far.other_far, bf16[1024,256]{1,0:T(8,128)(2,1)S(1)} %get-tuple-element.32.wide, ...), custom_call_target="tpu_custom_call" | custom-call | tf_op jit(solution)/shard_map/pallas_call | solution.py:325
  32.3 0.4 collective-permute-start.6
  32.7 0.9 collective-permute-done.6
  33.6 12.6 %all_to_all.35.sums = f32[16,16,128]{2,1,0:T(8,128)S(1)} all-to-all(f32[16,16,128]{2,1,0:T(8,128)S(1)} %broadcast_in_dim.6), channel_id=1, replica_groups=mesh['z'=8,'yl'=2,'x'=4,'yh'=2,'c'=2] {'yl','x','yh'}, dimensions={0} | all-to-all | bytes 262144 | tf_op jit(solution)/shard_map/all_to_all | solution.py:286
  46.2 2.0 %shard_map.90 = (f32[8,8,128]{2,1,0:T(8,128)S(1)}, f32[2048,1024]{1,0:T(8,128)S(1)}, f32[16,128]{1,0:T(8,128)S(1)}, f32[32,128]{1,0:T(8,128)S(1)}) custom-call(f32[16,16,128]{2,1,0:T(8,128)S(1)} %all_to_all.35.sums, bf16[4,144,128]{2,1,0:T(8,128)(2,1)S(1)} %constant_dynamic-update-slice_fusion.near.own_near, ...), custom_call_target="tpu_custom_call" | custom-call | tf_op jit(solution)/shard_map/pallas_call | solution.py:353
  48.2 14.9 %all_to_all.36.sums = f32[8,8,128]{2,1,0:T(8,128)S(1)} all-to-all(f32[8,8,128]{2,1,0:T(8,128)S(1)} %get-tuple-element.40), channel_id=1, replica_groups=mesh['z'=8,'yl'=2,'x'=4,'yh'=2,'c'=2] {'z'}, dimensions={0} | all-to-all | bytes 65536 | tf_op jit(solution)/shard_map/all_to_all | solution.py:286
  63.0 0.7 shard_map.91
  63.7 0.1 collective-permute-start.7
  63.8 1.2 %collective-permute-done.7 = f32[16,128]{1,0:T(8,128)S(1)} collective-permute-done((f32[16,128]{1,0:T(8,128)S(1)}, f32[16,128]{1,0:T(8,128)S(1)}, u32[]{:S(2)}, u32[]{:S(2)}) %collective-permute-start.7) | collective-permute-done | bytes 8224 | tf_op jit(solution)/shard_map/ppermute | solution.py:290
  65.0 11.2 %all_to_all.37.sums = f32[16,16,128]{2,1,0:T(8,128)S(1)} all-to-all(f32[16,16,128]{2,1,0:T(8,128)S(1)} %broadcast_in_dim.7), channel_id=1, replica_groups=mesh['z'=8,'yl'=2,'x'=4,'yh'=2,'c'=2] {'yl','x','yh'}, dimensions={0} | all-to-all | bytes 262144 | tf_op jit(solution)/shard_map/all_to_all | solution.py:286
  76.2 1.0 shard_map.92
  77.2 10.4 %all_to_all.38.sums = f32[8,8,128]{2,1,0:T(8,128)S(1)} all-to-all(f32[8,8,128]{2,1,0:T(8,128)S(1)} %shard_map.92), channel_id=1, replica_groups=mesh['z'=8,'yl'=2,'x'=4,'yh'=2,'c'=2] {'z'}, dimensions={0} | all-to-all | bytes 65536 | tf_op jit(solution)/shard_map/all_to_all | solution.py:286
  87.6 0.6 shard_map.93
  88.3 0.1 collective-permute-start.8
  88.4 1.2 %collective-permute-done.8 = f32[16,128]{1,0:T(8,128)S(1)} collective-permute-done((f32[16,128]{1,0:T(8,128)S(1)}, f32[16,128]{1,0:T(8,128)S(1)}, u32[]{:S(2)}, u32[]{:S(2)}) %collective-permute-start.8) | collective-permute-done | bytes 8224 | tf_op jit(solution)/shard_map/ppermute | solution.py:290
  89.5 11.2 %all_to_all.39.sums.rider_sums = f32[16,16,128]{2,1,0:T(8,128)S(1)} all-to-all(f32[16,16,128]{2,1,0:T(8,128)S(1)} %broadcast_in_dim.8), channel_id=1, replica_groups=mesh['z'=8,'yl'=2,'x'=4,'yh'=2,'c'=2] {'yl','x','yh'}, dimensions={0} | all-to-all | bytes 262144 | tf_op jit(solution)/shard_map/all_to_all | solution.py:286
  100.8 1.0 shard_map.94
  101.8 10.4 %all_to_all.40.sums = f32[8,8,128]{2,1,0:T(8,128)S(1)} all-to-all(f32[8,8,128]{2,1,0:T(8,128)S(1)} %shard_map.94), channel_id=1, replica_groups=mesh['z'=8,'yl'=2,'x'=4,'yh'=2,'c'=2] {'z'}, dimensions={0} | all-to-all | bytes 65536 | tf_op jit(solution)/shard_map/all_to_all | solution.py:286
  112.2 0.6 shard_map.95
  (14 shorter events, 0.2 us)
Async XLA Ops:
  3.1 4.3 %collective-permute-start = (bf16[1,144,128]{2,1,0:T(8,128)(2,1)S(1)}, bf16[1,144,128]{2,1,0:T(8,128)(2,1)S(1)}, u32[]{:S(2)}, u32[]{:S(2)}) collective-permute-start(bf16[1,144,128]{2,1,0:T(8,128)(2,1)S(1)} %get-tuple-element.25), channel_id=1, source_target_pairs={{0,4},{4,0},{8,12},{12,8},{1,5},{5,1},{9,13},{13,9},{2,6},{6,2},{1... | collective-permute-start | bytes 110600 | tf_op jit(solution)/shard_map/ppermute | solution.py:290
  7.4 21.2 %all-to-all-start = ((bf16[8,144,128]{2,1,0:T(8,128)(2,1)}), bf16[8,144,128]{2,1,0:T(8,128)(2,1)S(1)}, u32[]{:S(2)}, u32[]{:S(2)}) async-start(bf16[8,144,128]{2,1,0:T(8,128)(2,1)} %get-tuple-element.28), calls=%async_computation | async-start | bytes 589824 | tf_op jit(solution)/shard_map/all_to_all | solution.py:286
  15.6 7.4 %collective-permute-start.2 = (bf16[2,144,128]{2,1,0:T(8,128)(2,1)S(1)}, bf16[2,144,128]{2,1,0:T(8,128)(2,1)S(1)}, u32[]{:S(2)}, u32[]{:S(2)}) collective-permute-start(bf16[2,144,128]{2,1,0:T(8,128)(2,1)S(1)} %pad_maximum_fusion.1), channel_id=1, source_target_pairs={{0,18},{16,0},{2,16},{18,2},{1,19},{17,1},{3,17},{19,3},{4,22},{20... | collective-permute-start | bytes 221192 | tf_op jit(solution)/shard_map/ppermute | solution.py:295
  18.6 4.4 %collective-permute-start.1 = (bf16[2,144,128]{2,1,0:T(8,128)(2,1)S(1)}, bf16[2,144,128]{2,1,0:T(8,128)(2,1)S(1)}, u32[]{:S(2)}, u32[]{:S(2)}) collective-permute-start(bf16[2,144,128]{2,1,0:T(8,128)(2,1)S(1)} %pad_maximum_fusion.1), channel_id=1, source_target_pairs={{0,12},{4,8},{8,4},{12,0},{1,13},{5,9},{9,5},{13,1},{2,14},{6,10},... | collective-permute-start | bytes 221192 | tf_op jit(solution)/shard_map/ppermute | solution.py:290
  23.0 5.6 %collective-permute-start.3 = (bf16[2,144,128]{2,1,0:T(8,128)(2,1)S(1)}, bf16[2,144,128]{2,1,0:T(8,128)(2,1)S(1)}, u32[]{:S(2)}, u32[]{:S(2)}) collective-permute-start(bf16[2,144,128]{2,1,0:T(8,128)(2,1)S(1)} %collective-permute-done.1), channel_id=1, source_target_pairs={{0,16},{16,2},{2,18},{18,0},{1,17},{17,3},{3,19},{19,1},{4,20},{20... | collective-permute-start | bytes 221192 | tf_op jit(solution)/shard_map/ppermute | solution.py:295
  29.4 1.5 %collective-permute-start.4 = (bf16[4,144,128]{2,1,0:T(8,128)(2,1)S(1)}, bf16[4,144,128]{2,1,0:T(8,128)(2,1)S(1)}, u32[]{:S(2)}, u32[]{:S(2)}) collective-permute-start(bf16[4,144,128]{2,1,0:T(8,128)(2,1)S(1)} %constant_dynamic-update-slice_fusion.near.own_near), channel_id=1, source_target_pairs={{0,1},{1,0},{2,3},{3,2},{4,5},{5,4},{6,7},{7,6},{8,9},{9,8},{10,11... | collective-permute-start | bytes 442376 | tf_op jit(solution)/shard_map/ppermute | solution.py:290
  29.5 1.6 %collective-permute-start.5 = (bf16[4,144,128]{2,1,0:T(8,128)(2,1)S(1)}, bf16[4,144,128]{2,1,0:T(8,128)(2,1)S(1)}, u32[]{:S(2)}, u32[]{:S(2)}) collective-permute-start(bf16[4,144,128]{2,1,0:T(8,128)(2,1)S(1)} %pad_maximum_fusion.far.own_far), channel_id=1, source_target_pairs={{0,1},{1,0},{2,3},{3,2},{4,5},{5,4},{6,7},{7,6},{8,9},{9,8},{10,11... | collective-permute-start | bytes 442376 | tf_op jit(solution)/shard_map/ppermute | solution.py:290
  32.3 1.3 %collective-permute-start.6 = (f32[16,128]{1,0:T(8,128)S(1)}, f32[16,128]{1,0:T(8,128)S(1)}, u32[]{:S(2)}, u32[]{:S(2)}) collective-permute-start(f32[16,128]{1,0:T(8,128)S(1)} %get-tuple-element.35), channel_id=1, source_target_pairs={{0,1},{1,0},{2,3},{3,2},{4,5},{5,4},{6,7},{7,6},{8,9},{9,8},{10,11... | collective-permute-start | bytes 24584 | tf_op jit(solution)/shard_map/ppermute | solution.py:290
  63.7 1.3 %collective-permute-start.7 = (f32[16,128]{1,0:T(8,128)S(1)}, f32[16,128]{1,0:T(8,128)S(1)}, u32[]{:S(2)}, u32[]{:S(2)}) collective-permute-start(f32[16,128]{1,0:T(8,128)S(1)} %get-tuple-element.43), channel_id=1, source_target_pairs={{0,1},{1,0},{2,3},{3,2},{4,5},{5,4},{6,7},{7,6},{8,9},{9,8},{10,11... | collective-permute-start | bytes 24584 | tf_op jit(solution)/shard_map/ppermute | solution.py:290
  88.3 1.3 %collective-permute-start.8 = (f32[16,128]{1,0:T(8,128)S(1)}, f32[16,128]{1,0:T(8,128)S(1)}, u32[]{:S(2)}, u32[]{:S(2)}) collective-permute-start(f32[16,128]{1,0:T(8,128)S(1)} %shard_map.93), channel_id=1, source_target_pairs={{0,1},{1,0},{2,3},{3,2},{4,5},{5,4},{6,7},{7,6},{8,9},{9,8},{10,11... | collective-permute-start | bytes 24584 | tf_op jit(solution)/shard_map/ppermute | solution.py:290

commit v10 on v9

--- a/solution.py
+++ b/solution.py
@@ -309,7 +309,6 @@
 
 def rider_first(message, drivers):
     two = jnp.concatenate([message, swap(message, "x", lambda k: k ^ 1)], axis=0)
-    two, drivers = lax.optimization_barrier((two, drivers))
     drivers = exchange(drivers, "z")
     mirror = swap(two, "x", lambda k: 3 - k)
     near = jnp.concatenate([two, mirror], axis=0)

time: 113 us -> 112 us (level)
  waiting for transfers between devices: 13.8 us -> 11 us
  blocking collectives: 70.7 us -> 72 us
    ppermute x7, starting transfers between devices: 5.01 us -> 3.27 us  [swap(): lax.ppermute(value, axis, [(k, partner(k)) for k in range(SIZES[AXES.inde...]
    ppermute x2, starting transfers between devices: 3.02 us -> 4.43 us  [from_y(): lax.ppermute(value, ('yl', 'yh'), [(place_of(y), place_of((y - step) % 4)...]
    ppermute x2, waiting for transfers between devices: 5.54 us -> 4.13 us  [from_y(): lax.ppermute(value, ('yl', 'yh'), [(place_of(y), place_of((y - step) % 4)...]
    ppermute x7, waiting for transfers between devices: 8.28 us -> 6.9 us  [swap(): lax.ppermute(value, axis, [(k, partner(k)) for k in range(SIZES[AXES.inde...]
    all_to_all x6, blocking collectives: 70.7 us -> 72 us  [exchange(): return lax.all_to_all(message, axes, 0, 0, tiled=True)]
where the time goes in v10:
time: 112 us; the launch traced here: 111 us
  blocking collectives  72 us (64%)
  starting transfers between devices  16.2 us (14%)
  waiting for transfers between devices  11 us (10%)
  Pallas kernels  10.5 us (9%)
  between operations  1.37 us (1%)
    all_to_all x6, blocking collectives, exchange(): return lax.all_to_all(message, axes, 0, 0, tiled=True)  72 us
    all_to_all x1, starting transfers between devices, exchange(): return lax.all_to_all(message, axes, 0, 0, tiled=True)  8.48 us
    ppermute x7, waiting for transfers between devices, swap(): lax.ppermute(value, axis, [(k, partner(k)) for k in range(SIZES[AXES.inde...  6.9 us
    ppermute x2, starting transfers between devices, from_y(): lax.ppermute(value, ('yl', 'yh'), [(place_of(y), place_of((y - step) % 4)...  4.43 us
    ppermute x2, waiting for transfers between devices, from_y(): lax.ppermute(value, ('yl', 'yh'), [(place_of(y), place_of((y - step) % 4)...  4.13 us
    ppermute x7, starting transfers between devices, swap(): lax.ppermute(value, axis, [(k, partner(k)) for k in range(SIZES[AXES.inde...  3.27 us
  transfers between devices with their start and end apart: 10, of which 8 were waited for; matrix products, arithmetic and copies ran while one was open for 0% of the time, Pallas kernels for 1%

profile of v10, /device:TPU:2, one launch (start us, length us, event | category | flops | bytes accessed | tf_op | source)
XLA Modules:
  0.0 111.2 jit_solution(16563700773089862204)
XLA Ops:
  1.3 1.8 %shard_map.86 = (bf16[1,144,128]{2,1,0:T(8,128)(2,1)S(1)}, bf16[8,144,128]{2,1,0:T(8,128)(2,1)}) custom-call(bf16[2,128,128]{2,1,0:T(8,128)(2,1)} %bitcast.5, bf16[128,128]{1,0:T(8,128)(2,1)} %driver.1, f32[2,128]{1,0:T(2,128)} %bitcast.6, f32[1,128]{1,0:T(1,128)} %bitcast.7, s32[2]{0:T(128)} %rzone.1, s32[1]{0:T(128)S(6)} %copy.12.dzone, s32[16,16]{1,0:T(8,128)} %table.1), custom_call_target="tpu_custom_call" | custom-call | tf_op jit(solution)/shard_map/pallas_call | solution.py:332
  3.1 8.5 %all-to-all-start = ((bf16[8,144,128]{2,1,0:T(8,128)(2,1)}), bf16[8,144,128]{2,1,0:T(8,128)(2,1)S(1)}, u32[]{:S(2)}, u32[]{:S(2)}) async-start(bf16[8,144,128]{2,1,0:T(8,128)(2,1)} %get-tuple-element.24), calls=%async_computation | async-start | bytes 589824 | tf_op jit(solution)/shard_map/all_to_all | solution.py:286
  11.6 0.5 collective-permute-start
  12.1 3.4 %collective-permute-done = bf16[1,144,128]{2,1,0:T(8,128)(2,1)S(1)} collective-permute-done((bf16[1,144,128]{2,1,0:T(8,128)(2,1)S(1)}, bf16[1,144,128]{2,1,0:T(8,128)(2,1)S(1)}, u32[]{:S(2)}, u32[]{:S(2)}) %collective-permute-start) | collective-permute-done | bytes 36896 | tf_op jit(solution)/shard_map/ppermute | solution.py:290
  15.5 1.6 %collective-permute-start.1 = (bf16[2,144,128]{2,1,0:T(8,128)(2,1)S(1)}, bf16[2,144,128]{2,1,0:T(8,128)(2,1)S(1)}, u32[]{:S(2)}, u32[]{:S(2)}) collective-permute-start(bf16[2,144,128]{2,1,0:T(8,128)(2,1)S(1)} %get-tuple-element.44), channel_id=1, source_target_pairs={{0,12},{4,8},{8,4},{12,0},{1,13},{5,9},{9,5},{13,1},{2,14},{6,10},... | collective-permute-start | bytes 221192 | tf_op jit(solution)/shard_map/ppermute | solution.py:290
  17.1 3.0 %collective-permute-start.2 = (bf16[2,144,128]{2,1,0:T(8,128)(2,1)S(1)}, bf16[2,144,128]{2,1,0:T(8,128)(2,1)S(1)}, u32[]{:S(2)}, u32[]{:S(2)}) collective-permute-start(bf16[2,144,128]{2,1,0:T(8,128)(2,1)S(1)} %get-tuple-element.44), channel_id=1, source_target_pairs={{0,18},{16,0},{2,16},{18,2},{1,19},{17,1},{3,17},{19,3},{4,22},{20... | collective-permute-start | bytes 221192 | tf_op jit(solution)/shard_map/ppermute | solution.py:295
  20.1 1.4 %collective-permute-start.3 = (bf16[2,144,128]{2,1,0:T(8,128)(2,1)S(1)}, bf16[2,144,128]{2,1,0:T(8,128)(2,1)S(1)}, u32[]{:S(2)}, u32[]{:S(2)}) collective-permute-start(bf16[2,144,128]{2,1,0:T(8,128)(2,1)S(1)} %collective-permute-done.1), channel_id=1, source_target_pairs={{0,16},{16,2},{2,18},{18,0},{1,17},{17,3},{3,19},{19,1},{4,20},{20... | collective-permute-start | bytes 221192 | tf_op jit(solution)/shard_map/ppermute | solution.py:295
  21.6 0.5 collective-permute-done.2
  22.1 3.6 %collective-permute-done.3 = bf16[2,144,128]{2,1,0:T(8,128)(2,1)S(1)} collective-permute-done((bf16[2,144,128]{2,1,0:T(8,128)(2,1)S(1)}, bf16[2,144,128]{2,1,0:T(8,128)(2,1)S(1)}, u32[]{:S(2)}, u32[]{:S(2)}) %collective-permute-start.3) | collective-permute-done | bytes 73760 | tf_op jit(solution)/shard_map/ppermute | solution.py:295
  25.7 0.8 shard_map.87
  26.5 0.1 collective-permute-start.4
  26.6 0.5 collective-permute-start.5
  27.1 0.8 shard_map.88
  28.0 0.2 collective-permute-done.5.far.other_far
  28.2 1.3 %shard_map.89 = (f32[512,1024]{1,0:T(8,128)S(1)}, f32[512,1024]{1,0:T(8,128)S(1)}, f32[16,128]{1,0:T(8,128)S(1)}) custom-call(bf16[4,144,128]{2,1,0:T(8,128)(2,1)S(1)} %collective-permute-done.4.near.other_near, bf16[4,144,128]{2,1,0:T(8,128)(2,1)S(1)} %collective-permute-done.5.far.other_far, bf16[1024,256]{1,0:T(8,128)(2,1)S(1)} %get-tuple-element.28.wide, ...), custom_call_target="tpu_custom_call" | custom-call | tf_op jit(solution)/shard_map/pallas_call | solution.py:324
  29.4 0.4 collective-permute-start.6
  29.8 0.9 collective-permute-done.6
  30.7 13.7 %all_to_all.35.sums = f32[16,16,128]{2,1,0:T(8,128)S(1)} all-to-all(f32[16,16,128]{2,1,0:T(8,128)S(1)} %broadcast_in_dim.6), channel_id=1, replica_groups=mesh['z'=8,'yl'=2,'x'=4,'yh'=2,'c'=2] {'yl','x','yh'}, dimensions={0} | all-to-all | bytes 262144 | tf_op jit(solution)/shard_map/all_to_all | solution.py:286
  44.4 2.0 %shard_map.90 = (f32[8,8,128]{2,1,0:T(8,128)S(1)}, f32[2048,1024]{1,0:T(8,128)S(1)}, f32[16,128]{1,0:T(8,128)S(1)}, f32[32,128]{1,0:T(8,128)S(1)}) custom-call(f32[16,16,128]{2,1,0:T(8,128)S(1)} %all_to_all.35.sums, bf16[4,144,128]{2,1,0:T(8,128)(2,1)S(1)} %constant_dynamic-update-slice_fusion.2.near.own_near, ...), custom_call_target="tpu_custom_call" | custom-call | tf_op jit(solution)/shard_map/pallas_call | solution.py:352
  46.4 15.0 %all_to_all.36.sums = f32[8,8,128]{2,1,0:T(8,128)S(1)} all-to-all(f32[8,8,128]{2,1,0:T(8,128)S(1)} %get-tuple-element.36), channel_id=1, replica_groups=mesh['z'=8,'yl'=2,'x'=4,'yh'=2,'c'=2] {'z'}, dimensions={0} | all-to-all | bytes 65536 | tf_op jit(solution)/shard_map/all_to_all | solution.py:286
  61.5 0.7 shard_map.91
  62.1 0.1 collective-permute-start.7
  62.2 1.2 %collective-permute-done.7 = f32[16,128]{1,0:T(8,128)S(1)} collective-permute-done((f32[16,128]{1,0:T(8,128)S(1)}, f32[16,128]{1,0:T(8,128)S(1)}, u32[]{:S(2)}, u32[]{:S(2)}) %collective-permute-start.7) | collective-permute-done | bytes 8224 | tf_op jit(solution)/shard_map/ppermute | solution.py:290
  63.4 11.2 %all_to_all.37.sums = f32[16,16,128]{2,1,0:T(8,128)S(1)} all-to-all(f32[16,16,128]{2,1,0:T(8,128)S(1)} %broadcast_in_dim.7), channel_id=1, replica_groups=mesh['z'=8,'yl'=2,'x'=4,'yh'=2,'c'=2] {'yl','x','yh'}, dimensions={0} | all-to-all | bytes 262144 | tf_op jit(solution)/shard_map/all_to_all | solution.py:286
  74.7 1.0 shard_map.92
  75.7 10.4 %all_to_all.38.sums = f32[8,8,128]{2,1,0:T(8,128)S(1)} all-to-all(f32[8,8,128]{2,1,0:T(8,128)S(1)} %shard_map.92), channel_id=1, replica_groups=mesh['z'=8,'yl'=2,'x'=4,'yh'=2,'c'=2] {'z'}, dimensions={0} | all-to-all | bytes 65536 | tf_op jit(solution)/shard_map/all_to_all | solution.py:286
  86.0 0.6 shard_map.93
  86.8 1.2 %collective-permute-done.8 = f32[16,128]{1,0:T(8,128)S(1)} collective-permute-done((f32[16,128]{1,0:T(8,128)S(1)}, f32[16,128]{1,0:T(8,128)S(1)}, u32[]{:S(2)}, u32[]{:S(2)}) %collective-permute-start.8) | collective-permute-done | bytes 8224 | tf_op jit(solution)/shard_map/ppermute | solution.py:290
  88.0 11.2 %all_to_all.39.sums.rider_sums = f32[16,16,128]{2,1,0:T(8,128)S(1)} all-to-all(f32[16,16,128]{2,1,0:T(8,128)S(1)} %broadcast_in_dim.8), channel_id=1, replica_groups=mesh['z'=8,'yl'=2,'x'=4,'yh'=2,'c'=2] {'yl','x','yh'}, dimensions={0} | all-to-all | bytes 262144 | tf_op jit(solution)/shard_map/all_to_all | solution.py:286
  99.2 1.0 shard_map.94
  100.2 10.4 %all_to_all.40.sums = f32[8,8,128]{2,1,0:T(8,128)S(1)} all-to-all(f32[8,8,128]{2,1,0:T(8,128)S(1)} %shard_map.94), channel_id=1, replica_groups=mesh['z'=8,'yl'=2,'x'=4,'yh'=2,'c'=2] {'z'}, dimensions={0} | all-to-all | bytes 65536 | tf_op jit(solution)/shard_map/all_to_all | solution.py:286
  110.6 0.6 shard_map.95
  (14 shorter events, 0.3 us)
Async XLA Ops:
  3.1 22.6 %all-to-all-start = ((bf16[8,144,128]{2,1,0:T(8,128)(2,1)}), bf16[8,144,128]{2,1,0:T(8,128)(2,1)S(1)}, u32[]{:S(2)}, u32[]{:S(2)}) async-start(bf16[8,144,128]{2,1,0:T(8,128)(2,1)} %get-tuple-element.24), calls=%async_computation | async-start | bytes 589824 | tf_op jit(solution)/shard_map/all_to_all | solution.py:286
  11.6 4.0 %collective-permute-start = (bf16[1,144,128]{2,1,0:T(8,128)(2,1)S(1)}, bf16[1,144,128]{2,1,0:T(8,128)(2,1)S(1)}, u32[]{:S(2)}, u32[]{:S(2)}) collective-permute-start(bf16[1,144,128]{2,1,0:T(8,128)(2,1)S(1)} %get-tuple-element.23), channel_id=1, source_target_pairs={{0,4},{4,0},{8,12},{12,8},{1,5},{5,1},{9,13},{13,9},{2,6},{6,2},{1... | collective-permute-start | bytes 110600 | tf_op jit(solution)/shard_map/ppermute | solution.py:290
  15.5 4.6 %collective-permute-start.1 = (bf16[2,144,128]{2,1,0:T(8,128)(2,1)S(1)}, bf16[2,144,128]{2,1,0:T(8,128)(2,1)S(1)}, u32[]{:S(2)}, u32[]{:S(2)}) collective-permute-start(bf16[2,144,128]{2,1,0:T(8,128)(2,1)S(1)} %get-tuple-element.44), channel_id=1, source_target_pairs={{0,12},{4,8},{8,4},{12,0},{1,13},{5,9},{9,5},{13,1},{2,14},{6,10},... | collective-permute-start | bytes 221192 | tf_op jit(solution)/shard_map/ppermute | solution.py:290
  17.1 5.0 %collective-permute-start.2 = (bf16[2,144,128]{2,1,0:T(8,128)(2,1)S(1)}, bf16[2,144,128]{2,1,0:T(8,128)(2,1)S(1)}, u32[]{:S(2)}, u32[]{:S(2)}) collective-permute-start(bf16[2,144,128]{2,1,0:T(8,128)(2,1)S(1)} %get-tuple-element.44), channel_id=1, source_target_pairs={{0,18},{16,0},{2,16},{18,2},{1,19},{17,1},{3,17},{19,3},{4,22},{20... | collective-permute-start | bytes 221192 | tf_op jit(solution)/shard_map/ppermute | solution.py:295
  20.1 5.6 %collective-permute-start.3 = (bf16[2,144,128]{2,1,0:T(8,128)(2,1)S(1)}, bf16[2,144,128]{2,1,0:T(8,128)(2,1)S(1)}, u32[]{:S(2)}, u32[]{:S(2)}) collective-permute-start(bf16[2,144,128]{2,1,0:T(8,128)(2,1)S(1)} %collective-permute-done.1), channel_id=1, source_target_pairs={{0,16},{16,2},{2,18},{18,0},{1,17},{17,3},{3,19},{19,1},{4,20},{20... | collective-permute-start | bytes 221192 | tf_op jit(solution)/shard_map/ppermute | solution.py:295
  26.5 1.5 %collective-permute-start.4 = (bf16[4,144,128]{2,1,0:T(8,128)(2,1)S(1)}, bf16[4,144,128]{2,1,0:T(8,128)(2,1)S(1)}, u32[]{:S(2)}, u32[]{:S(2)}) collective-permute-start(bf16[4,144,128]{2,1,0:T(8,128)(2,1)S(1)} %constant_dynamic-update-slice_fusion.2.near.own_near), channel_id=1, source_target_pairs={{0,1},{1,0},{2,3},{3,2},{4,5},{5,4},{6,7},{7,6},{8,9},{9,8},{10,11... | collective-permute-start | bytes 442376 | tf_op jit(solution)/shard_map/ppermute | solution.py:290
  26.6 1.6 %collective-permute-start.5 = (bf16[4,144,128]{2,1,0:T(8,128)(2,1)S(1)}, bf16[4,144,128]{2,1,0:T(8,128)(2,1)S(1)}, u32[]{:S(2)}, u32[]{:S(2)}) collective-permute-start(bf16[4,144,128]{2,1,0:T(8,128)(2,1)S(1)} %pad_maximum_fusion.far.own_far), channel_id=1, source_target_pairs={{0,1},{1,0},{2,3},{3,2},{4,5},{5,4},{6,7},{7,6},{8,9},{9,8},{10,11... | collective-permute-start | bytes 442376 | tf_op jit(solution)/shard_map/ppermute | solution.py:290
  29.4 1.3 %collective-permute-start.6 = (f32[16,128]{1,0:T(8,128)S(1)}, f32[16,128]{1,0:T(8,128)S(1)}, u32[]{:S(2)}, u32[]{:S(2)}) collective-permute-start(f32[16,128]{1,0:T(8,128)S(1)} %get-tuple-element.31), channel_id=1, source_target_pairs={{0,1},{1,0},{2,3},{3,2},{4,5},{5,4},{6,7},{7,6},{8,9},{9,8},{10,11... | collective-permute-start | bytes 24584 | tf_op jit(solution)/shard_map/ppermute | solution.py:290
  62.1 1.3 %collective-permute-start.7 = (f32[16,128]{1,0:T(8,128)S(1)}, f32[16,128]{1,0:T(8,128)S(1)}, u32[]{:S(2)}, u32[]{:S(2)}) collective-permute-start(f32[16,128]{1,0:T(8,128)S(1)} %get-tuple-element.39), channel_id=1, source_target_pairs={{0,1},{1,0},{2,3},{3,2},{4,5},{5,4},{6,7},{7,6},{8,9},{9,8},{10,11... | collective-permute-start | bytes 24584 | tf_op jit(solution)/shard_map/ppermute | solution.py:290
  86.7 1.3 %collective-permute-start.8 = (f32[16,128]{1,0:T(8,128)S(1)}, f32[16,128]{1,0:T(8,128)S(1)}, u32[]{:S(2)}, u32[]{:S(2)}) collective-permute-start(f32[16,128]{1,0:T(8,128)S(1)} %shard_map.93), channel_id=1, source_target_pairs={{0,1},{1,0},{2,3},{3,2},{4,5},{5,4},{6,7},{7,6},{8,9},{9,8},{10,11... | collective-permute-start | bytes 24584 | tf_op jit(solution)/shard_map/ppermute | solution.py:290

commit v11 on v10

--- a/solution.py
+++ b/solution.py
@@ -308,9 +308,13 @@
 
 
 def rider_first(message, drivers):
-    two = jnp.concatenate([message, swap(message, "x", lambda k: k ^ 1)], axis=0)
+    beside, across, behind = (
+        swap(message, "x", partner)
+        for partner in (lambda k: k ^ 1, lambda k: 3 - k, lambda k: k ^ 2)
+    )
+    two = jnp.concatenate([message, beside], axis=0)
     drivers = exchange(drivers, "z")
-    mirror = swap(two, "x", lambda k: 3 - k)
+    mirror = jnp.concatenate([across, behind], axis=0)
     near = jnp.concatenate([two, mirror], axis=0)
     far = jnp.concatenate([from_y(two, 1), from_y(mirror, -1)], axis=0)
     quarter = pl.CostEstimate(flops=2**30, transcendentals=2**19, bytes_accessed=2**21)

time: 112 us -> 110 us (0.982)
  blocking collectives: 72 us -> 67.8 us
  starting transfers between devices: 16.2 us -> 17.8 us
    all_to_all x1, waiting for transfers between devices: 0.01 us -> 5.57 us  [exchange(): return lax.all_to_all(message, axes, 0, 0, tiled=True)]
    all_to_all x6, blocking collectives: 72 us -> 67.8 us  [exchange(): return lax.all_to_all(message, axes, 0, 0, tiled=True)]
    ppermute x7 -> x8, waiting for transfers between devices: 6.9 us -> 3.5 us  [swap(): lax.ppermute(value, axis, [(k, partner(k)) for k in range(SIZES[AXES.inde...]
    ppermute x7 -> x8, starting transfers between devices: 3.27 us -> 5.94 us  [swap(): lax.ppermute(value, axis, [(k, partner(k)) for k in range(SIZES[AXES.inde...]
    ppermute x2, waiting for transfers between devices: 4.13 us -> 2.66 us  [from_y(): lax.ppermute(value, ('yl', 'yh'), [(place_of(y), place_of((y - step) % 4)...]
  transfers between devices with their start and end apart: 10 -> 11, of which waited for: 8 -> 8; matrix products, arithmetic and copies ran while one was open for 0% -> 0% of each run, Pallas kernels for 1% -> 1%
where the time goes in v11:
time: 110 us; the launch traced here: 109 us
  blocking collectives  67.8 us (62%)
  starting transfers between devices  17.8 us (16%)
  waiting for transfers between devices  11.7 us (11%)
  Pallas kernels  10.5 us (10%)
  between operations  1.4 us (1%)
    all_to_all x6, blocking collectives, exchange(): return lax.all_to_all(message, axes, 0, 0, tiled=True)  67.8 us
    all_to_all x1, starting transfers between devices, exchange(): return lax.all_to_all(message, axes, 0, 0, tiled=True)  8.47 us
    ppermute x8, starting transfers between devices, swap(): lax.ppermute(value, axis, [(k, partner(k)) for k in range(SIZES[AXES.inde...  5.94 us
    all_to_all x1, waiting for transfers between devices, exchange(): return lax.all_to_all(message, axes, 0, 0, tiled=True)  5.57 us
    ppermute x8, waiting for transfers between devices, swap(): lax.ppermute(value, axis, [(k, partner(k)) for k in range(SIZES[AXES.inde...  3.5 us
    ppermute x2, starting transfers between devices, from_y(): lax.ppermute(value, ('yl', 'yh'), [(place_of(y), place_of((y - step) % 4)...  3.39 us
    ppermute x2, waiting for transfers between devices, from_y(): lax.ppermute(value, ('yl', 'yh'), [(place_of(y), place_of((y - step) % 4)...  2.66 us
  transfers between devices with their start and end apart: 11, of which 8 were waited for; matrix products, arithmetic and copies ran while one was open for 0% of the time, Pallas kernels for 1%

profile of v11, /device:TPU:2, one launch (start us, length us, event | category | flops | bytes accessed | tf_op | source)
XLA Modules:
  0.0 109.3 jit_solution(1860845413406435253)
XLA Ops:
  1.3 1.8 %shard_map.86 = (bf16[1,144,128]{2,1,0:T(8,128)(2,1)S(1)}, bf16[8,144,128]{2,1,0:T(8,128)(2,1)}) custom-call(bf16[2,128,128]{2,1,0:T(8,128)(2,1)} %bitcast.5, bf16[128,128]{1,0:T(8,128)(2,1)} %driver.1, f32[2,128]{1,0:T(2,128)} %bitcast.6, f32[1,128]{1,0:T(1,128)} %bitcast.7, s32[2]{0:T(128)} %rzone.1, s32[1]{0:T(128)S(6)} %copy.12.dzone, s32[16,16]{1,0:T(8,128)} %table.1), custom_call_target="tpu_custom_call" | custom-call | tf_op jit(solution)/shard_map/pallas_call | solution.py:336
  3.1 2.2 %collective-permute-start.2 = (bf16[1,144,128]{2,1,0:T(8,128)(2,1)S(1)}, bf16[1,144,128]{2,1,0:T(8,128)(2,1)S(1)}, u32[]{:S(2)}, u32[]{:S(2)}) collective-permute-start(bf16[1,144,128]{2,1,0:T(8,128)(2,1)S(1)} %get-tuple-element.23), channel_id=1, source_target_pairs={{0,8},{4,12},{8,0},{12,4},{1,9},{5,13},{9,1},{13,5},{2,10},{6,14},... | collective-permute-start | bytes 110600 | tf_op jit(solution)/shard_map/ppermute | solution.py:290
  5.3 1.6 %collective-permute-start.1 = (bf16[1,144,128]{2,1,0:T(8,128)(2,1)S(1)}, bf16[1,144,128]{2,1,0:T(8,128)(2,1)S(1)}, u32[]{:S(2)}, u32[]{:S(2)}) collective-permute-start(bf16[1,144,128]{2,1,0:T(8,128)(2,1)S(1)} %get-tuple-element.23), channel_id=1, source_target_pairs={{0,12},{4,8},{8,4},{12,0},{1,13},{5,9},{9,5},{13,1},{2,14},{6,10},... | collective-permute-start | bytes 110600 | tf_op jit(solution)/shard_map/ppermute | solution.py:290
  6.9 1.0 collective-permute-start
  7.9 8.5 %all-to-all-start = ((bf16[8,144,128]{2,1,0:T(8,128)(2,1)}), bf16[8,144,128]{2,1,0:T(8,128)(2,1)S(1)}, u32[]{:S(2)}, u32[]{:S(2)}) async-start(bf16[8,144,128]{2,1,0:T(8,128)(2,1)} %get-tuple-element.24), calls=%async_computation | async-start | bytes 589824 | tf_op jit(solution)/shard_map/all_to_all | solution.py:286
  16.4 1.7 %collective-permute-start.4 = (bf16[2,144,128]{2,1,0:T(8,128)(2,1)S(1)}, bf16[2,144,128]{2,1,0:T(8,128)(2,1)S(1)}, u32[]{:S(2)}, u32[]{:S(2)}) collective-permute-start(bf16[2,144,128]{2,1,0:T(8,128)(2,1)S(1)} %pad_maximum_fusion.2), channel_id=1, source_target_pairs={{0,16},{16,2},{2,18},{18,0},{1,17},{17,3},{3,19},{19,1},{4,20},{20... | collective-permute-start | bytes 221192 | tf_op jit(solution)/shard_map/ppermute | solution.py:295
  18.0 1.7 %collective-permute-start.3 = (bf16[2,144,128]{2,1,0:T(8,128)(2,1)S(1)}, bf16[2,144,128]{2,1,0:T(8,128)(2,1)S(1)}, u32[]{:S(2)}, u32[]{:S(2)}) collective-permute-start(bf16[2,144,128]{2,1,0:T(8,128)(2,1)S(1)} %pad_maximum_fusion.1), channel_id=1, source_target_pairs={{0,18},{16,0},{2,16},{18,2},{1,19},{17,1},{3,17},{19,3},{4,22},{20... | collective-permute-start | bytes 221192 | tf_op jit(solution)/shard_map/ppermute | solution.py:295
  19.8 2.2 %collective-permute-done.4 = bf16[2,144,128]{2,1,0:T(8,128)(2,1)S(1)} collective-permute-done((bf16[2,144,128]{2,1,0:T(8,128)(2,1)S(1)}, bf16[2,144,128]{2,1,0:T(8,128)(2,1)S(1)}, u32[]{:S(2)}, u32[]{:S(2)}) %collective-permute-start.4) | collective-permute-done | bytes 73760 | tf_op jit(solution)/shard_map/ppermute | solution.py:295
  22.0 0.5 collective-permute-done.3
  22.5 5.6 %all-to-all-done.driver = bf16[8,144,128]{2,1,0:T(8,128)(2,1)S(1)} async-done(((bf16[8,144,128]{2,1,0:T(8,128)(2,1)}), bf16[8,144,128]{2,1,0:T(8,128)(2,1)S(1)}, u32[]{:S(2)}, u32[]{:S(2)}) %all-to-all-start) | async-done | bytes 294944 | tf_op jit(solution)/shard_map/all_to_all | solution.py:286
  28.1 0.8 shard_map.87
  29.0 0.5 collective-permute-start.6
  29.4 0.8 shard_map.88
  30.3 0.2 collective-permute-done.6.far.other_far
  30.5 1.3 %shard_map.89 = (f32[512,1024]{1,0:T(8,128)S(1)}, f32[512,1024]{1,0:T(8,128)S(1)}, f32[16,128]{1,0:T(8,128)S(1)}) custom-call(bf16[4,144,128]{2,1,0:T(8,128)(2,1)S(1)} %collective-permute-done.5.near.other_near, bf16[4,144,128]{2,1,0:T(8,128)(2,1)S(1)} %collective-permute-done.6.far.other_far, bf16[1024,256]{1,0:T(8,128)(2,1)S(1)} %get-tuple-element.28.wide, ...), custom_call_target="tpu_custom_call" | custom-call | tf_op jit(solution)/shard_map/pallas_call | solution.py:328
  31.8 0.4 collective-permute-start.7
  32.2 0.9 collective-permute-done.7
  33.1 14.1 %all_to_all.35.sums = f32[16,16,128]{2,1,0:T(8,128)S(1)} all-to-all(f32[16,16,128]{2,1,0:T(8,128)S(1)} %broadcast_in_dim.6), channel_id=1, replica_groups=mesh['z'=8,'yl'=2,'x'=4,'yh'=2,'c'=2] {'yl','x','yh'}, dimensions={0} | all-to-all | bytes 262144 | tf_op jit(solution)/shard_map/all_to_all | solution.py:286
  47.2 2.0 %shard_map.90 = (f32[8,8,128]{2,1,0:T(8,128)S(1)}, f32[2048,1024]{1,0:T(8,128)S(1)}, f32[16,128]{1,0:T(8,128)S(1)}, f32[32,128]{1,0:T(8,128)S(1)}) custom-call(f32[16,16,128]{2,1,0:T(8,128)S(1)} %all_to_all.35.sums, bf16[4,144,128]{2,1,0:T(8,128)(2,1)S(1)} %constant_dynamic-update-slice_fusion.near.own_near, ...), custom_call_target="tpu_custom_call" | custom-call | tf_op jit(solution)/shard_map/pallas_call | solution.py:356
  49.2 10.4 %all_to_all.36.sums = f32[8,8,128]{2,1,0:T(8,128)S(1)} all-to-all(f32[8,8,128]{2,1,0:T(8,128)S(1)} %get-tuple-element.36), channel_id=1, replica_groups=mesh['z'=8,'yl'=2,'x'=4,'yh'=2,'c'=2] {'z'}, dimensions={0} | all-to-all | bytes 65536 | tf_op jit(solution)/shard_map/all_to_all | solution.py:286
  59.6 0.7 shard_map.91
  60.3 0.1 collective-permute-start.8
  60.4 1.2 %collective-permute-done.8 = f32[16,128]{1,0:T(8,128)S(1)} collective-permute-done((f32[16,128]{1,0:T(8,128)S(1)}, f32[16,128]{1,0:T(8,128)S(1)}, u32[]{:S(2)}, u32[]{:S(2)}) %collective-permute-start.8) | collective-permute-done | bytes 8224 | tf_op jit(solution)/shard_map/ppermute | solution.py:290
  61.6 11.2 %all_to_all.37.sums = f32[16,16,128]{2,1,0:T(8,128)S(1)} all-to-all(f32[16,16,128]{2,1,0:T(8,128)S(1)} %broadcast_in_dim.7), channel_id=1, replica_groups=mesh['z'=8,'yl'=2,'x'=4,'yh'=2,'c'=2] {'yl','x','yh'}, dimensions={0} | all-to-all | bytes 262144 | tf_op jit(solution)/shard_map/all_to_all | solution.py:286
  72.8 1.0 shard_map.92
  73.8 10.4 %all_to_all.38.sums = f32[8,8,128]{2,1,0:T(8,128)S(1)} all-to-all(f32[8,8,128]{2,1,0:T(8,128)S(1)} %shard_map.92), channel_id=1, replica_groups=mesh['z'=8,'yl'=2,'x'=4,'yh'=2,'c'=2] {'z'}, dimensions={0} | all-to-all | bytes 65536 | tf_op jit(solution)/shard_map/all_to_all | solution.py:286
  84.2 0.6 shard_map.93
  84.9 1.2 %collective-permute-done.9 = f32[16,128]{1,0:T(8,128)S(1)} collective-permute-done((f32[16,128]{1,0:T(8,128)S(1)}, f32[16,128]{1,0:T(8,128)S(1)}, u32[]{:S(2)}, u32[]{:S(2)}) %collective-permute-start.9) | collective-permute-done | bytes 8224 | tf_op jit(solution)/shard_map/ppermute | solution.py:290
  86.1 11.2 %all_to_all.39.sums.rider_sums = f32[16,16,128]{2,1,0:T(8,128)S(1)} all-to-all(f32[16,16,128]{2,1,0:T(8,128)S(1)} %broadcast_in_dim.8), channel_id=1, replica_groups=mesh['z'=8,'yl'=2,'x'=4,'yh'=2,'c'=2] {'yl','x','yh'}, dimensions={0} | all-to-all | bytes 262144 | tf_op jit(solution)/shard_map/all_to_all | solution.py:286
  97.3 1.0 shard_map.94
  98.3 10.4 %all_to_all.40.sums = f32[8,8,128]{2,1,0:T(8,128)S(1)} all-to-all(f32[8,8,128]{2,1,0:T(8,128)S(1)} %shard_map.94), channel_id=1, replica_groups=mesh['z'=8,'yl'=2,'x'=4,'yh'=2,'c'=2] {'z'}, dimensions={0} | all-to-all | bytes 65536 | tf_op jit(solution)/shard_map/all_to_all | solution.py:286
  108.7 0.6 shard_map.95
  (19 shorter events, 0.4 us)
Async XLA Ops:
  3.1 13.3 %collective-permute-start.2 = (bf16[1,144,128]{2,1,0:T(8,128)(2,1)S(1)}, bf16[1,144,128]{2,1,0:T(8,128)(2,1)S(1)}, u32[]{:S(2)}, u32[]{:S(2)}) collective-permute-start(bf16[1,144,128]{2,1,0:T(8,128)(2,1)S(1)} %get-tuple-element.23), channel_id=1, source_target_pairs={{0,8},{4,12},{8,0},{12,4},{1,9},{5,13},{9,1},{13,5},{2,10},{6,14},... | collective-permute-start | bytes 110600 | tf_op jit(solution)/shard_map/ppermute | solution.py:290
  5.3 11.1 %collective-permute-start.1 = (bf16[1,144,128]{2,1,0:T(8,128)(2,1)S(1)}, bf16[1,144,128]{2,1,0:T(8,128)(2,1)S(1)}, u32[]{:S(2)}, u32[]{:S(2)}) collective-permute-start(bf16[1,144,128]{2,1,0:T(8,128)(2,1)S(1)} %get-tuple-element.23), channel_id=1, source_target_pairs={{0,12},{4,8},{8,4},{12,0},{1,13},{5,9},{9,5},{13,1},{2,14},{6,10},... | collective-permute-start | bytes 110600 | tf_op jit(solution)/shard_map/ppermute | solution.py:290
  6.9 11.1 %collective-permute-start = (bf16[1,144,128]{2,1,0:T(8,128)(2,1)S(1)}, bf16[1,144,128]{2,1,0:T(8,128)(2,1)S(1)}, u32[]{:S(2)}, u32[]{:S(2)}) collective-permute-start(bf16[1,144,128]{2,1,0:T(8,128)(2,1)S(1)} %get-tuple-element.23), channel_id=1, source_target_pairs={{0,4},{4,0},{8,12},{12,8},{1,5},{5,1},{9,13},{13,9},{2,6},{6,2},{1... | collective-permute-start | bytes 110600 | tf_op jit(solution)/shard_map/ppermute | solution.py:290
  7.9 20.2 %all-to-all-start = ((bf16[8,144,128]{2,1,0:T(8,128)(2,1)}), bf16[8,144,128]{2,1,0:T(8,128)(2,1)S(1)}, u32[]{:S(2)}, u32[]{:S(2)}) async-start(bf16[8,144,128]{2,1,0:T(8,128)(2,1)} %get-tuple-element.24), calls=%async_computation | async-start | bytes 589824 | tf_op jit(solution)/shard_map/all_to_all | solution.py:286
  16.4 5.6 %collective-permute-start.4 = (bf16[2,144,128]{2,1,0:T(8,128)(2,1)S(1)}, bf16[2,144,128]{2,1,0:T(8,128)(2,1)S(1)}, u32[]{:S(2)}, u32[]{:S(2)}) collective-permute-start(bf16[2,144,128]{2,1,0:T(8,128)(2,1)S(1)} %pad_maximum_fusion.2), channel_id=1, source_target_pairs={{0,16},{16,2},{2,18},{18,0},{1,17},{17,3},{3,19},{19,1},{4,20},{20... | collective-permute-start | bytes 221192 | tf_op jit(solution)/shard_map/ppermute | solution.py:295
  18.0 4.4 %collective-permute-start.3 = (bf16[2,144,128]{2,1,0:T(8,128)(2,1)S(1)}, bf16[2,144,128]{2,1,0:T(8,128)(2,1)S(1)}, u32[]{:S(2)}, u32[]{:S(2)}) collective-permute-start(bf16[2,144,128]{2,1,0:T(8,128)(2,1)S(1)} %pad_maximum_fusion.1), channel_id=1, source_target_pairs={{0,18},{16,0},{2,16},{18,2},{1,19},{17,1},{3,17},{19,3},{4,22},{20... | collective-permute-start | bytes 221192 | tf_op jit(solution)/shard_map/ppermute | solution.py:295
  28.9 1.5 %collective-permute-start.5 = (bf16[4,144,128]{2,1,0:T(8,128)(2,1)S(1)}, bf16[4,144,128]{2,1,0:T(8,128)(2,1)S(1)}, u32[]{:S(2)}, u32[]{:S(2)}) collective-permute-start(bf16[4,144,128]{2,1,0:T(8,128)(2,1)S(1)} %constant_dynamic-update-slice_fusion.near.own_near), channel_id=1, source_target_pairs={{0,1},{1,0},{2,3},{3,2},{4,5},{5,4},{6,7},{7,6},{8,9},{9,8},{10,11... | collective-permute-start | bytes 442376 | tf_op jit(solution)/shard_map/ppermute | solution.py:290
  29.0 1.6 %collective-permute-start.6 = (bf16[4,144,128]{2,1,0:T(8,128)(2,1)S(1)}, bf16[4,144,128]{2,1,0:T(8,128)(2,1)S(1)}, u32[]{:S(2)}, u32[]{:S(2)}) collective-permute-start(bf16[4,144,128]{2,1,0:T(8,128)(2,1)S(1)} %pad_maximum_fusion.far.own_far), channel_id=1, source_target_pairs={{0,1},{1,0},{2,3},{3,2},{4,5},{5,4},{6,7},{7,6},{8,9},{9,8},{10,11... | collective-permute-start | bytes 442376 | tf_op jit(solution)/shard_map/ppermute | solution.py:290
  31.8 1.3 %collective-permute-start.7 = (f32[16,128]{1,0:T(8,128)S(1)}, f32[16,128]{1,0:T(8,128)S(1)}, u32[]{:S(2)}, u32[]{:S(2)}) collective-permute-start(f32[16,128]{1,0:T(8,128)S(1)} %get-tuple-element.31), channel_id=1, source_target_pairs={{0,1},{1,0},{2,3},{3,2},{4,5},{5,4},{6,7},{7,6},{8,9},{9,8},{10,11... | collective-permute-start | bytes 24584 | tf_op jit(solution)/shard_map/ppermute | solution.py:290
  60.3 1.3 %collective-permute-start.8 = (f32[16,128]{1,0:T(8,128)S(1)}, f32[16,128]{1,0:T(8,128)S(1)}, u32[]{:S(2)}, u32[]{:S(2)}) collective-permute-start(f32[16,128]{1,0:T(8,128)S(1)} %get-tuple-element.39), channel_id=1, source_target_pairs={{0,1},{1,0},{2,3},{3,2},{4,5},{5,4},{6,7},{7,6},{8,9},{9,8},{10,11... | collective-permute-start | bytes 24584 | tf_op jit(solution)/shard_map/ppermute | solution.py:290
  84.8 1.3 %collective-permute-start.9 = (f32[16,128]{1,0:T(8,128)S(1)}, f32[16,128]{1,0:T(8,128)S(1)}, u32[]{:S(2)}, u32[]{:S(2)}) collective-permute-start(f32[16,128]{1,0:T(8,128)S(1)} %shard_map.93), channel_id=1, source_target_pairs={{0,1},{1,0},{2,3},{3,2},{4,5},{5,4},{6,7},{7,6},{8,9},{9,8},{10,11... | collective-permute-start | bytes 24584 | tf_op jit(solution)/shard_map/ppermute | solution.py:290

commit v12 on v11

--- a/solution.py
+++ b/solution.py
@@ -29,13 +29,12 @@
 FAR = pl.BlockSpec(memory_space=pltpu.HBM)
 
 
-def call(body, outs, ins, scratch=(), limit=20, cost=None):
+def call(body, outs, ins, scratch=(), limit=20):
     return pl.pallas_call(
         body,
         out_shape=outs,
         in_specs=ins,
         out_specs=[VM] * len(outs),
-        cost_estimate=cost,
         scratch_shapes=list(scratch),
         compiler_params=pltpu.CompilerParams(vmem_limit_bytes=limit * 2**20),
     )
@@ -155,20 +154,11 @@
         rows[first + k : first + k + 1, :] = jnp.log(mass) - least
 
 
-def rider_near_body(near, driver, cost, rows, wide, left):
+def rider_first_body(own_near, own_far, other_near, other_far, driver, *rest):
+    *costs, out, rows, wide, left = rest
     widen([driver[z] for z in range(DB)], wide)
-    rider_rows(near, wide, cost, rows, 0, left)
-
-
-def rider_far_body(far, wide, cost, rows, left):
-    rider_rows(far, wide, cost, rows, 0, left)
-
-
-def rider_other_body(near, far, wide, own_near, own_far, near_cost, far_cost, out, rows, left):
-    rows[0:4] = own_near[...]
-    rows[4:8] = own_far[...]
-    rider_rows(near, wide, near_cost, rows, 8, left)
-    rider_rows(far, wide, far_cost, rows, 12, left)
+    for k, riders in enumerate((own_near, own_far, other_near, other_far)):
+        rider_rows(riders, wide, costs[k], rows, 4 * k, left)
     for r in range(RB):
         out[pl.ds(block_of(r), 1), :] = rows[r : r + 1]
 
@@ -307,29 +297,18 @@
     return exchange(jnp.broadcast_to(value[None], (PEERS, RB, B)), PLANE)
 
 
-def rider_first(message, drivers):
+def gather(message, drivers):
+    drivers = exchange(drivers, "z")
     beside, across, behind = (
         swap(message, "x", partner)
         for partner in (lambda k: k ^ 1, lambda k: 3 - k, lambda k: k ^ 2)
     )
     two = jnp.concatenate([message, beside], axis=0)
-    drivers = exchange(drivers, "z")
     mirror = jnp.concatenate([across, behind], axis=0)
     near = jnp.concatenate([two, mirror], axis=0)
     far = jnp.concatenate([from_y(two, 1), from_y(mirror, -1)], axis=0)
-    quarter = pl.CostEstimate(flops=2**30, transcendentals=2**19, bytes_accessed=2**21)
-    cost, rows, left = f32(4 * B, DB * B), f32(4, B), pltpu.VMEM((4 * B, 2 * B), BF16)
-    own_near_cost, near_rows, wide = call(
-        rider_near_body, [cost, rows, bf16(DB * B, 2 * B)], [VM] * 2, [left], cost=quarter
-    )(near, drivers)
-    near, far, near_rows = lax.optimization_barrier((near, far, near_rows))
     other_near, other_far = (swap(value, "c", lambda k: 1 - k) for value in (near, far))
-    own_far_cost, far_rows = call(rider_far_body, [cost, rows], [VM] * 2, [left], cost=quarter)(far, wide)
-    other_near_cost, other_far_cost, sums = call(
-        rider_other_body, [cost, cost, f32(RB, B)], [VM] * 5, [pltpu.VMEM((RB, B), F32), left]
-    )(other_near, other_far, wide, near_rows, far_rows)
-    costs = own_near_cost, own_far_cost, other_near_cost, other_far_cost
-    return sums, (near, far, other_near, other_far, drivers, *costs)
+    return near, far, other_near, other_far, drivers
 
 
 def per_device(rider_emb, driver_emb, log_a, log_b, rider_zone, driver_zone, zone_table):
@@ -350,7 +329,17 @@
         rider_emb.reshape(2, B, B), driver_emb, log_a.reshape(2, B), log_b.reshape(1, B),
         rider_zone, driver_zone, zone_table,
     )
-    sums, gathered = rider_first(rider_msg, driver_msg)
+    messages = gather(rider_msg, driver_msg)
+    *costs, sums = call(
+        rider_first_body,
+        [f32(4 * B, DB * B)] * 4 + [f32(RB, B)],
+        [VM] * 5,
+        [
+            pltpu.VMEM((RB, B), F32),
+            pltpu.VMEM((DB * B, 2 * B), BF16),
+            pltpu.VMEM((4 * B, 2 * B), BF16),
+        ],
+    )(*messages)
     sums = close(sums, log_add)
     columns = pltpu.VMEM((RB * B, B), F32)
     sums, kernel, peaks, pots = call(
@@ -358,7 +347,7 @@
         [f32(DB, DB, B), f32(RB * B, DB * B), f32(2 * DB, B), f32(2 * RB, B)],
         [VM] * 10,
         [columns],
-    )(sums, *gathered)
+    )(sums, *messages, *costs)
     sums = exchange(sums, "z")
     columns = [columns, pltpu.VMEM((RB, B), F32)]
     sums, state = call(rider_second_body, [f32(RB, B), f32(3 * DB, B)], [VM] * 3)(

time: 110 us -> 109 us (level)
    all_to_all x1, waiting for transfers between devices: 5.57 us -> 4.1 us  [exchange(): return lax.all_to_all(message, axes, 0, 0, tiled=True)]
    ppermute x8, waiting for transfers between devices: 3.5 us -> 4.83 us  [swap(): lax.ppermute(value, axis, [(k, partner(k)) for k in range(SIZES[AXES.inde...]
    pallas_call x3 -> x1, Pallas kernels: 2.82 us -> 2.25 us  [per_device(): call(rider_first_body, [f32(4 * B, DB * B)] * 4 + [f32(RB, B)], [VM] * 5,...]
  transfers between devices with their start and end apart: 11 -> 11, of which waited for: 8 -> 6; matrix products, arithmetic and copies ran while one was open for 0% -> 0% of each run, Pallas kernels for 1% -> 0%
where the time goes in v12:
time: 109 us; the launch traced here: 108 us
  blocking collectives  68 us (62%)
  starting transfers between devices  17.1 us (16%)
  waiting for transfers between devices  11.5 us (11%)
  Pallas kernels  9.93 us (9%)
  between operations  1.42 us (1%)
    all_to_all x6, blocking collectives, exchange(): return lax.all_to_all(message, axes, 0, 0, tiled=True)  68 us
    all_to_all x1, starting transfers between devices, exchange(): return lax.all_to_all(message, axes, 0, 0, tiled=True)  8.47 us
    ppermute x8, starting transfers between devices, swap(): lax.ppermute(value, axis, [(k, partner(k)) for k in range(SIZES[AXES.inde...  5.25 us
    ppermute x8, waiting for transfers between devices, swap(): lax.ppermute(value, axis, [(k, partner(k)) for k in range(SIZES[AXES.inde...  4.83 us
    all_to_all x1, waiting for transfers between devices, exchange(): return lax.all_to_all(message, axes, 0, 0, tiled=True)  4.1 us
    ppermute x2, starting transfers between devices, from_y(): lax.ppermute(value, ('yl', 'yh'), [(place_of(y), place_of((y - step) % 4)...  3.39 us
    ppermute x2, waiting for transfers between devices, from_y(): lax.ppermute(value, ('yl', 'yh'), [(place_of(y), place_of((y - step) % 4)...  2.56 us
    pallas_call x1, Pallas kernels, per_device(): call(rider_first_body, [f32(4 * B, DB * B)] * 4 + [f32(RB, B)], [VM] * 5,...  2.25 us
  transfers between devices with their start and end apart: 11, of which 6 were waited for; matrix products, arithmetic and copies ran while one was open for 0% of the time, Pallas kernels for 0%

profile of v12, /device:TPU:2, one launch (start us, length us, event | category | flops | bytes accessed | tf_op | source)
XLA Modules:
  0.0 108.1 jit_solution(17693990685976824388)
XLA Ops:
  1.3 1.8 %shard_map.86 = (bf16[1,144,128]{2,1,0:T(8,128)(2,1)S(1)}, bf16[8,144,128]{2,1,0:T(8,128)(2,1)}) custom-call(bf16[2,128,128]{2,1,0:T(8,128)(2,1)} %bitcast.5, bf16[128,128]{1,0:T(8,128)(2,1)} %driver.1, f32[2,128]{1,0:T(2,128)} %bitcast.6, f32[1,128]{1,0:T(1,128)} %bitcast.7, s32[2]{0:T(128)} %rzone.1, s32[1]{0:T(128)S(6)} %copy.13.dzone, s32[16,16]{1,0:T(8,128)} %table.1), custom_call_target="tpu_custom_call" | custom-call | tf_op jit(solution)/shard_map/pallas_call | solution.py:315
  3.1 2.2 %collective-permute-start.2 = (bf16[1,144,128]{2,1,0:T(8,128)(2,1)S(1)}, bf16[1,144,128]{2,1,0:T(8,128)(2,1)S(1)}, u32[]{:S(2)}, u32[]{:S(2)}) collective-permute-start(bf16[1,144,128]{2,1,0:T(8,128)(2,1)S(1)} %get-tuple-element.17), channel_id=1, source_target_pairs={{0,8},{4,12},{8,0},{12,4},{1,9},{5,13},{9,1},{13,5},{2,10},{6,14},... | collective-permute-start | bytes 110600 | tf_op jit(solution)/shard_map/ppermute | solution.py:280
  5.3 1.6 %collective-permute-start.1 = (bf16[1,144,128]{2,1,0:T(8,128)(2,1)S(1)}, bf16[1,144,128]{2,1,0:T(8,128)(2,1)S(1)}, u32[]{:S(2)}, u32[]{:S(2)}) collective-permute-start(bf16[1,144,128]{2,1,0:T(8,128)(2,1)S(1)} %get-tuple-element.17), channel_id=1, source_target_pairs={{0,12},{4,8},{8,4},{12,0},{1,13},{5,9},{9,5},{13,1},{2,14},{6,10},... | collective-permute-start | bytes 110600 | tf_op jit(solution)/shard_map/ppermute | solution.py:280
  6.9 1.0 collective-permute-start
  7.9 8.5 %all-to-all-start = ((bf16[8,144,128]{2,1,0:T(8,128)(2,1)}), bf16[8,144,128]{2,1,0:T(8,128)(2,1)S(1)}, u32[]{:S(2)}, u32[]{:S(2)}) async-start(bf16[8,144,128]{2,1,0:T(8,128)(2,1)} %get-tuple-element.18), calls=%async_computation | async-start | bytes 589824 | tf_op jit(solution)/shard_map/all_to_all | solution.py:276
  16.3 0.0 collective-permute-done.2
  16.4 1.7 %collective-permute-start.4 = (bf16[2,144,128]{2,1,0:T(8,128)(2,1)S(1)}, bf16[2,144,128]{2,1,0:T(8,128)(2,1)S(1)}, u32[]{:S(2)}, u32[]{:S(2)}) collective-permute-start(bf16[2,144,128]{2,1,0:T(8,128)(2,1)S(1)} %pad_maximum_fusion.1), channel_id=1, source_target_pairs={{0,16},{16,2},{2,18},{18,0},{1,17},{17,3},{3,19},{19,1},{4,20},{20... | collective-permute-start | bytes 221192 | tf_op jit(solution)/shard_map/ppermute | solution.py:285
  18.0 1.7 %collective-permute-start.3 = (bf16[2,144,128]{2,1,0:T(8,128)(2,1)S(1)}, bf16[2,144,128]{2,1,0:T(8,128)(2,1)S(1)}, u32[]{:S(2)}, u32[]{:S(2)}) collective-permute-start(bf16[2,144,128]{2,1,0:T(8,128)(2,1)S(1)} %pad_maximum_fusion), channel_id=1, source_target_pairs={{0,18},{16,0},{2,16},{18,2},{1,19},{17,1},{3,17},{19,3},{4,22},{20... | collective-permute-start | bytes 221192 | tf_op jit(solution)/shard_map/ppermute | solution.py:285
  19.8 0.1 collective-permute-start.5
  19.9 2.6 %collective-permute-done.3 = bf16[2,144,128]{2,1,0:T(8,128)(2,1)S(1)} collective-permute-done((bf16[2,144,128]{2,1,0:T(8,128)(2,1)S(1)}, bf16[2,144,128]{2,1,0:T(8,128)(2,1)S(1)}, u32[]{:S(2)}, u32[]{:S(2)}) %collective-permute-start.3) | collective-permute-done | bytes 73760 | tf_op jit(solution)/shard_map/ppermute | solution.py:285
  22.5 0.1 collective-permute-start.6
  22.6 1.3 %collective-permute-done.6.other_far = bf16[4,144,128]{2,1,0:T(8,128)(2,1)S(1)} collective-permute-done((bf16[4,144,128]{2,1,0:T(8,128)(2,1)S(1)}, bf16[4,144,128]{2,1,0:T(8,128)(2,1)S(1)}, u32[]{:S(2)}, u32[]{:S(2)}) %collective-permute-start.6) | collective-permute-done | bytes 147488 | tf_op jit(solution)/shard_map/ppermute | solution.py:280
  24.0 4.1 %all-to-all-done.driver = bf16[8,144,128]{2,1,0:T(8,128)(2,1)S(1)} async-done(((bf16[8,144,128]{2,1,0:T(8,128)(2,1)}), bf16[8,144,128]{2,1,0:T(8,128)(2,1)S(1)}, u32[]{:S(2)}, u32[]{:S(2)}) %all-to-all-start) | async-done | bytes 294944 | tf_op jit(solution)/shard_map/all_to_all | solution.py:276
  28.1 2.3 %shard_map.87 = (f32[512,1024]{1,0:T(8,128)S(1)}, f32[512,1024]{1,0:T(8,128)S(1)}, f32[512,1024]{1,0:T(8,128)S(1)}, f32[512,1024]{1,0:T(8,128)S(1)}, f32[16,128]{1,0:T(8,128)S(1)}) custom-call(bf16[4,144,128]{2,1,0:T(8,128)(2,1)S(1)} %constant_dynamic-update-slice_fusion.own_near, bf16[4,144,128]{2,1,0:T(8,128)(2,1)S(1)} %constant_dynamic-update-slice_fusion.4.own_far, ...), custom_call_target="tpu_custom_call" | custom-call | tf_op jit(solution)/shard_map/pallas_call | solution.py:333
  30.3 0.1 collective-permute-start.7
  30.4 1.2 %collective-permute-done.7 = f32[16,128]{1,0:T(8,128)S(1)} collective-permute-done((f32[16,128]{1,0:T(8,128)S(1)}, f32[16,128]{1,0:T(8,128)S(1)}, u32[]{:S(2)}, u32[]{:S(2)}) %collective-permute-start.7) | collective-permute-done | bytes 8224 | tf_op jit(solution)/shard_map/ppermute | solution.py:280
  31.6 14.1 %all_to_all.35.sums = f32[16,16,128]{2,1,0:T(8,128)S(1)} all-to-all(f32[16,16,128]{2,1,0:T(8,128)S(1)} %broadcast_in_dim.6), channel_id=1, replica_groups=mesh['z'=8,'yl'=2,'x'=4,'yh'=2,'c'=2] {'yl','x','yh'}, dimensions={0} | all-to-all | bytes 262144 | tf_op jit(solution)/shard_map/all_to_all | solution.py:276
  45.7 2.0 %shard_map.88 = (f32[8,8,128]{2,1,0:T(8,128)S(1)}, f32[2048,1024]{1,0:T(8,128)S(1)}, f32[16,128]{1,0:T(8,128)S(1)}, f32[32,128]{1,0:T(8,128)S(1)}) custom-call(f32[16,16,128]{2,1,0:T(8,128)S(1)} %all_to_all.35.sums, bf16[4,144,128]{2,1,0:T(8,128)(2,1)S(1)} %constant_dynamic-update-slice_fusion.own_near, ...), custom_call_target="tpu_custom_call" | custom-call | tf_op jit(solution)/shard_map/pallas_call | solution.py:345
  47.7 10.6 %all_to_all.36.sums = f32[8,8,128]{2,1,0:T(8,128)S(1)} all-to-all(f32[8,8,128]{2,1,0:T(8,128)S(1)} %get-tuple-element.24), channel_id=1, replica_groups=mesh['z'=8,'yl'=2,'x'=4,'yh'=2,'c'=2] {'z'}, dimensions={0} | all-to-all | bytes 65536 | tf_op jit(solution)/shard_map/all_to_all | solution.py:276
  58.4 0.7 shard_map.89
  59.0 0.1 collective-permute-start.8
  59.1 1.2 %collective-permute-done.8 = f32[16,128]{1,0:T(8,128)S(1)} collective-permute-done((f32[16,128]{1,0:T(8,128)S(1)}, f32[16,128]{1,0:T(8,128)S(1)}, u32[]{:S(2)}, u32[]{:S(2)}) %collective-permute-start.8) | collective-permute-done | bytes 8224 | tf_op jit(solution)/shard_map/ppermute | solution.py:280
  60.3 11.2 %all_to_all.37.sums = f32[16,16,128]{2,1,0:T(8,128)S(1)} all-to-all(f32[16,16,128]{2,1,0:T(8,128)S(1)} %broadcast_in_dim.7), channel_id=1, replica_groups=mesh['z'=8,'yl'=2,'x'=4,'yh'=2,'c'=2] {'yl','x','yh'}, dimensions={0} | all-to-all | bytes 262144 | tf_op jit(solution)/shard_map/all_to_all | solution.py:276
  71.5 1.0 shard_map.90
  72.5 10.4 %all_to_all.38.sums = f32[8,8,128]{2,1,0:T(8,128)S(1)} all-to-all(f32[8,8,128]{2,1,0:T(8,128)S(1)} %shard_map.90), channel_id=1, replica_groups=mesh['z'=8,'yl'=2,'x'=4,'yh'=2,'c'=2] {'z'}, dimensions={0} | all-to-all | bytes 65536 | tf_op jit(solution)/shard_map/all_to_all | solution.py:276
  82.9 0.6 shard_map.91
  83.6 0.1 collective-permute-start.9
  83.7 1.2 %collective-permute-done.9 = f32[16,128]{1,0:T(8,128)S(1)} collective-permute-done((f32[16,128]{1,0:T(8,128)S(1)}, f32[16,128]{1,0:T(8,128)S(1)}, u32[]{:S(2)}, u32[]{:S(2)}) %collective-permute-start.9) | collective-permute-done | bytes 8224 | tf_op jit(solution)/shard_map/ppermute | solution.py:280
  84.8 11.2 %all_to_all.39.sums.rider_sums = f32[16,16,128]{2,1,0:T(8,128)S(1)} all-to-all(f32[16,16,128]{2,1,0:T(8,128)S(1)} %broadcast_in_dim.8), channel_id=1, replica_groups=mesh['z'=8,'yl'=2,'x'=4,'yh'=2,'c'=2] {'yl','x','yh'}, dimensions={0} | all-to-all | bytes 262144 | tf_op jit(solution)/shard_map/all_to_all | solution.py:276
  96.1 1.0 shard_map.92
  97.1 10.4 %all_to_all.40.sums = f32[8,8,128]{2,1,0:T(8,128)S(1)} all-to-all(f32[8,8,128]{2,1,0:T(8,128)S(1)} %shard_map.92), channel_id=1, replica_groups=mesh['z'=8,'yl'=2,'x'=4,'yh'=2,'c'=2] {'z'}, dimensions={0} | all-to-all | bytes 65536 | tf_op jit(solution)/shard_map/all_to_all | solution.py:276
  107.5 0.6 shard_map.93
  (18 shorter events, 0.1 us)
Async XLA Ops:
  3.1 13.3 %collective-permute-start.2 = (bf16[1,144,128]{2,1,0:T(8,128)(2,1)S(1)}, bf16[1,144,128]{2,1,0:T(8,128)(2,1)S(1)}, u32[]{:S(2)}, u32[]{:S(2)}) collective-permute-start(bf16[1,144,128]{2,1,0:T(8,128)(2,1)S(1)} %get-tuple-element.17), channel_id=1, source_target_pairs={{0,8},{4,12},{8,0},{12,4},{1,9},{5,13},{9,1},{13,5},{2,10},{6,14},... | collective-permute-start | bytes 110600 | tf_op jit(solution)/shard_map/ppermute | solution.py:280
  5.3 11.1 %collective-permute-start.1 = (bf16[1,144,128]{2,1,0:T(8,128)(2,1)S(1)}, bf16[1,144,128]{2,1,0:T(8,128)(2,1)S(1)}, u32[]{:S(2)}, u32[]{:S(2)}) collective-permute-start(bf16[1,144,128]{2,1,0:T(8,128)(2,1)S(1)} %get-tuple-element.17), channel_id=1, source_target_pairs={{0,12},{4,8},{8,4},{12,0},{1,13},{5,9},{9,5},{13,1},{2,14},{6,10},... | collective-permute-start | bytes 110600 | tf_op jit(solution)/shard_map/ppermute | solution.py:280
  6.9 11.1 %collective-permute-start = (bf16[1,144,128]{2,1,0:T(8,128)(2,1)S(1)}, bf16[1,144,128]{2,1,0:T(8,128)(2,1)S(1)}, u32[]{:S(2)}, u32[]{:S(2)}) collective-permute-start(bf16[1,144,128]{2,1,0:T(8,128)(2,1)S(1)} %get-tuple-element.17), channel_id=1, source_target_pairs={{0,4},{4,0},{8,12},{12,8},{1,5},{5,1},{9,13},{13,9},{2,6},{6,2},{1... | collective-permute-start | bytes 110600 | tf_op jit(solution)/shard_map/ppermute | solution.py:280
  7.9 20.2 %all-to-all-start = ((bf16[8,144,128]{2,1,0:T(8,128)(2,1)}), bf16[8,144,128]{2,1,0:T(8,128)(2,1)S(1)}, u32[]{:S(2)}, u32[]{:S(2)}) async-start(bf16[8,144,128]{2,1,0:T(8,128)(2,1)} %get-tuple-element.18), calls=%async_computation | async-start | bytes 589824 | tf_op jit(solution)/shard_map/all_to_all | solution.py:276
  16.4 6.1 %collective-permute-start.4 = (bf16[2,144,128]{2,1,0:T(8,128)(2,1)S(1)}, bf16[2,144,128]{2,1,0:T(8,128)(2,1)S(1)}, u32[]{:S(2)}, u32[]{:S(2)}) collective-permute-start(bf16[2,144,128]{2,1,0:T(8,128)(2,1)S(1)} %pad_maximum_fusion.1), channel_id=1, source_target_pairs={{0,16},{16,2},{2,18},{18,0},{1,17},{17,3},{3,19},{19,1},{4,20},{20... | collective-permute-start | bytes 221192 | tf_op jit(solution)/shard_map/ppermute | solution.py:285
  18.0 4.4 %collective-permute-start.3 = (bf16[2,144,128]{2,1,0:T(8,128)(2,1)S(1)}, bf16[2,144,128]{2,1,0:T(8,128)(2,1)S(1)}, u32[]{:S(2)}, u32[]{:S(2)}) collective-permute-start(bf16[2,144,128]{2,1,0:T(8,128)(2,1)S(1)} %pad_maximum_fusion), channel_id=1, source_target_pairs={{0,18},{16,0},{2,16},{18,2},{1,19},{17,1},{3,17},{19,3},{4,22},{20... | collective-permute-start | bytes 221192 | tf_op jit(solution)/shard_map/ppermute | solution.py:285
  19.8 2.8 %collective-permute-start.5 = (bf16[4,144,128]{2,1,0:T(8,128)(2,1)S(1)}, bf16[4,144,128]{2,1,0:T(8,128)(2,1)S(1)}, u32[]{:S(2)}, u32[]{:S(2)}) collective-permute-start(bf16[4,144,128]{2,1,0:T(8,128)(2,1)S(1)} %constant_dynamic-update-slice_fusion.own_near), channel_id=1, source_target_pairs={{0,1},{1,0},{2,3},{3,2},{4,5},{5,4},{6,7},{7,6},{8,9},{9,8},{10,11... | collective-permute-start | bytes 442376 | tf_op jit(solution)/shard_map/ppermute | solution.py:280
  22.5 1.5 %collective-permute-start.6 = (bf16[4,144,128]{2,1,0:T(8,128)(2,1)S(1)}, bf16[4,144,128]{2,1,0:T(8,128)(2,1)S(1)}, u32[]{:S(2)}, u32[]{:S(2)}) collective-permute-start(bf16[4,144,128]{2,1,0:T(8,128)(2,1)S(1)} %constant_dynamic-update-slice_fusion.4.own_far), channel_id=1, source_target_pairs={{0,1},{1,0},{2,3},{3,2},{4,5},{5,4},{6,7},{7,6},{8,9},{9,8},{10,11... | collective-permute-start | bytes 442376 | tf_op jit(solution)/shard_map/ppermute | solution.py:280
  30.3 1.3 %collective-permute-start.7 = (f32[16,128]{1,0:T(8,128)S(1)}, f32[16,128]{1,0:T(8,128)S(1)}, u32[]{:S(2)}, u32[]{:S(2)}) collective-permute-start(f32[16,128]{1,0:T(8,128)S(1)} %get-tuple-element.19), channel_id=1, source_target_pairs={{0,1},{1,0},{2,3},{3,2},{4,5},{5,4},{6,7},{7,6},{8,9},{9,8},{10,11... | collective-permute-start | bytes 24584 | tf_op jit(solution)/shard_map/ppermute | solution.py:280
  59.0 1.3 %collective-permute-start.8 = (f32[16,128]{1,0:T(8,128)S(1)}, f32[16,128]{1,0:T(8,128)S(1)}, u32[]{:S(2)}, u32[]{:S(2)}) collective-permute-start(f32[16,128]{1,0:T(8,128)S(1)} %get-tuple-element.27), channel_id=1, source_target_pairs={{0,1},{1,0},{2,3},{3,2},{4,5},{5,4},{6,7},{7,6},{8,9},{9,8},{10,11... | collective-permute-start | bytes 24584 | tf_op jit(solution)/shard_map/ppermute | solution.py:280
  83.6 1.3 %collective-permute-start.9 = (f32[16,128]{1,0:T(8,128)S(1)}, f32[16,128]{1,0:T(8,128)S(1)}, u32[]{:S(2)}, u32[]{:S(2)}) collective-permute-start(f32[16,128]{1,0:T(8,128)S(1)} %shard_map.91), channel_id=1, source_target_pairs={{0,1},{1,0},{2,3},{3,2},{4,5},{5,4},{6,7},{7,6},{8,9},{9,8},{10,11... | collective-permute-start | bytes 24584 | tf_op jit(solution)/shard_map/ppermute | solution.py:280

commit v13 on v12

--- a/solution.py
+++ b/solution.py
@@ -154,13 +154,18 @@
         rows[first + k : first + k + 1, :] = jnp.log(mass) - least
 
 
-def rider_first_body(own_near, own_far, other_near, other_far, driver, *rest):
-    *costs, out, rows, wide, left = rest
+def rider_early_body(own_near, own_far, other_near, driver, *rest):
+    *costs, rows, wide, left = rest
     widen([driver[z] for z in range(DB)], wide)
-    for k, riders in enumerate((own_near, own_far, other_near, other_far)):
+    for k, riders in enumerate((own_near, own_far, other_near)):
         rider_rows(riders, wide, costs[k], rows, 4 * k, left)
-    for r in range(RB):
-        out[pl.ds(block_of(r), 1), :] = rows[r : r + 1]
+
+
+def rider_late_body(other_far, wide, early, cost, out, rows, left):
+    rider_rows(other_far, wide, cost, rows, 0, left)
+    for r in range(RB):
+        row = early[r : r + 1] if r < 12 else rows[r - 12 : r - 11]
+        out[pl.ds(block_of(r), 1), :] = row
 
 
 def log_total(sums):
@@ -330,16 +335,15 @@
         rider_zone, driver_zone, zone_table,
     )
     messages = gather(rider_msg, driver_msg)
-    *costs, sums = call(
-        rider_first_body,
-        [f32(4 * B, DB * B)] * 4 + [f32(RB, B)],
-        [VM] * 5,
-        [
-            pltpu.VMEM((RB, B), F32),
-            pltpu.VMEM((DB * B, 2 * B), BF16),
-            pltpu.VMEM((4 * B, 2 * B), BF16),
-        ],
-    )(*messages)
+    own_near, own_far, other_near, other_far, driver = messages
+    cost, left = f32(4 * B, DB * B), pltpu.VMEM((4 * B, 2 * B), BF16)
+    *costs, rows, wide = call(
+        rider_early_body, [cost] * 3 + [f32(12, B), bf16(DB * B, 2 * B)], [VM] * 4, [left]
+    )(own_near, own_far, other_near, driver)
+    last, sums = call(
+        rider_late_body, [cost, f32(RB, B)], [VM] * 3, [pltpu.VMEM((4, B), F32), left]
+    )(other_far, wide, rows)
+    costs.append(last)
     sums = close(sums, log_add)
     columns = pltpu.VMEM((RB * B, B), F32)
     sums, kernel, peaks, pots = call(

time: 109 us -> 109 us (level)
    all_to_all x1, waiting for transfers between devices: 4.1 us -> 5.45 us  [exchange(): return lax.all_to_all(message, axes, 0, 0, tiled=True)]
    ppermute x8, waiting for transfers between devices: 4.83 us -> 3.49 us  [swap(): lax.ppermute(value, axis, [(k, partner(k)) for k in range(SIZES[AXES.inde...]
    pallas_call x1 -> x2, Pallas kernels: 2.25 us -> 2.59 us  [the longest x1 1.78 us: per_device(): call(rider_early_body, [cost] * 3 + [f32(12, B), bf16(DB * B, 2 * B)], [V...]
  transfers between devices with their start and end apart: 11 -> 11, of which waited for: 6 -> 5; matrix products, arithmetic and copies ran while one was open for 0% -> 0% of each run, Pallas kernels for 0% -> 2%
where the time goes in v13:
time: 109 us; the launch traced here: 108 us
  blocking collectives  67.8 us (62%)
  starting transfers between devices  17.1 us (16%)
  waiting for transfers between devices  11.5 us (11%)
  Pallas kernels  10.3 us (9%)
  between operations  1.43 us (1%)
    all_to_all x6, blocking collectives, exchange(): return lax.all_to_all(message, axes, 0, 0, tiled=True)  67.8 us
    all_to_all x1, starting transfers between devices, exchange(): return lax.all_to_all(message, axes, 0, 0, tiled=True)  8.47 us
    all_to_all x1, waiting for transfers between devices, exchange(): return lax.all_to_all(message, axes, 0, 0, tiled=True)  5.45 us
    ppermute x8, starting transfers between devices, swap(): lax.ppermute(value, axis, [(k, partner(k)) for k in range(SIZES[AXES.inde...  5.25 us
    ppermute x8, waiting for transfers between devices, swap(): lax.ppermute(value, axis, [(k, partner(k)) for k in range(SIZES[AXES.inde...  3.49 us
    ppermute x2, starting transfers between devices, from_y(): lax.ppermute(value, ('yl', 'yh'), [(place_of(y), place_of((y - step) % 4)...  3.39 us
    ppermute x2, waiting for transfers between devices, from_y(): lax.ppermute(value, ('yl', 'yh'), [(place_of(y), place_of((y - step) % 4)...  2.56 us
  transfers between devices with their start and end apart: 11, of which 5 were waited for; matrix products, arithmetic and copies ran while one was open for 0% of the time, Pallas kernels for 2%

profile of v13, /device:TPU:2, one launch (start us, length us, event | category | flops | bytes accessed | tf_op | source)
XLA Modules:
  0.0 108.2 jit_solution(5955377386116570935)
XLA Ops:
  1.3 1.8 %shard_map.86 = (bf16[1,144,128]{2,1,0:T(8,128)(2,1)S(1)}, bf16[8,144,128]{2,1,0:T(8,128)(2,1)}) custom-call(bf16[2,128,128]{2,1,0:T(8,128)(2,1)} %bitcast.5, bf16[128,128]{1,0:T(8,128)(2,1)} %driver.1, f32[2,128]{1,0:T(2,128)} %bitcast.6, f32[1,128]{1,0:T(1,128)} %bitcast.7, s32[2]{0:T(128)} %rzone.1, s32[1]{0:T(128)S(6)} %copy.13.dzone, s32[16,16]{1,0:T(8,128)} %table.1), custom_call_target="tpu_custom_call" | custom-call | tf_op jit(solution)/shard_map/pallas_call | solution.py:320
  3.1 2.2 %collective-permute-start.3 = (bf16[1,144,128]{2,1,0:T(8,128)(2,1)S(1)}, bf16[1,144,128]{2,1,0:T(8,128)(2,1)S(1)}, u32[]{:S(2)}, u32[]{:S(2)}) collective-permute-start(bf16[1,144,128]{2,1,0:T(8,128)(2,1)S(1)} %get-tuple-element.19), channel_id=1, source_target_pairs={{0,8},{4,12},{8,0},{12,4},{1,9},{5,13},{9,1},{13,5},{2,10},{6,14},... | collective-permute-start | bytes 110600 | tf_op jit(solution)/shard_map/ppermute | solution.py:285
  5.3 1.6 %collective-permute-start.2 = (bf16[1,144,128]{2,1,0:T(8,128)(2,1)S(1)}, bf16[1,144,128]{2,1,0:T(8,128)(2,1)S(1)}, u32[]{:S(2)}, u32[]{:S(2)}) collective-permute-start(bf16[1,144,128]{2,1,0:T(8,128)(2,1)S(1)} %get-tuple-element.19), channel_id=1, source_target_pairs={{0,12},{4,8},{8,4},{12,0},{1,13},{5,9},{9,5},{13,1},{2,14},{6,10},... | collective-permute-start | bytes 110600 | tf_op jit(solution)/shard_map/ppermute | solution.py:285
  6.9 1.0 collective-permute-start
  7.9 8.5 %all-to-all-start = ((bf16[8,144,128]{2,1,0:T(8,128)(2,1)}), bf16[8,144,128]{2,1,0:T(8,128)(2,1)S(1)}, u32[]{:S(2)}, u32[]{:S(2)}) async-start(bf16[8,144,128]{2,1,0:T(8,128)(2,1)} %get-tuple-element.20), calls=%async_computation | async-start | bytes 589824 | tf_op jit(solution)/shard_map/all_to_all | solution.py:281
  16.3 0.0 collective-permute-done.3
  16.4 1.7 %collective-permute-start.4 = (bf16[2,144,128]{2,1,0:T(8,128)(2,1)S(1)}, bf16[2,144,128]{2,1,0:T(8,128)(2,1)S(1)}, u32[]{:S(2)}, u32[]{:S(2)}) collective-permute-start(bf16[2,144,128]{2,1,0:T(8,128)(2,1)S(1)} %pad_maximum_fusion.1), channel_id=1, source_target_pairs={{0,16},{16,2},{2,18},{18,0},{1,17},{17,3},{3,19},{19,1},{4,20},{20... | collective-permute-start | bytes 221192 | tf_op jit(solution)/shard_map/ppermute | solution.py:290
  18.0 1.7 %collective-permute-start.1 = (bf16[2,144,128]{2,1,0:T(8,128)(2,1)S(1)}, bf16[2,144,128]{2,1,0:T(8,128)(2,1)S(1)}, u32[]{:S(2)}, u32[]{:S(2)}) collective-permute-start(bf16[2,144,128]{2,1,0:T(8,128)(2,1)S(1)} %pad_maximum_fusion), channel_id=1, source_target_pairs={{0,18},{16,0},{2,16},{18,2},{1,19},{17,1},{3,17},{19,3},{4,22},{20... | collective-permute-start | bytes 221192 | tf_op jit(solution)/shard_map/ppermute | solution.py:290
  19.8 0.1 collective-permute-start.6
  19.9 2.6 %collective-permute-done.1 = bf16[2,144,128]{2,1,0:T(8,128)(2,1)S(1)} collective-permute-done((bf16[2,144,128]{2,1,0:T(8,128)(2,1)S(1)}, bf16[2,144,128]{2,1,0:T(8,128)(2,1)S(1)}, u32[]{:S(2)}, u32[]{:S(2)}) %collective-permute-start.1) | collective-permute-done | bytes 73760 | tf_op jit(solution)/shard_map/ppermute | solution.py:290
  22.5 0.1 collective-permute-start.5
  22.6 5.4 %all-to-all-done.driver = bf16[8,144,128]{2,1,0:T(8,128)(2,1)S(1)} async-done(((bf16[8,144,128]{2,1,0:T(8,128)(2,1)}), bf16[8,144,128]{2,1,0:T(8,128)(2,1)S(1)}, u32[]{:S(2)}, u32[]{:S(2)}) %all-to-all-start) | async-done | bytes 294944 | tf_op jit(solution)/shard_map/all_to_all | solution.py:281
  28.1 1.8 %shard_map.87 = (f32[512,1024]{1,0:T(8,128)S(1)}, f32[512,1024]{1,0:T(8,128)S(1)}, f32[512,1024]{1,0:T(8,128)S(1)}, f32[12,128]{1,0:T(8,128)S(1)}, bf16[1024,256]{1,0:T(8,128)(2,1)S(1)}) custom-call(bf16[4,144,128]{2,1,0:T(8,128)(2,1)S(1)} %constant_dynamic-update-slice_fusion.2.own_near, bf16[4,144,128]{2,1,0:T(8,128)(2,1)S(1)} %constant_dynamic-update-slice_fusion.own_far, ...), custom_call_target="tpu_custom_call" | custom-call | tf_op jit(solution)/shard_map/pallas_call | solution.py:340
  29.9 0.8 shard_map.88
  30.7 0.1 collective-permute-start.7
  30.8 1.2 %collective-permute-done.7 = f32[16,128]{1,0:T(8,128)S(1)} collective-permute-done((f32[16,128]{1,0:T(8,128)S(1)}, f32[16,128]{1,0:T(8,128)S(1)}, u32[]{:S(2)}, u32[]{:S(2)}) %collective-permute-start.7) | collective-permute-done | bytes 8224 | tf_op jit(solution)/shard_map/ppermute | solution.py:285
  32.0 14.1 %all_to_all.35.sums = f32[16,16,128]{2,1,0:T(8,128)S(1)} all-to-all(f32[16,16,128]{2,1,0:T(8,128)S(1)} %broadcast_in_dim.6), channel_id=1, replica_groups=mesh['z'=8,'yl'=2,'x'=4,'yh'=2,'c'=2] {'yl','x','yh'}, dimensions={0} | all-to-all | bytes 262144 | tf_op jit(solution)/shard_map/all_to_all | solution.py:281
  46.1 2.0 %shard_map.89 = (f32[8,8,128]{2,1,0:T(8,128)S(1)}, f32[2048,1024]{1,0:T(8,128)S(1)}, f32[16,128]{1,0:T(8,128)S(1)}, f32[32,128]{1,0:T(8,128)S(1)}) custom-call(f32[16,16,128]{2,1,0:T(8,128)S(1)} %all_to_all.35.sums, bf16[4,144,128]{2,1,0:T(8,128)(2,1)S(1)} %constant_dynamic-update-slice_fusion.2.own_near, ...), custom_call_target="tpu_custom_call" | custom-call | tf_op jit(solution)/shard_map/pallas_call | solution.py:349
  48.1 10.4 %all_to_all.36.sums = f32[8,8,128]{2,1,0:T(8,128)S(1)} all-to-all(f32[8,8,128]{2,1,0:T(8,128)S(1)} %get-tuple-element.28), channel_id=1, replica_groups=mesh['z'=8,'yl'=2,'x'=4,'yh'=2,'c'=2] {'z'}, dimensions={0} | all-to-all | bytes 65536 | tf_op jit(solution)/shard_map/all_to_all | solution.py:281
  58.5 0.7 shard_map.90
  59.1 0.1 collective-permute-start.8
  59.2 1.2 %collective-permute-done.8 = f32[16,128]{1,0:T(8,128)S(1)} collective-permute-done((f32[16,128]{1,0:T(8,128)S(1)}, f32[16,128]{1,0:T(8,128)S(1)}, u32[]{:S(2)}, u32[]{:S(2)}) %collective-permute-start.8) | collective-permute-done | bytes 8224 | tf_op jit(solution)/shard_map/ppermute | solution.py:285
  60.4 11.2 %all_to_all.37.sums = f32[16,16,128]{2,1,0:T(8,128)S(1)} all-to-all(f32[16,16,128]{2,1,0:T(8,128)S(1)} %broadcast_in_dim.7), channel_id=1, replica_groups=mesh['z'=8,'yl'=2,'x'=4,'yh'=2,'c'=2] {'yl','x','yh'}, dimensions={0} | all-to-all | bytes 262144 | tf_op jit(solution)/shard_map/all_to_all | solution.py:281
  71.7 1.0 shard_map.91
  72.7 10.4 %all_to_all.38.sums = f32[8,8,128]{2,1,0:T(8,128)S(1)} all-to-all(f32[8,8,128]{2,1,0:T(8,128)S(1)} %shard_map.91), channel_id=1, replica_groups=mesh['z'=8,'yl'=2,'x'=4,'yh'=2,'c'=2] {'z'}, dimensions={0} | all-to-all | bytes 65536 | tf_op jit(solution)/shard_map/all_to_all | solution.py:281
  83.0 0.6 shard_map.92
  83.7 0.1 collective-permute-start.9
  83.8 1.2 %collective-permute-done.9 = f32[16,128]{1,0:T(8,128)S(1)} collective-permute-done((f32[16,128]{1,0:T(8,128)S(1)}, f32[16,128]{1,0:T(8,128)S(1)}, u32[]{:S(2)}, u32[]{:S(2)}) %collective-permute-start.9) | collective-permute-done | bytes 8224 | tf_op jit(solution)/shard_map/ppermute | solution.py:285
  85.0 11.2 %all_to_all.39.sums.rider_sums = f32[16,16,128]{2,1,0:T(8,128)S(1)} all-to-all(f32[16,16,128]{2,1,0:T(8,128)S(1)} %broadcast_in_dim.8), channel_id=1, replica_groups=mesh['z'=8,'yl'=2,'x'=4,'yh'=2,'c'=2] {'yl','x','yh'}, dimensions={0} | all-to-all | bytes 262144 | tf_op jit(solution)/shard_map/all_to_all | solution.py:281
  96.2 1.0 shard_map.93
  97.2 10.4 %all_to_all.40.sums = f32[8,8,128]{2,1,0:T(8,128)S(1)} all-to-all(f32[8,8,128]{2,1,0:T(8,128)S(1)} %shard_map.93), channel_id=1, replica_groups=mesh['z'=8,'yl'=2,'x'=4,'yh'=2,'c'=2] {'z'}, dimensions={0} | all-to-all | bytes 65536 | tf_op jit(solution)/shard_map/all_to_all | solution.py:281
  107.6 0.6 shard_map.94
  (19 shorter events, 0.1 us)
Async XLA Ops:
  3.1 13.3 %collective-permute-start.3 = (bf16[1,144,128]{2,1,0:T(8,128)(2,1)S(1)}, bf16[1,144,128]{2,1,0:T(8,128)(2,1)S(1)}, u32[]{:S(2)}, u32[]{:S(2)}) collective-permute-start(bf16[1,144,128]{2,1,0:T(8,128)(2,1)S(1)} %get-tuple-element.19), channel_id=1, source_target_pairs={{0,8},{4,12},{8,0},{12,4},{1,9},{5,13},{9,1},{13,5},{2,10},{6,14},... | collective-permute-start | bytes 110600 | tf_op jit(solution)/shard_map/ppermute | solution.py:285
  5.3 11.1 %collective-permute-start.2 = (bf16[1,144,128]{2,1,0:T(8,128)(2,1)S(1)}, bf16[1,144,128]{2,1,0:T(8,128)(2,1)S(1)}, u32[]{:S(2)}, u32[]{:S(2)}) collective-permute-start(bf16[1,144,128]{2,1,0:T(8,128)(2,1)S(1)} %get-tuple-element.19), channel_id=1, source_target_pairs={{0,12},{4,8},{8,4},{12,0},{1,13},{5,9},{9,5},{13,1},{2,14},{6,10},... | collective-permute-start | bytes 110600 | tf_op jit(solution)/shard_map/ppermute | solution.py:285
  6.9 11.1 %collective-permute-start = (bf16[1,144,128]{2,1,0:T(8,128)(2,1)S(1)}, bf16[1,144,128]{2,1,0:T(8,128)(2,1)S(1)}, u32[]{:S(2)}, u32[]{:S(2)}) collective-permute-start(bf16[1,144,128]{2,1,0:T(8,128)(2,1)S(1)} %get-tuple-element.19), channel_id=1, source_target_pairs={{0,4},{4,0},{8,12},{12,8},{1,5},{5,1},{9,13},{13,9},{2,6},{6,2},{1... | collective-permute-start | bytes 110600 | tf_op jit(solution)/shard_map/ppermute | solution.py:285
  7.9 20.2 %all-to-all-start = ((bf16[8,144,128]{2,1,0:T(8,128)(2,1)}), bf16[8,144,128]{2,1,0:T(8,128)(2,1)S(1)}, u32[]{:S(2)}, u32[]{:S(2)}) async-start(bf16[8,144,128]{2,1,0:T(8,128)(2,1)} %get-tuple-element.20), calls=%async_computation | async-start | bytes 589824 | tf_op jit(solution)/shard_map/all_to_all | solution.py:281
  16.4 6.1 %collective-permute-start.4 = (bf16[2,144,128]{2,1,0:T(8,128)(2,1)S(1)}, bf16[2,144,128]{2,1,0:T(8,128)(2,1)S(1)}, u32[]{:S(2)}, u32[]{:S(2)}) collective-permute-start(bf16[2,144,128]{2,1,0:T(8,128)(2,1)S(1)} %pad_maximum_fusion.1), channel_id=1, source_target_pairs={{0,16},{16,2},{2,18},{18,0},{1,17},{17,3},{3,19},{19,1},{4,20},{20... | collective-permute-start | bytes 221192 | tf_op jit(solution)/shard_map/ppermute | solution.py:290
  18.0 4.4 %collective-permute-start.1 = (bf16[2,144,128]{2,1,0:T(8,128)(2,1)S(1)}, bf16[2,144,128]{2,1,0:T(8,128)(2,1)S(1)}, u32[]{:S(2)}, u32[]{:S(2)}) collective-permute-start(bf16[2,144,128]{2,1,0:T(8,128)(2,1)S(1)} %pad_maximum_fusion), channel_id=1, source_target_pairs={{0,18},{16,0},{2,16},{18,2},{1,19},{17,1},{3,17},{19,3},{4,22},{20... | collective-permute-start | bytes 221192 | tf_op jit(solution)/shard_map/ppermute | solution.py:290
  19.8 2.8 %collective-permute-start.6 = (bf16[4,144,128]{2,1,0:T(8,128)(2,1)S(1)}, bf16[4,144,128]{2,1,0:T(8,128)(2,1)S(1)}, u32[]{:S(2)}, u32[]{:S(2)}) collective-permute-start(bf16[4,144,128]{2,1,0:T(8,128)(2,1)S(1)} %constant_dynamic-update-slice_fusion.2.own_near), channel_id=1, source_target_pairs={{0,1},{1,0},{2,3},{3,2},{4,5},{5,4},{6,7},{7,6},{8,9},{9,8},{10,11... | collective-permute-start | bytes 442376 | tf_op jit(solution)/shard_map/ppermute | solution.py:285
  22.5 7.3 %collective-permute-start.5 = (bf16[4,144,128]{2,1,0:T(8,128)(2,1)S(1)}, bf16[4,144,128]{2,1,0:T(8,128)(2,1)S(1)}, u32[]{:S(2)}, u32[]{:S(2)}) collective-permute-start(bf16[4,144,128]{2,1,0:T(8,128)(2,1)S(1)} %constant_dynamic-update-slice_fusion.own_far), channel_id=1, source_target_pairs={{0,1},{1,0},{2,3},{3,2},{4,5},{5,4},{6,7},{7,6},{8,9},{9,8},{10,11... | collective-permute-start | bytes 442376 | tf_op jit(solution)/shard_map/ppermute | solution.py:285
  30.7 1.3 %collective-permute-start.7 = (f32[16,128]{1,0:T(8,128)S(1)}, f32[16,128]{1,0:T(8,128)S(1)}, u32[]{:S(2)}, u32[]{:S(2)}) collective-permute-start(f32[16,128]{1,0:T(8,128)S(1)} %get-tuple-element.23), channel_id=1, source_target_pairs={{0,1},{1,0},{2,3},{3,2},{4,5},{5,4},{6,7},{7,6},{8,9},{9,8},{10,11... | collective-permute-start | bytes 24584 | tf_op jit(solution)/shard_map/ppermute | solution.py:285
  59.1 1.3 %collective-permute-start.8 = (f32[16,128]{1,0:T(8,128)S(1)}, f32[16,128]{1,0:T(8,128)S(1)}, u32[]{:S(2)}, u32[]{:S(2)}) collective-permute-start(f32[16,128]{1,0:T(8,128)S(1)} %get-tuple-element.31), channel_id=1, source_target_pairs={{0,1},{1,0},{2,3},{3,2},{4,5},{5,4},{6,7},{7,6},{8,9},{9,8},{10,11... | collective-permute-start | bytes 24584 | tf_op jit(solution)/shard_map/ppermute | solution.py:285
  83.7 1.3 %collective-permute-start.9 = (f32[16,128]{1,0:T(8,128)S(1)}, f32[16,128]{1,0:T(8,128)S(1)}, u32[]{:S(2)}, u32[]{:S(2)}) collective-permute-start(f32[16,128]{1,0:T(8,128)S(1)} %shard_map.92), channel_id=1, source_target_pairs={{0,1},{1,0},{2,3},{3,2},{4,5},{5,4},{6,7},{7,6},{8,9},{9,8},{10,11... | collective-permute-start | bytes 24584 | tf_op jit(solution)/shard_map/ppermute | solution.py:285

commit v14 on v12

--- a/solution.py
+++ b/solution.py
@@ -74,7 +74,7 @@
 
 
 def zone_rows(message):
-    return jnp.broadcast_to(message[B : B + 1].astype(F32), (16, B)).astype(BF16)
+    return jnp.broadcast_to(message[B:].astype(F32)[0:1], (16, B)).astype(BF16)
 
 
 def weight_row(message):

time: 109 us -> 109 us (level)
  no operation moved by 1% of the time
where the time goes in v14:
time: 109 us; the launch traced here: 108 us
  blocking collectives  68 us (62%)
  starting transfers between devices  17.1 us (16%)
  waiting for transfers between devices  11.5 us (11%)
  Pallas kernels  9.93 us (9%)
  between operations  1.42 us (1%)
    all_to_all x6, blocking collectives, exchange(): return lax.all_to_all(message, axes, 0, 0, tiled=True)  68 us
    all_to_all x1, starting transfers between devices, exchange(): return lax.all_to_all(message, axes, 0, 0, tiled=True)  8.47 us
    ppermute x8, starting transfers between devices, swap(): lax.ppermute(value, axis, [(k, partner(k)) for k in range(SIZES[AXES.inde...  5.25 us
    ppermute x8, waiting for transfers between devices, swap(): lax.ppermute(value, axis, [(k, partner(k)) for k in range(SIZES[AXES.inde...  4.83 us
    all_to_all x1, waiting for transfers between devices, exchange(): return lax.all_to_all(message, axes, 0, 0, tiled=True)  4.1 us
    ppermute x2, starting transfers between devices, from_y(): lax.ppermute(value, ('yl', 'yh'), [(place_of(y), place_of((y - step) % 4)...  3.39 us
    ppermute x2, waiting for transfers between devices, from_y(): lax.ppermute(value, ('yl', 'yh'), [(place_of(y), place_of((y - step) % 4)...  2.56 us
    pallas_call x1, Pallas kernels, per_device(): call(rider_first_body, [f32(4 * B, DB * B)] * 4 + [f32(RB, B)], [VM] * 5,...  2.25 us
  transfers between devices with their start and end apart: 11, of which 6 were waited for; matrix products, arithmetic and copies ran while one was open for 0% of the time, Pallas kernels for 0%

profile of v14, /device:TPU:2, one launch (start us, length us, event | category | flops | bytes accessed | tf_op | source)
XLA Modules:
  0.0 108.1 jit_solution(17693990685976824388)
XLA Ops:
  1.3 1.8 %shard_map.86 = (bf16[1,144,128]{2,1,0:T(8,128)(2,1)S(1)}, bf16[8,144,128]{2,1,0:T(8,128)(2,1)}) custom-call(bf16[2,128,128]{2,1,0:T(8,128)(2,1)} %bitcast.5, bf16[128,128]{1,0:T(8,128)(2,1)} %driver.1, f32[2,128]{1,0:T(2,128)} %bitcast.6, f32[1,128]{1,0:T(1,128)} %bitcast.7, s32[2]{0:T(128)} %rzone.1, s32[1]{0:T(128)S(6)} %copy.13.dzone, s32[16,16]{1,0:T(8,128)} %table.1), custom_call_target="tpu_custom_call" | custom-call | tf_op jit(solution)/shard_map/pallas_call | solution.py:315
  3.1 2.2 %collective-permute-start.2 = (bf16[1,144,128]{2,1,0:T(8,128)(2,1)S(1)}, bf16[1,144,128]{2,1,0:T(8,128)(2,1)S(1)}, u32[]{:S(2)}, u32[]{:S(2)}) collective-permute-start(bf16[1,144,128]{2,1,0:T(8,128)(2,1)S(1)} %get-tuple-element.17), channel_id=1, source_target_pairs={{0,8},{4,12},{8,0},{12,4},{1,9},{5,13},{9,1},{13,5},{2,10},{6,14},... | collective-permute-start | bytes 110600 | tf_op jit(solution)/shard_map/ppermute | solution.py:280
  5.3 1.6 %collective-permute-start.1 = (bf16[1,144,128]{2,1,0:T(8,128)(2,1)S(1)}, bf16[1,144,128]{2,1,0:T(8,128)(2,1)S(1)}, u32[]{:S(2)}, u32[]{:S(2)}) collective-permute-start(bf16[1,144,128]{2,1,0:T(8,128)(2,1)S(1)} %get-tuple-element.17), channel_id=1, source_target_pairs={{0,12},{4,8},{8,4},{12,0},{1,13},{5,9},{9,5},{13,1},{2,14},{6,10},... | collective-permute-start | bytes 110600 | tf_op jit(solution)/shard_map/ppermute | solution.py:280
  6.9 1.0 collective-permute-start
  7.9 8.5 %all-to-all-start = ((bf16[8,144,128]{2,1,0:T(8,128)(2,1)}), bf16[8,144,128]{2,1,0:T(8,128)(2,1)S(1)}, u32[]{:S(2)}, u32[]{:S(2)}) async-start(bf16[8,144,128]{2,1,0:T(8,128)(2,1)} %get-tuple-element.18), calls=%async_computation | async-start | bytes 589824 | tf_op jit(solution)/shard_map/all_to_all | solution.py:276
  16.3 0.0 collective-permute-done.2
  16.4 1.7 %collective-permute-start.4 = (bf16[2,144,128]{2,1,0:T(8,128)(2,1)S(1)}, bf16[2,144,128]{2,1,0:T(8,128)(2,1)S(1)}, u32[]{:S(2)}, u32[]{:S(2)}) collective-permute-start(bf16[2,144,128]{2,1,0:T(8,128)(2,1)S(1)} %pad_maximum_fusion.1), channel_id=1, source_target_pairs={{0,16},{16,2},{2,18},{18,0},{1,17},{17,3},{3,19},{19,1},{4,20},{20... | collective-permute-start | bytes 221192 | tf_op jit(solution)/shard_map/ppermute | solution.py:285
  18.0 1.7 %collective-permute-start.3 = (bf16[2,144,128]{2,1,0:T(8,128)(2,1)S(1)}, bf16[2,144,128]{2,1,0:T(8,128)(2,1)S(1)}, u32[]{:S(2)}, u32[]{:S(2)}) collective-permute-start(bf16[2,144,128]{2,1,0:T(8,128)(2,1)S(1)} %pad_maximum_fusion), channel_id=1, source_target_pairs={{0,18},{16,0},{2,16},{18,2},{1,19},{17,1},{3,17},{19,3},{4,22},{20... | collective-permute-start | bytes 221192 | tf_op jit(solution)/shard_map/ppermute | solution.py:285
  19.8 0.1 collective-permute-start.5
  19.9 2.6 %collective-permute-done.3 = bf16[2,144,128]{2,1,0:T(8,128)(2,1)S(1)} collective-permute-done((bf16[2,144,128]{2,1,0:T(8,128)(2,1)S(1)}, bf16[2,144,128]{2,1,0:T(8,128)(2,1)S(1)}, u32[]{:S(2)}, u32[]{:S(2)}) %collective-permute-start.3) | collective-permute-done | bytes 73760 | tf_op jit(solution)/shard_map/ppermute | solution.py:285
  22.5 0.1 collective-permute-start.6
  22.6 1.3 %collective-permute-done.6.other_far = bf16[4,144,128]{2,1,0:T(8,128)(2,1)S(1)} collective-permute-done((bf16[4,144,128]{2,1,0:T(8,128)(2,1)S(1)}, bf16[4,144,128]{2,1,0:T(8,128)(2,1)S(1)}, u32[]{:S(2)}, u32[]{:S(2)}) %collective-permute-start.6) | collective-permute-done | bytes 147488 | tf_op jit(solution)/shard_map/ppermute | solution.py:280
  24.0 4.1 %all-to-all-done.driver = bf16[8,144,128]{2,1,0:T(8,128)(2,1)S(1)} async-done(((bf16[8,144,128]{2,1,0:T(8,128)(2,1)}), bf16[8,144,128]{2,1,0:T(8,128)(2,1)S(1)}, u32[]{:S(2)}, u32[]{:S(2)}) %all-to-all-start) | async-done | bytes 294944 | tf_op jit(solution)/shard_map/all_to_all | solution.py:276
  28.1 2.3 %shard_map.87 = (f32[512,1024]{1,0:T(8,128)S(1)}, f32[512,1024]{1,0:T(8,128)S(1)}, f32[512,1024]{1,0:T(8,128)S(1)}, f32[512,1024]{1,0:T(8,128)S(1)}, f32[16,128]{1,0:T(8,128)S(1)}) custom-call(bf16[4,144,128]{2,1,0:T(8,128)(2,1)S(1)} %constant_dynamic-update-slice_fusion.own_near, bf16[4,144,128]{2,1,0:T(8,128)(2,1)S(1)} %constant_dynamic-update-slice_fusion.4.own_far, ...), custom_call_target="tpu_custom_call" | custom-call | tf_op jit(solution)/shard_map/pallas_call | solution.py:333
  30.3 0.1 collective-permute-start.7
  30.4 1.2 %collective-permute-done.7 = f32[16,128]{1,0:T(8,128)S(1)} collective-permute-done((f32[16,128]{1,0:T(8,128)S(1)}, f32[16,128]{1,0:T(8,128)S(1)}, u32[]{:S(2)}, u32[]{:S(2)}) %collective-permute-start.7) | collective-permute-done | bytes 8224 | tf_op jit(solution)/shard_map/ppermute | solution.py:280
  31.6 14.1 %all_to_all.35.sums = f32[16,16,128]{2,1,0:T(8,128)S(1)} all-to-all(f32[16,16,128]{2,1,0:T(8,128)S(1)} %broadcast_in_dim.6), channel_id=1, replica_groups=mesh['z'=8,'yl'=2,'x'=4,'yh'=2,'c'=2] {'yl','x','yh'}, dimensions={0} | all-to-all | bytes 262144 | tf_op jit(solution)/shard_map/all_to_all | solution.py:276
  45.7 2.0 %shard_map.88 = (f32[8,8,128]{2,1,0:T(8,128)S(1)}, f32[2048,1024]{1,0:T(8,128)S(1)}, f32[16,128]{1,0:T(8,128)S(1)}, f32[32,128]{1,0:T(8,128)S(1)}) custom-call(f32[16,16,128]{2,1,0:T(8,128)S(1)} %all_to_all.35.sums, bf16[4,144,128]{2,1,0:T(8,128)(2,1)S(1)} %constant_dynamic-update-slice_fusion.own_near, ...), custom_call_target="tpu_custom_call" | custom-call | tf_op jit(solution)/shard_map/pallas_call | solution.py:345
  47.7 10.6 %all_to_all.36.sums = f32[8,8,128]{2,1,0:T(8,128)S(1)} all-to-all(f32[8,8,128]{2,1,0:T(8,128)S(1)} %get-tuple-element.24), channel_id=1, replica_groups=mesh['z'=8,'yl'=2,'x'=4,'yh'=2,'c'=2] {'z'}, dimensions={0} | all-to-all | bytes 65536 | tf_op jit(solution)/shard_map/all_to_all | solution.py:276
  58.4 0.7 shard_map.89
  59.0 0.1 collective-permute-start.8
  59.1 1.2 %collective-permute-done.8 = f32[16,128]{1,0:T(8,128)S(1)} collective-permute-done((f32[16,128]{1,0:T(8,128)S(1)}, f32[16,128]{1,0:T(8,128)S(1)}, u32[]{:S(2)}, u32[]{:S(2)}) %collective-permute-start.8) | collective-permute-done | bytes 8224 | tf_op jit(solution)/shard_map/ppermute | solution.py:280
  60.3 11.2 %all_to_all.37.sums = f32[16,16,128]{2,1,0:T(8,128)S(1)} all-to-all(f32[16,16,128]{2,1,0:T(8,128)S(1)} %broadcast_in_dim.7), channel_id=1, replica_groups=mesh['z'=8,'yl'=2,'x'=4,'yh'=2,'c'=2] {'yl','x','yh'}, dimensions={0} | all-to-all | bytes 262144 | tf_op jit(solution)/shard_map/all_to_all | solution.py:276
  71.5 1.0 shard_map.90
  72.5 10.4 %all_to_all.38.sums = f32[8,8,128]{2,1,0:T(8,128)S(1)} all-to-all(f32[8,8,128]{2,1,0:T(8,128)S(1)} %shard_map.90), channel_id=1, replica_groups=mesh['z'=8,'yl'=2,'x'=4,'yh'=2,'c'=2] {'z'}, dimensions={0} | all-to-all | bytes 65536 | tf_op jit(solution)/shard_map/all_to_all | solution.py:276
  82.9 0.6 shard_map.91
  83.6 0.1 collective-permute-start.9
  83.7 1.2 %collective-permute-done.9 = f32[16,128]{1,0:T(8,128)S(1)} collective-permute-done((f32[16,128]{1,0:T(8,128)S(1)}, f32[16,128]{1,0:T(8,128)S(1)}, u32[]{:S(2)}, u32[]{:S(2)}) %collective-permute-start.9) | collective-permute-done | bytes 8224 | tf_op jit(solution)/shard_map/ppermute | solution.py:280
  84.8 11.2 %all_to_all.39.sums.rider_sums = f32[16,16,128]{2,1,0:T(8,128)S(1)} all-to-all(f32[16,16,128]{2,1,0:T(8,128)S(1)} %broadcast_in_dim.8), channel_id=1, replica_groups=mesh['z'=8,'yl'=2,'x'=4,'yh'=2,'c'=2] {'yl','x','yh'}, dimensions={0} | all-to-all | bytes 262144 | tf_op jit(solution)/shard_map/all_to_all | solution.py:276
  96.1 1.0 shard_map.92
  97.1 10.4 %all_to_all.40.sums = f32[8,8,128]{2,1,0:T(8,128)S(1)} all-to-all(f32[8,8,128]{2,1,0:T(8,128)S(1)} %shard_map.92), channel_id=1, replica_groups=mesh['z'=8,'yl'=2,'x'=4,'yh'=2,'c'=2] {'z'}, dimensions={0} | all-to-all | bytes 65536 | tf_op jit(solution)/shard_map/all_to_all | solution.py:276
  107.5 0.6 shard_map.93
  (18 shorter events, 0.1 us)
Async XLA Ops:
  3.1 13.3 %collective-permute-start.2 = (bf16[1,144,128]{2,1,0:T(8,128)(2,1)S(1)}, bf16[1,144,128]{2,1,0:T(8,128)(2,1)S(1)}, u32[]{:S(2)}, u32[]{:S(2)}) collective-permute-start(bf16[1,144,128]{2,1,0:T(8,128)(2,1)S(1)} %get-tuple-element.17), channel_id=1, source_target_pairs={{0,8},{4,12},{8,0},{12,4},{1,9},{5,13},{9,1},{13,5},{2,10},{6,14},... | collective-permute-start | bytes 110600 | tf_op jit(solution)/shard_map/ppermute | solution.py:280
  5.3 11.1 %collective-permute-start.1 = (bf16[1,144,128]{2,1,0:T(8,128)(2,1)S(1)}, bf16[1,144,128]{2,1,0:T(8,128)(2,1)S(1)}, u32[]{:S(2)}, u32[]{:S(2)}) collective-permute-start(bf16[1,144,128]{2,1,0:T(8,128)(2,1)S(1)} %get-tuple-element.17), channel_id=1, source_target_pairs={{0,12},{4,8},{8,4},{12,0},{1,13},{5,9},{9,5},{13,1},{2,14},{6,10},... | collective-permute-start | bytes 110600 | tf_op jit(solution)/shard_map/ppermute | solution.py:280
  6.9 11.1 %collective-permute-start = (bf16[1,144,128]{2,1,0:T(8,128)(2,1)S(1)}, bf16[1,144,128]{2,1,0:T(8,128)(2,1)S(1)}, u32[]{:S(2)}, u32[]{:S(2)}) collective-permute-start(bf16[1,144,128]{2,1,0:T(8,128)(2,1)S(1)} %get-tuple-element.17), channel_id=1, source_target_pairs={{0,4},{4,0},{8,12},{12,8},{1,5},{5,1},{9,13},{13,9},{2,6},{6,2},{1... | collective-permute-start | bytes 110600 | tf_op jit(solution)/shard_map/ppermute | solution.py:280
  7.9 20.2 %all-to-all-start = ((bf16[8,144,128]{2,1,0:T(8,128)(2,1)}), bf16[8,144,128]{2,1,0:T(8,128)(2,1)S(1)}, u32[]{:S(2)}, u32[]{:S(2)}) async-start(bf16[8,144,128]{2,1,0:T(8,128)(2,1)} %get-tuple-element.18), calls=%async_computation | async-start | bytes 589824 | tf_op jit(solution)/shard_map/all_to_all | solution.py:276
  16.4 6.1 %collective-permute-start.4 = (bf16[2,144,128]{2,1,0:T(8,128)(2,1)S(1)}, bf16[2,144,128]{2,1,0:T(8,128)(2,1)S(1)}, u32[]{:S(2)}, u32[]{:S(2)}) collective-permute-start(bf16[2,144,128]{2,1,0:T(8,128)(2,1)S(1)} %pad_maximum_fusion.1), channel_id=1, source_target_pairs={{0,16},{16,2},{2,18},{18,0},{1,17},{17,3},{3,19},{19,1},{4,20},{20... | collective-permute-start | bytes 221192 | tf_op jit(solution)/shard_map/ppermute | solution.py:285
  18.0 4.4 %collective-permute-start.3 = (bf16[2,144,128]{2,1,0:T(8,128)(2,1)S(1)}, bf16[2,144,128]{2,1,0:T(8,128)(2,1)S(1)}, u32[]{:S(2)}, u32[]{:S(2)}) collective-permute-start(bf16[2,144,128]{2,1,0:T(8,128)(2,1)S(1)} %pad_maximum_fusion), channel_id=1, source_target_pairs={{0,18},{16,0},{2,16},{18,2},{1,19},{17,1},{3,17},{19,3},{4,22},{20... | collective-permute-start | bytes 221192 | tf_op jit(solution)/shard_map/ppermute | solution.py:285
  19.8 2.8 %collective-permute-start.5 = (bf16[4,144,128]{2,1,0:T(8,128)(2,1)S(1)}, bf16[4,144,128]{2,1,0:T(8,128)(2,1)S(1)}, u32[]{:S(2)}, u32[]{:S(2)}) collective-permute-start(bf16[4,144,128]{2,1,0:T(8,128)(2,1)S(1)} %constant_dynamic-update-slice_fusion.own_near), channel_id=1, source_target_pairs={{0,1},{1,0},{2,3},{3,2},{4,5},{5,4},{6,7},{7,6},{8,9},{9,8},{10,11... | collective-permute-start | bytes 442376 | tf_op jit(solution)/shard_map/ppermute | solution.py:280
  22.5 1.5 %collective-permute-start.6 = (bf16[4,144,128]{2,1,0:T(8,128)(2,1)S(1)}, bf16[4,144,128]{2,1,0:T(8,128)(2,1)S(1)}, u32[]{:S(2)}, u32[]{:S(2)}) collective-permute-start(bf16[4,144,128]{2,1,0:T(8,128)(2,1)S(1)} %constant_dynamic-update-slice_fusion.4.own_far), channel_id=1, source_target_pairs={{0,1},{1,0},{2,3},{3,2},{4,5},{5,4},{6,7},{7,6},{8,9},{9,8},{10,11... | collective-permute-start | bytes 442376 | tf_op jit(solution)/shard_map/ppermute | solution.py:280
  30.3 1.3 %collective-permute-start.7 = (f32[16,128]{1,0:T(8,128)S(1)}, f32[16,128]{1,0:T(8,128)S(1)}, u32[]{:S(2)}, u32[]{:S(2)}) collective-permute-start(f32[16,128]{1,0:T(8,128)S(1)} %get-tuple-element.19), channel_id=1, source_target_pairs={{0,1},{1,0},{2,3},{3,2},{4,5},{5,4},{6,7},{7,6},{8,9},{9,8},{10,11... | collective-permute-start | bytes 24584 | tf_op jit(solution)/shard_map/ppermute | solution.py:280
  59.0 1.3 %collective-permute-start.8 = (f32[16,128]{1,0:T(8,128)S(1)}, f32[16,128]{1,0:T(8,128)S(1)}, u32[]{:S(2)}, u32[]{:S(2)}) collective-permute-start(f32[16,128]{1,0:T(8,128)S(1)} %get-tuple-element.27), channel_id=1, source_target_pairs={{0,1},{1,0},{2,3},{3,2},{4,5},{5,4},{6,7},{7,6},{8,9},{9,8},{10,11... | collective-permute-start | bytes 24584 | tf_op jit(solution)/shard_map/ppermute | solution.py:280
  83.6 1.3 %collective-permute-start.9 = (f32[16,128]{1,0:T(8,128)S(1)}, f32[16,128]{1,0:T(8,128)S(1)}, u32[]{:S(2)}, u32[]{:S(2)}) collective-permute-start(f32[16,128]{1,0:T(8,128)S(1)} %shard_map.91), channel_id=1, source_target_pairs={{0,1},{1,0},{2,3},{3,2},{4,5},{5,4},{6,7},{7,6},{8,9},{9,8},{10,11... | collective-permute-start | bytes 24584 | tf_op jit(solution)/shard_map/ppermute | solution.py:280
